TPU v7x, 32 devices: a whole 2x2x4 slice. The times are simulated.
32 devices in a mesh: dp: 8 (over z, y), mp: 4 (over x, core).
Axes of the slice: x: 2, y: 2, z: 4, core: 2. Of those that a mesh axis runs over, the one named last changes fastest.
Arguments:
- feats: bfloat16 [19456, 384], P('dp'), may hold values from -6 to 6
- centres: float32 [3, 19456], P(None, 'dp'), may hold values from -5 to 5
- counts: int32 [512], P('dp'), may hold values from 13 to 38, as said below
- cotangent: bfloat16 [19456, 384], P('dp'), may hold values from -6 to 6
- qkv_weight: float32 [3, 384, 512], P(None, 'dp', 'mp'), may hold values from -0.3125 to 0.3125
- out_weight: float32 [512, 384], P('mp', 'dp'), may hold values from -1.5 to 1.5
- up_weight: float32 [384, 1536], P('dp', 'mp'), may hold values from -0.3125 to 0.3125
- up_bias: float32 [1536], P('mp'), may hold values from -1 to 1
- down_weight: float32 [1536, 384], P('mp', 'dp'), may hold values from -0.15625 to 0.15625
- norm_vectors: float32 [7, 384], replicated, may hold values from -1 to 1.5, as said below
- pos_hidden: float32 [4, 128], replicated, may hold values from -3.5 to 3.5
- pos_proj: float32 [128, 384], replicated, may hold values from -0.5 to 0.5
- qkv_moment: float32 [3, 384, 512], P(None, 'dp', 'mp'), may hold values from -0.00390625 to 0.00390625
- out_moment: float32 [512, 384], P('mp', 'dp'), may hold values from -0.00390625 to 0.00390625
- up_moment: float32 [384, 1536], P('dp', 'mp'), may hold values from -0.00390625 to 0.00390625
- bias_moment: float32 [1536], P('mp'), may hold values from -0.00390625 to 0.00390625
- down_moment: float32 [1536, 384], P('mp', 'dp'), may hold values from -0.00390625 to 0.00390625
- vector_moment: float32 [7, 384], replicated, may hold values from -0.00390625 to 0.00390625
- hidden_moment: float32 [4, 128], replicated, may hold values from -0.00390625 to 0.00390625
- proj_moment: float32 [128, 384], replicated, may hold values from -0.00390625 to 0.00390625
- qkv_second: float32 [3, 384, 512], P(None, 'dp', 'mp'), may hold values from 4.9505735e-07 to 1.9802294e-06
- out_second: float32 [512, 384], P('mp', 'dp'), may hold values from 4.9505735e-07 to 1.9802294e-06
- up_second: float32 [384, 1536], P('dp', 'mp'), may hold values from 4.9505735e-07 to 1.9802294e-06
- bias_second: float32 [1536], P('mp'), may hold values from 4.9505735e-07 to 1.9802294e-06
- down_second: float32 [1536, 384], P('mp', 'dp'), may hold values from 4.9505735e-07 to 1.9802294e-06
- vector_second: float32 [7, 384], replicated, may hold values from 4.9505735e-07 to 1.9802294e-06
- hidden_second: float32 [4, 128], replicated, may hold values from 4.9505735e-07 to 1.9802294e-06
- proj_second: float32 [128, 384], replicated, may hold values from 4.9505735e-07 to 1.9802294e-06
Outputs:
- block_out: bfloat16 [19456, 384], P(('dp', 'mp'))
- feats_grad: float32 [19456, 384], P(('dp', 'mp'))
- clip_norm: float32 [], replicated
- trust_norms: float32 [2, 14], replicated
- qkv_weight_grad: float32 [3, 384, 512], P(None, 'dp', 'mp')
- qkv_weight_new: float32 [3, 384, 512], P(None, 'dp', 'mp')
- qkv_moment_new: float32 [3, 384, 512], P(None, 'dp', 'mp')
- qkv_second_new: float32 [3, 384, 512], P(None, 'dp', 'mp')
- qkv_weight_copy: bfloat16 [3, 384, 512], P(None, 'dp', 'mp')
- out_weight_grad: float32 [512, 384], P('mp', 'dp')
- out_weight_new: float32 [512, 384], P('mp', 'dp')
- out_moment_new: float32 [512, 384], P('mp', 'dp')
- out_second_new: float32 [512, 384], P('mp', 'dp')
- out_weight_copy: bfloat16 [512, 384], P('mp', 'dp')
- up_weight_grad: float32 [384, 1536], P('dp', 'mp')
- up_weight_new: float32 [384, 1536], P('dp', 'mp')
- up_moment_new: float32 [384, 1536], P('dp', 'mp')
- up_second_new: float32 [384, 1536], P('dp', 'mp')
- up_weight_copy: bfloat16 [384, 1536], P('dp', 'mp')
- up_bias_grad: float32 [1536], P('mp')
- up_bias_new: float32 [1536], P('mp')
- bias_moment_new: float32 [1536], P('mp')
- bias_second_new: float32 [1536], P('mp')
- up_bias_copy: bfloat16 [1536], P('mp')
- down_weight_grad: float32 [1536, 384], P('mp', 'dp')
- down_weight_new: float32 [1536, 384], P('mp', 'dp')
- down_moment_new: float32 [1536, 384], P('mp', 'dp')
- down_second_new: float32 [1536, 384], P('mp', 'dp')
- down_weight_copy: bfloat16 [1536, 384], P('mp', 'dp')
- norm_vectors_grad: float32 [7, 384], replicated
- norm_vectors_new: float32 [7, 384], replicated
- vector_moment_new: float32 [7, 384], replicated
- vector_second_new: float32 [7, 384], replicated
- norm_vectors_copy: bfloat16 [7, 384], replicated
- pos_hidden_grad: float32 [4, 128], replicated
- pos_hidden_new: float32 [4, 128], replicated
- hidden_moment_new: float32 [4, 128], replicated
- hidden_second_new: float32 [4, 128], replicated
- pos_hidden_copy: bfloat16 [4, 128], replicated
- pos_proj_grad: float32 [128, 384], replicated
- pos_proj_new: float32 [128, 384], replicated
- proj_moment_new: float32 [128, 384], replicated
- proj_second_new: float32 [128, 384], replicated
- pos_proj_copy: bfloat16 [128, 384], replicated
Inputs may be any that keep to these rules, and one draw needn't show every extreme that they name: `counts`: among the clouds of each index of dp, one has exactly 38 visible patches and another exactly 13. `norm_vectors`: gains of the two norms and the biases of the layer.
All inputs are finite; a program needn't handle non-finite values.
Results may differ from a plain program's by a relative error of at most 0.011.
Values may be sent and summed in bfloat16 or wider, within the bound.
A program may use at most 128 MiB of HBM per device.

v0:
```python
import math

import jax
import jax.numpy as jnp
from jax import lax
from jax.sharding import PartitionSpec as P

HD = 64
PAD = 38
BLOCK_CLOUDS = 16


norm_eps = 1e-05
beta_one = 0.5
beta_two = 0.5
adam_eps = 1e-06
decay_rate = 0.01
learn_rate = 0.3
clip_max = 1.0
step_count = 3.0
neg_fill = -1e30
highest = lax.Precision.HIGHEST


def layer_norm(values, gain, shift):
    centre = values - jnp.mean(values, axis=-1, keepdims=True)
    spread = jnp.mean(centre * centre, axis=-1, keepdims=True)
    return centre * lax.rsqrt(spread + norm_eps) * gain + shift


def gelu_exact(values):
    return 0.5 * values * (1.0 + lax.erf(values * 0.7071067811865476))


def piece_squares(array, tensor_index):
    if tensor_index == 5:
        return jnp.sum(array * array, axis=1)
    return jnp.sum(array * array)[None]


def piece_ratio(trust_ratio, tensor_index):
    if tensor_index < 5:
        return trust_ratio[tensor_index]
    if tensor_index == 5:
        return trust_ratio[5:12][:, None]
    return trust_ratio[tensor_index + 6]


def block_scores(query, keys, keep, score_scale):
    span = query.shape[0]
    cloud_ids = jnp.arange(span) // PAD
    allowed = (cloud_ids[:, None] == cloud_ids[None, :]) & (keep[None, :] > 0.5)
    raw = jnp.einsum("qsd,ksd->sqk", query, keys, preferred_element_type=jnp.float32)
    return (jnp.where(allowed[None], raw * score_scale, neg_fill), allowed)


def shards(
    feats,
    centres,
    counts,
    cotangent,
    qkv_weight,
    out_weight,
    up_weight,
    up_bias,
    down_weight,
    norm_vectors,
    pos_hidden,
    pos_proj,
    qkv_moment,
    out_moment,
    up_moment,
    bias_moment,
    down_moment,
    vector_moment,
    hidden_moment,
    proj_moment,
    qkv_second,
    out_second,
    up_second,
    bias_second,
    down_second,
    vector_second,
    hidden_second,
    proj_second,
):
    mp_count = lax.axis_size("mp")
    mp_index = lax.axis_index("mp")
    dp_index = lax.axis_index("dp")
    row_count = feats.shape[0]
    share_rows = row_count // mp_count
    row_start = mp_index * share_rows
    slot_cols = out_weight.shape[0]
    local_slots = slot_cols // HD
    block_rows = BLOCK_CLOUDS * PAD
    block_count = row_count // block_rows
    score_scale = 1.0 / math.sqrt(HD)
    keep_rows = (jnp.arange(PAD)[None, :] < counts[:, None]).reshape(row_count).astype(jnp.float32)
    slot_ids = mp_index * local_slots + jnp.arange(local_slots, dtype=jnp.int32)
    live = ((slot_ids % 2 == 0) | (slot_ids // 2 < mp_count // 2)).astype(jnp.float32)
    col_keep = jnp.repeat(live, HD)
    keep_share = lax.dynamic_slice_in_dim(keep_rows, row_start, share_rows, 0)
    centre_share = lax.dynamic_slice_in_dim(centres, row_start, share_rows, 1)

    def attend(parts):
        query, keys, values, keep = parts
        scores, allowed = block_scores(query, keys, keep, score_scale)
        top = jnp.max(scores, axis=-1, keepdims=True)
        expo = jnp.exp(scores - top)
        total = jnp.sum(expo, axis=-1, keepdims=True)
        probs = (expo / total).astype(jnp.bfloat16)
        mixed = jnp.einsum("sqk,ksd->qsd", probs, values, preferred_element_type=jnp.float32)
        return (mixed, (top + jnp.log(total))[..., 0])

    def attend_back(parts):
        query, keys, values, keep, grad_out, log_total = parts
        scores, allowed = block_scores(query, keys, keep, score_scale)
        probs = jnp.where(allowed[None], jnp.exp(scores - log_total[..., None]), 0.0)
        probs_low = probs.astype(jnp.bfloat16)
        grad_values = jnp.einsum(
            "sqk,qsd->ksd", probs_low, grad_out, preferred_element_type=jnp.float32
        )
        grad_probs = jnp.einsum(
            "qsd,ksd->sqk", grad_out, values, preferred_element_type=jnp.float32
        )
        inner = jnp.sum(probs * grad_probs, axis=-1, keepdims=True)
        grad_scores = (probs * (grad_probs - inner)).astype(jnp.bfloat16)
        grad_query = (
            jnp.einsum("sqk,ksd->qsd", grad_scores, keys, preferred_element_type=jnp.float32)
            * score_scale
        )
        grad_keys = (
            jnp.einsum("sqk,qsd->ksd", grad_scores, query, preferred_element_type=jnp.float32)
            * score_scale
        )
        return (grad_query, grad_keys, grad_values)

    gathered = (
        lax.all_gather(qkv_weight.astype(jnp.bfloat16), "dp", axis=1, tiled=True),
        lax.all_gather(out_weight.astype(jnp.bfloat16), "dp", axis=1, tiled=True),
        lax.all_gather(up_weight.astype(jnp.bfloat16), "dp", axis=0, tiled=True),
        lax.all_gather(down_weight.astype(jnp.bfloat16), "dp", axis=1, tiled=True),
    )
    proj_low = pos_proj.astype(jnp.bfloat16)
    qkv_low = gathered[0] * col_keep.astype(jnp.bfloat16)
    out_low = gathered[1]
    up_low = gathered[2]
    down_low = gathered[3]
    pre_pos = jnp.dot(centres.T, pos_hidden[:3], precision=highest) + pos_hidden[3]
    hidden_pos = gelu_exact(pre_pos).astype(jnp.bfloat16)
    stream_in = feats.astype(jnp.float32) + (
        jnp.dot(hidden_pos, proj_low, preferred_element_type=jnp.float32) + norm_vectors[6]
    )
    normed_one = layer_norm(stream_in, norm_vectors[0], norm_vectors[2]).astype(jnp.bfloat16)
    projected = jnp.einsum(
        "rd,tdc->trc", normed_one, qkv_low, preferred_element_type=jnp.float32
    ).astype(jnp.bfloat16)
    heads_view = projected.reshape(3, block_count, block_rows, local_slots, HD)
    keep_blocks = keep_rows.reshape(block_count, block_rows)
    mixed, log_total = lax.map(attend, (heads_view[0], heads_view[1], heads_view[2], keep_blocks))
    attn_low = mixed.reshape(row_count, slot_cols).astype(jnp.bfloat16)
    attn_term = jnp.dot(attn_low, out_low, preferred_element_type=jnp.float32)
    stream_share = lax.dynamic_slice_in_dim(stream_in, row_start, share_rows, 0)
    attn_full = lax.psum(attn_term, "mp")
    middle = stream_in + attn_full + norm_vectors[4]
    normed_two = layer_norm(middle, norm_vectors[1], norm_vectors[3]).astype(jnp.bfloat16)
    middle_share = lax.dynamic_slice_in_dim(middle, row_start, share_rows, 0)
    pre_up = jnp.dot(normed_two, up_low, preferred_element_type=jnp.float32) + up_bias
    activated = gelu_exact(pre_up).astype(jnp.bfloat16)
    mlp_term = jnp.dot(activated, down_low, preferred_element_type=jnp.float32)
    mlp_full = lax.psum(mlp_term.astype(jnp.bfloat16), "mp").astype(jnp.float32)
    mlp_share = lax.dynamic_slice_in_dim(mlp_full, row_start, share_rows, 0)
    block_out = ((middle_share + mlp_share + norm_vectors[5]) * keep_share[:, None]).astype(
        jnp.bfloat16
    )
    grad_top = cotangent * keep_rows[:, None].astype(jnp.bfloat16)
    down_grad = jnp.einsum("rf,rd->fd", activated, grad_top, preferred_element_type=jnp.float32)
    grad_act = jnp.einsum("rd,fd->rf", grad_top, down_low, preferred_element_type=jnp.float32)
    grad_pre = jax.vjp(gelu_exact, pre_up)[1](grad_act)[0].astype(jnp.bfloat16)
    bias_term = jnp.sum(grad_pre, axis=0, dtype=jnp.float32)
    up_grad = jnp.einsum("rd,rf->df", normed_two, grad_pre, preferred_element_type=jnp.float32)
    normed_two_grad = jnp.einsum("rf,df->rd", grad_pre, up_low, preferred_element_type=jnp.float32)
    two_share = lax.psum_scatter(normed_two_grad, "mp", scatter_dimension=0, tiled=True)
    middle_norm, gain_two, shift_two = jax.vjp(
        layer_norm, middle_share, norm_vectors[1], norm_vectors[3]
    )[1](two_share)
    top_share = lax.dynamic_slice_in_dim(grad_top, row_start, share_rows, 0).astype(jnp.float32)
    middle_grad = top_share + middle_norm
    middle_rows = lax.all_gather(middle_grad.astype(jnp.bfloat16), "mp", axis=0, tiled=True)
    out_grad = jnp.einsum("rc,rd->cd", attn_low, middle_rows, preferred_element_type=jnp.float32)
    attn_grad = jnp.einsum(
        "rd,cd->rc", middle_rows, out_low, preferred_element_type=jnp.float32
    ).astype(jnp.bfloat16)
    grad_query, grad_keys, grad_values = lax.map(
        attend_back,
        (
            heads_view[0],
            heads_view[1],
            heads_view[2],
            keep_blocks,
            attn_grad.reshape(block_count, block_rows, local_slots, HD),
            log_total,
        ),
    )
    grad_proj = (
        jnp.stack((grad_query, grad_keys, grad_values))
        .reshape(3, row_count, slot_cols)
        .astype(jnp.bfloat16)
    )
    qkv_grad = (
        jnp.einsum("rd,trc->tdc", normed_one, grad_proj, preferred_element_type=jnp.float32)
        * col_keep
    )
    qkv_grad, out_grad, up_grad, down_grad = (
        lax.psum_scatter(qkv_grad, "dp", scatter_dimension=1, tiled=True),
        lax.psum_scatter(out_grad, "dp", scatter_dimension=1, tiled=True),
        lax.psum_scatter(up_grad, "dp", scatter_dimension=0, tiled=True),
        lax.psum_scatter(down_grad, "dp", scatter_dimension=1, tiled=True),
    )
    normed_one_grad = jnp.einsum(
        "trc,tdc->rd", grad_proj, qkv_low, preferred_element_type=jnp.float32
    )
    one_share = lax.psum_scatter(normed_one_grad, "mp", scatter_dimension=0, tiled=True)
    stream_norm, gain_one, shift_one = jax.vjp(
        layer_norm, stream_share, norm_vectors[0], norm_vectors[2]
    )[1](one_share)
    feats_grad = middle_grad + stream_norm
    hidden_share = lax.dynamic_slice_in_dim(hidden_pos, row_start, share_rows, 0)
    pre_share = lax.dynamic_slice_in_dim(pre_pos, row_start, share_rows, 0)
    bias_cols = bias_term.shape[0]
    bias_whole = lax.dynamic_update_slice_in_dim(
        jnp.zeros((bias_cols * mp_count,), jnp.float32), bias_term, mp_index * bias_cols, 0
    )
    pos_low = feats_grad.astype(jnp.bfloat16)
    proj_grad = jnp.einsum("rh,rd->hd", hidden_share, pos_low, preferred_element_type=jnp.float32)
    hidden_grad = jnp.einsum("rd,hd->rh", pos_low, proj_low, preferred_element_type=jnp.float32)
    pre_grad = jax.vjp(gelu_exact, pre_share)[1](hidden_grad)[0]
    pos_grad = jnp.concatenate(
        (jnp.dot(centre_share, pre_grad, precision=highest), jnp.sum(pre_grad, axis=0)[None]),
        axis=0,
    )
    vector_grad = jnp.stack(
        (
            gain_one,
            gain_two,
            shift_one,
            shift_two,
            jnp.sum(middle_grad, axis=0),
            jnp.sum(top_share, axis=0),
            jnp.sum(feats_grad, axis=0),
        )
    )
    vector_grad, pos_grad, proj_grad, bias_whole = lax.psum(
        (vector_grad, pos_grad, proj_grad, bias_whole), ("dp", "mp")
    )
    bias_cols = up_bias.shape[0]
    bias_grad = lax.dynamic_slice_in_dim(bias_whole, mp_index * bias_cols, bias_cols, 0)
    leader = ((dp_index == 0) & (mp_index == 0)).astype(jnp.float32)
    first_dp = (dp_index == 0).astype(jnp.float32)
    owners = [1.0, 1.0, 1.0, first_dp, 1.0, leader, leader, leader]
    weights = [
        qkv_weight,
        out_weight,
        up_weight,
        up_bias,
        down_weight,
        norm_vectors,
        pos_hidden,
        pos_proj,
    ]
    moments = [
        qkv_moment,
        out_moment,
        up_moment,
        bias_moment,
        down_moment,
        vector_moment,
        hidden_moment,
        proj_moment,
    ]
    seconds = [
        qkv_second,
        out_second,
        up_second,
        bias_second,
        down_second,
        vector_second,
        hidden_second,
        proj_second,
    ]
    grads = [qkv_grad, out_grad, up_grad, bias_grad, down_grad, vector_grad, pos_grad, proj_grad]
    grad_square = jnp.zeros((), jnp.float32)
    weight_square = []
    for tensor_index in range(8):
        grad_square = grad_square + owners[tensor_index] * jnp.sum(
            grads[tensor_index] * grads[tensor_index]
        )
        weight_square.append(
            owners[tensor_index] * piece_squares(weights[tensor_index], tensor_index)
        )
    grad_total, weight_total = lax.psum((grad_square, jnp.concatenate(weight_square)), ("dp", "mp"))
    clip_norm = jnp.sqrt(grad_total)
    factor = jnp.minimum(1.0, clip_max / (clip_norm + 1e-06))
    clipped_list = []
    moment_list = []
    second_list = []
    direction_list = []
    update_square = []
    for tensor_index in range(8):
        clipped = grads[tensor_index] * factor
        moment_new = beta_one * moments[tensor_index] + (1.0 - beta_one) * clipped
        second_new = beta_two * seconds[tensor_index] + (1.0 - beta_two) * clipped * clipped
        direction = (
            moment_new
            / (1.0 - beta_one**step_count)
            / (jnp.sqrt(second_new / (1.0 - beta_two**step_count)) + adam_eps)
            + decay_rate * weights[tensor_index]
        )
        clipped_list.append(clipped)
        moment_list.append(moment_new)
        second_list.append(second_new)
        direction_list.append(direction)
        update_square.append(owners[tensor_index] * piece_squares(direction, tensor_index))
    update_total = lax.psum(jnp.concatenate(update_square), ("dp", "mp"))
    weight_norm = jnp.sqrt(weight_total)
    update_norm = jnp.sqrt(update_total)
    trust_ratio = weight_norm / (update_norm + 1e-06)
    trust_norms = jnp.stack((weight_norm, update_norm))
    outputs = [block_out, feats_grad, clip_norm, trust_norms]
    for tensor_index in range(8):
        new_weight = (
            weights[tensor_index]
            - learn_rate * piece_ratio(trust_ratio, tensor_index) * direction_list[tensor_index]
        )
        outputs.append(clipped_list[tensor_index])
        outputs.append(new_weight)
        outputs.append(moment_list[tensor_index])
        outputs.append(second_list[tensor_index])
        outputs.append(new_weight.astype(jnp.bfloat16))
    return tuple(outputs)


def solution(mesh):
    in_specs = (
        P("dp", None),
        P(None, "dp"),
        P("dp"),
        P("dp", None),
        P(None, "dp", "mp"),
        P("mp", "dp"),
        P("dp", "mp"),
        P("mp"),
        P("mp", "dp"),
        P(),
        P(),
        P(),
        P(None, "dp", "mp"),
        P("mp", "dp"),
        P("dp", "mp"),
        P("mp"),
        P("mp", "dp"),
        P(),
        P(),
        P(),
        P(None, "dp", "mp"),
        P("mp", "dp"),
        P("dp", "mp"),
        P("mp"),
        P("mp", "dp"),
        P(),
        P(),
        P(),
    )
    out_specs = (
        P(("dp", "mp"), None),
        P(("dp", "mp"), None),
        P(),
        P(),
        P(None, "dp", "mp"),
        P(None, "dp", "mp"),
        P(None, "dp", "mp"),
        P(None, "dp", "mp"),
        P(None, "dp", "mp"),
        P("mp", "dp"),
        P("mp", "dp"),
        P("mp", "dp"),
        P("mp", "dp"),
        P("mp", "dp"),
        P("dp", "mp"),
        P("dp", "mp"),
        P("dp", "mp"),
        P("dp", "mp"),
        P("dp", "mp"),
        P("mp"),
        P("mp"),
        P("mp"),
        P("mp"),
        P("mp"),
        P("mp", "dp"),
        P("mp", "dp"),
        P("mp", "dp"),
        P("mp", "dp"),
        P("mp", "dp"),
        P(),
        P(),
        P(),
        P(),
        P(),
        P(),
        P(),
        P(),
        P(),
        P(),
        P(),
        P(),
        P(),
        P(),
        P(),
    )
    return jax.shard_map(shards, mesh=mesh, in_specs=in_specs, out_specs=out_specs, check_vma=False)
```

profile of v0, /device:TPU:0, one launch (start us, length us, event | category | flops | bytes accessed | tf_op | source)
XLA Modules:
  0.0 896.9 jit_solution(13360168621311204578)
XLA Ops:
  12.6 34.3 %all_gather.16 = bf16[128,384]{0,1:T(8,128)(2,1)} all-gather(bf16[128,48]{0,1:T(8,128)(2,1)S(1)} %convert_element_type.159), channel_id=1, replica_groups=mesh['dp'=8,'mp'=4] {'dp'}, dimensions={1}, use_global_device_ids=true | all-gather | bytes 110592 | tf_op jit(solution)/shard_map/all_gather | solution.py:140
  46.9 30.8 %all_gather.15 = bf16[3,384,128]{2,1,0:T(8,128)(2,1)S(1)} all-gather(bf16[3,48,128]{2,1,0:T(8,128)(2,1)S(1)} %convert_element_type.150), channel_id=1, replica_groups=mesh['dp'=8,'mp'=4] {'dp'}, dimensions={1}, use_global_device_ids=true | all-gather | bytes 331776 | tf_op jit(solution)/shard_map/all_gather | solution.py:139
  77.7 3.8 multiply_convert_fusion.2
  89.9 14.9 %while.30 = (s32[]{:T(128)}, bf16[4,608,2,64]{1,3,2,0:T(8,128)(2,1)S(1)}, f32[4,2,608]{2,1,0:T(2,128)}, bf16[4,608,2,64]{1,3,2,0:T(8,128)(2,1)S(1)}, f32[4,608]{...) while((s32[]{:T(128)}, ...), condition=%wide.region_5.6_spmd, body=%wide.region_2.5_spmd.sunk | while | flops 198883488 | bytes 11414693 | solution.py:160
  111.5 33.0 %all_gather.18 = bf16[384,384]{0,1:T(8,128)(2,1)} all-gather(bf16[384,48]{0,1:T(8,128)(2,1)S(1)} %convert_element_type.163), channel_id=1, replica_groups=mesh['dp'=8,'mp'=4] {'dp'}, dimensions={1}, use_global_device_ids=true | all-gather | bytes 331776 | tf_op jit(solution)/shard_map/all_gather | solution.py:142
  144.5 30.8 %all_gather.17 = bf16[384,384]{1,0:T(8,128)(2,1)S(1)} all-gather(bf16[48,384]{1,0:T(8,128)(2,1)S(1)} %convert_element_type.161), channel_id=1, replica_groups=mesh['dp'=8,'mp'=4] {'dp'}, dimensions={0}, use_global_device_ids=true | all-gather | bytes 331776 | tf_op jit(solution)/shard_map/all_gather | solution.py:141
  177.0 12.8 %all-reduce.8.cloned.1.call-done = f32[2432,384]{1,0:T(8,128)} async-done(((f32[2432,384]{1,0:T(8,128)}), f32[2432,384]{1,0:T(8,128)}) %all-reduce.8.cloned.1.call-update) | async-done | bytes 3735568 | tf_op jit(solution)/shard_map/psum | solution.py:164
  189.8 3.7 fusion.110
  197.5 4.6 convert_reduce_fusion
  203.4 3.2 fusion.116
  209.5 4.1 convolution_convert_fusion
  215.2 33.4 %reduce-scatter.6.cloned.1.call-done = f32[608,384]{1,0:T(8,128)} async-done(((f32[2432,384]{1,0:T(8,128)}), f32[608,384]{1,0:T(8,128)}) %reduce-scatter.6.cloned.1.call-update) | async-done | bytes 933904 | tf_op jit(solution)/shard_map/reduce_scatter | solution.py:183
  251.7 47.0 %all-reduce.10.cloned.1.call-done = bf16[2432,384]{1,0:T(8,128)(2,1)} async-done(((bf16[2432,384]{1,0:T(8,128)(2,1)}), bf16[2432,384]{1,0:T(8,128)(2,1)}) %all-reduce.10.cloned.1.call-update) | async-done | bytes 1867792 | tf_op jit(solution)/shard_map/psum | solution.py:171
  303.7 3.6 fusion.118
  307.3 4.1 fusion.119
  311.5 13.7 %all-gather.2.cloned.1.call-done = bf16[2432,384]{1,0:T(8,128)(2,1)} async-done(((bf16[608,384]{1,0:T(8,128)(2,1)}), bf16[2432,384]{1,0:T(8,128)(2,1)}) %all-gather.2.cloned.1.call-update) | async-done | bytes 1867792 | tf_op jit(solution)/shard_map/all_gather | solution.py:189
  328.9 2.9 copy.170
  334.6 34.3 %while.31 = (s32[]{:T(128)}, bf16[4,608,2,64]{1,3,2,0:T(8,128)(2,1)}, bf16[4,608,2,64]{1,3,2,0:T(8,128)(2,1)}, bf16[4,608,2,64]{1,3,2,0:T(8,128)(2,1)}, bf16[4,6...) while((s32[]{:T(128)}, ...), condition=%wide.region_17.18_spmd, body=%wide.region_15.17_spmd.sunk | while | flops 481462432 | bytes 43006592 | solution.py:194
  372.8 3.7 copy.189
  376.5 3.5 reshape.453
  380.0 3.7 copy.190
  383.7 3.3 reshape.454
  391.1 4.5 fusion.57
  398.0 3.2 convolution_bitcast_fusion
  407.7 47.5 %reduce-scatter.14.cloned.1.call-done = f32[384,48]{0,1:T(8,128)} async-done(((f32[384,384]{0,1:T(8,128)}), f32[384,48]{0,1:T(8,128)}) %reduce-scatter.14.cloned.1.call-update) | async-done | bytes 73744 | tf_op jit(solution)/shard_map/reduce_scatter | solution.py:218
  456.7 62.5 %reduce-scatter.10.cloned.1.call-done = f32[128,48]{0,1:T(8,128)} async-done(((f32[128,384]{0,1:T(8,128)}), f32[128,48]{0,1:T(8,128)}) %reduce-scatter.10.cloned.1.call-update) | async-done | bytes 24592 | tf_op jit(solution)/shard_map/reduce_scatter | solution.py:216
  520.5 76.4 %all-reduce.14.cloned.1.call-done = f32[3,384,128]{2,0,1:T(4,128)} async-done(((f32[3,384,128]{2,0,1:T(4,128)}), f32[3,384,128]{2,0,1:T(4,128)}) %all-reduce.14.cloned.1.call-update) | async-done | bytes 589840
  600.4 40.1 %reduce-scatter.8.cloned.1.call-done = f32[608,384]{1,0:T(8,128)} async-done(((f32[2432,384]{1,0:T(8,128)}), f32[608,384]{1,0:T(8,128)}) %reduce-scatter.8.cloned.1.call-update) | async-done | bytes 933904 | tf_op jit(solution)/shard_map/reduce_scatter | solution.py:223
  650.3 39.8 %all-reduce.2 = (f32[1536]{0:T(1024)S(1)}, f32[7,384]{1,0:T(8,128)S(1)}, f32[4,128]{1,0:T(4,128)S(1)}) all-reduce(f32[1536]{0:T(1024)S(1)} %dynamic_update_slice.35, f32[7,384]{1,0:T(8,128)S(1)} %stack.44, f32[4,128]{1,0:T(4,128)S(1)} %pad_maximum_fusion), channel_id=1, replica_groups=mesh['dp'=8,'mp'=4] {'dp','mp'}, use_global_device_ids=true, to_apply=%region_30.31 | all-reduce | flops 4736 | bytes 37888 | tf_op jit(solution)/shard_map/psum | solution.py:253
  694.6 78.5 %all-reduce.12.cloned.1.call-done = f32[128,384]{1,0:T(8,128)} async-done(((f32[128,384]{1,0:T(8,128)}), f32[128,384]{1,0:T(8,128)}) %all-reduce.12.cloned.1.call-update) | async-done | bytes 196624 | tf_op jit(solution)/shard_map/psum | solution.py:253
  775.3 41.2 %psum.69 = f32[]{:T(128)} all-reduce(f32[]{:T(128)S(6)} %add.444), channel_id=1, replica_groups=mesh['dp'=8,'mp'=4] {'dp','mp'}, use_global_device_ids=true, to_apply=%region_48.49 | all-reduce | flops 1 | bytes 8 | tf_op jit(solution)/shard_map/psum | solution.py:301
  837.4 40.1 %all-reduce.1 = (f32[14]{0:T(128)S(1)}, f32[14]{0:T(128)S(1)}) all-reduce(f32[14]{0:T(128)S(1)} %concatenate.13, f32[14]{0:T(128)S(1)} %concatenate.12), channel_id=1, replica_groups=mesh['dp'=8,'mp'=4] {'dp','mp'}, use_global_device_ids=true, to_apply=%region_66.67 | all-reduce | flops 28 | bytes 224 | tf_op jit(solution)/shard_map/psum | solution.py:324
  (426 shorter events, 151.0 us)
Async XLA Ops:
  7.3 182.5 %all-reduce.8.cloned.1.call-start = ((), (), s32[]{:S(2)}) async-start(), calls=%async_computation.5 | async-start | bytes 7471104 | tf_op jit(solution)/shard_map/psum | solution.py:164
  11.5 182.8 %copy-start.61 = (f32[384]{0:T(512)}, f32[384]{0:T(512)S(1)}, u32[]{:S(2)}) copy-start(f32[384]{0:T(512)S(1)} %get-tuple-element.490) | copy-start | bytes 4612
  110.6 138.0 %reduce-scatter.6.cloned.1.call-start = ((), (), s32[]{:S(2)}) async-start(), calls=%async_computation.7 | async-start | bytes 4669440 | tf_op jit(solution)/shard_map/reduce_scatter | solution.py:183
  206.7 92.0 %all-reduce.10.cloned.1.call-start = ((), (), s32[]{:S(2)}) async-start(), calls=%async_computation.6 | async-start | bytes 3735552 | tf_op jit(solution)/shard_map/psum | solution.py:171
  213.6 111.6 %all-gather.2.cloned.1.call-start = ((), (), s32[]{:S(2)}) async-start(), calls=%async_computation.8 | async-start | bytes 2334720 | tf_op jit(solution)/shard_map/all_gather | solution.py:189
  303.6 102.6 %reduce-scatter.12.cloned.1.call-start = ((), (), s32[]{:S(2)}) async-start(), calls=%async_computation.11 | async-start | bytes 663552 | tf_op jit(solution)/shard_map/reduce_scatter | solution.py:217
  307.3 147.9 %reduce-scatter.14.cloned.1.call-start = ((), (), s32[]{:S(2)}) async-start(), calls=%async_computation.12 | async-start | bytes 663552 | tf_op jit(solution)/shard_map/reduce_scatter | solution.py:218
  311.4 207.7 %reduce-scatter.10.cloned.1.call-start = ((), (), s32[]{:S(2)}) async-start(), calls=%async_computation.10 | async-start | bytes 221184 | tf_op jit(solution)/shard_map/reduce_scatter | solution.py:216
  389.8 207.1 %all-reduce.14.cloned.1.call-start = ((), (), s32[]{:S(2)}) async-start(), calls=%async_computation.14 | async-start | bytes 1572864
  397.9 242.5 %reduce-scatter.8.cloned.1.call-start = ((), (), s32[]{:S(2)}) async-start(), calls=%async_computation.9 | async-start | bytes 4669440 | tf_op jit(solution)/shard_map/reduce_scatter | solution.py:223
  401.2 239.3 %copy-start.68 = (f32[384]{0:T(512)S(1)}, f32[384]{0:T(512)}, u32[]{:S(2)}) copy-start(f32[384]{0:T(512)} %copy-done.67) | copy-start | bytes 4612
  401.2 371.8 %all-reduce.12.cloned.1.call-start = ((), (), s32[]{:S(2)}) async-start(), calls=%async_computation.13 | async-start | bytes 393216 | tf_op jit(solution)/shard_map/psum | solution.py:253
  644.4 177.9 %copy-start.45 = (f32[7,384]{1,0:T(8,128)S(1)}, f32[7,384]{1,0:T(8,128)}, u32[]{:S(2)}) copy-start(f32[7,384]{1,0:T(8,128)} %param.41) | copy-start | bytes 32260
  644.4 177.9 %copy-start.71 = (f32[7,384]{1,0:T(8,128)S(1)}, f32[7,384]{1,0:T(8,128)}, u32[]{:S(2)}) copy-start(f32[7,384]{1,0:T(8,128)} %param.49) | copy-start | bytes 32260
  644.4 177.9 %copy-start.72 = (f32[7,384]{1,0:T(8,128)S(1)}, f32[7,384]{1,0:T(8,128)}, u32[]{:S(2)}) copy-start(f32[7,384]{1,0:T(8,128)} %param.57) | copy-start | bytes 32260
  644.4 178.6 %copy-start.43 = (f32[128,384]{1,0:T(8,128)S(1)}, f32[128,384]{1,0:T(8,128)}, u32[]{:S(2)}) copy-start(f32[128,384]{1,0:T(8,128)} %param.51) | copy-start | bytes 589828
  644.5 178.6 %copy-start.44 = (f32[128,384]{1,0:T(8,128)S(1)}, f32[128,384]{1,0:T(8,128)}, u32[]{:S(2)}) copy-start(f32[128,384]{1,0:T(8,128)} %param.59) | copy-start | bytes 589828
  645.9 184.8 %copy-start.4 = (f32[608,384]{1,0:T(8,128)}, f32[608,384]{1,0:T(8,128)S(1)}, u32[]{:S(2)}) copy-start(f32[608,384]{1,0:T(8,128)S(1)} %get-tuple-element.597) | copy-start | bytes 2801668
  645.9 180.9 %copy-start.33 = (f32[3,48,128]{2,1,0:T(8,128)S(1)}, f32[3,48,128]{2,1,0:T(8,128)}, u32[]{:S(2)}) copy-start(f32[3,48,128]{2,1,0:T(8,128)} %param.36) | copy-start | bytes 221188
  645.9 180.9 %copy-start.49 = (f32[3,48,128]{2,1,0:T(8,128)S(1)}, f32[3,48,128]{2,1,0:T(8,128)}, u32[]{:S(2)}) copy-start(f32[3,48,128]{2,1,0:T(8,128)} %param.44) | copy-start | bytes 221188
  645.9 180.9 %copy-start.50 = (f32[3,48,128]{2,1,0:T(8,128)S(1)}, f32[3,48,128]{2,1,0:T(8,128)}, u32[]{:S(2)}) copy-start(f32[3,48,128]{2,1,0:T(8,128)} %param.52) | copy-start | bytes 221188
  646.0 182.1 %copy-start.42 = (f32[128,48]{0,1:T(8,128)S(1)}, f32[128,48]{0,1:T(8,128)}, u32[]{:S(2)}) copy-start(f32[128,48]{0,1:T(8,128)} %param.37) | copy-start | bytes 73732
  646.0 182.1 %copy-start.48 = (f32[128,48]{0,1:T(8,128)S(1)}, f32[128,48]{0,1:T(8,128)}, u32[]{:S(2)}) copy-start(f32[128,48]{0,1:T(8,128)} %reduce-scatter.10.cloned.1.call-done) | copy-start | bytes 73732
  646.0 182.1 %copy-start.65 = (f32[128,48]{0,1:T(8,128)S(1)}, f32[128,48]{0,1:T(8,128)}, u32[]{:S(2)}) copy-start(f32[128,48]{0,1:T(8,128)} %param.45) | copy-start | bytes 73732
  646.0 182.1 %copy-start.66 = (f32[128,48]{0,1:T(8,128)S(1)}, f32[128,48]{0,1:T(8,128)}, u32[]{:S(2)}) copy-start(f32[128,48]{0,1:T(8,128)} %param.53) | copy-start | bytes 73732
  646.0 183.4 %copy-start.35 = (f32[384,48]{0,1:T(8,128)S(1)}, f32[384,48]{0,1:T(8,128)}, u32[]{:S(2)}) copy-start(f32[384,48]{0,1:T(8,128)} %reduce-scatter.14.cloned.1.call-done) | copy-start | bytes 221188
  646.0 183.4 %copy-start.51 = (f32[384,48]{0,1:T(8,128)S(1)}, f32[384,48]{0,1:T(8,128)}, u32[]{:S(2)}) copy-start(f32[384,48]{0,1:T(8,128)} %param.48) | copy-start | bytes 221188
  646.0 183.4 %copy-start.52 = (f32[384,48]{0,1:T(8,128)S(1)}, f32[384,48]{0,1:T(8,128)}, u32[]{:S(2)}) copy-start(f32[384,48]{0,1:T(8,128)} %param.56) | copy-start | bytes 221188
  646.0 184.7 %copy-start.32 = (f32[48,384]{1,0:T(8,128)S(1)}, f32[48,384]{1,0:T(8,128)}, u32[]{:S(2)}) copy-start(f32[48,384]{1,0:T(8,128)} %param.38) | copy-start | bytes 221188
  646.1 184.7 %copy-start.34 = (f32[48,384]{1,0:T(8,128)S(1)}, f32[48,384]{1,0:T(8,128)}, u32[]{:S(2)}) copy-start(f32[48,384]{1,0:T(8,128)} %reduce-scatter.12.cloned.1.call-done) | copy-start | bytes 221188
  646.1 184.6 %copy-start.53 = (f32[48,384]{1,0:T(8,128)S(1)}, f32[48,384]{1,0:T(8,128)}, u32[]{:S(2)}) copy-start(f32[48,384]{1,0:T(8,128)} %param.46) | copy-start | bytes 221188
  646.1 184.6 %copy-start.54 = (f32[48,384]{1,0:T(8,128)S(1)}, f32[48,384]{1,0:T(8,128)}, u32[]{:S(2)}) copy-start(f32[48,384]{1,0:T(8,128)} %param.54) | copy-start | bytes 221188
  (87 other events, 2695.6 us)
Sparse Core Ops, SparseCore 0:
  110.7 78.9 all-reduce.7
  206.8 41.7 reduce-scatter.5
  251.0 47.6 all-reduce.9
  303.8 21.3 all-gather.1
  328.3 62.0 reduce-scatter.11
  393.9 61.2 reduce-scatter.13
  459.0 60.1 reduce-scatter.9
  523.2 73.7 all-reduce.13
  599.6 40.7 reduce-scatter.7
  650.0 123.0 all-reduce.11
where the time goes:
time: 903 us; the launch traced here: 897 us
  waiting for transfers between devices  412 us (46%)
  blocking collectives  250 us (28%)
  matrix products  73.6 us (8%)
  other arithmetic  65.6 us (7%)
  local copies, waits for them, and re-layouts  63.1 us (7%)
  between operations  31.8 us (4%)
    psum x1, waiting for transfers between devices, shards(): lax.psum((vector_grad, pos_grad, proj_grad, bias_whole), ('dp', 'mp'))  78.5 us
    unnamed x11, waiting for transfers between devices  76.5 us
    reduce_scatter x1, waiting for transfers between devices, shards(): lax.psum_scatter(out_grad, 'dp', scatter_dimension=1, tiled=True)  62.5 us
    reduce_scatter x1, waiting for transfers between devices, shards(): lax.psum_scatter(down_grad, 'dp', scatter_dimension=1, tiled=True)  47.5 us
    psum x1, waiting for transfers between devices, shards(): mlp_full = lax.psum(mlp_term.astype(jnp.bfloat16), 'mp').astype(jnp.float32)  47 us
    psum x1, blocking collectives, shards(): lax.psum((grad_square, jnp.concatenate(weight_square)), ('dp', 'mp'))  41.2 us
    psum x1, blocking collectives, shards(): update_total = lax.psum(jnp.concatenate(update_square), ('dp', 'mp'))  40.1 us
    reduce_scatter x1, waiting for transfers between devices, shards(): lax.psum_scatter(normed_one_grad, 'mp', scatter_dimension=0, tiled=True)  40.1 us
  transfers between devices with their start and end apart: 10, of which 9 were waited for; matrix products, arithmetic and copies ran while one was open for 11% of the time, Pallas kernels for 0%

commit v1 on v0

v1 whole, which is shorter than its diff:
```python
import functools
import math

import jax
import jax.numpy as jnp
from jax import lax
from jax.experimental import pallas as pl
from jax.experimental.pallas import tpu as pltpu
from jax.sharding import PartitionSpec as P

HD = 64
PAD = 38
SLOT = 40
GROUP = 4

norm_eps = 1e-05
beta_one = 0.5
beta_two = 0.5
adam_eps = 1e-06
decay_rate = 0.01
learn_rate = 0.3
clip_max = 1.0
step_count = 3.0
neg_fill = -1e30
highest = lax.Precision.HIGHEST
f32 = jnp.float32
bf16 = jnp.bfloat16

NN = (((1,), (0,)), ((), ()))
NT = (((1,), (1,)), ((), ()))
TN = (((0,), (0,)), ((), ()))


def dot(a, b, dims=NN, precision=None):
    return lax.dot_general(a, b, dims, precision=precision, preferred_element_type=f32)


def gelu_pair(v):
    cdf = 0.5 * (1.0 + lax.erf(v * 0.7071067811865476))
    return v * cdf, cdf + v * jnp.exp(-0.5 * v * v) * 0.3989422804014327


def piece_squares(array, tensor_index):
    if tensor_index == 5:
        return jnp.sum(array * array, axis=1)
    return jnp.sum(array * array)[None]


def piece_ratio(trust_ratio, tensor_index):
    if tensor_index < 5:
        return trust_ratio[tensor_index]
    if tensor_index == 5:
        return trust_ratio[5:12][:, None]
    return trust_ratio[tensor_index + 6]


class Layer:
    def __init__(self, refs, mp, clouds, width, inner):
        self.__dict__.update(refs)
        self.mp = mp
        self.clouds = clouds
        self.width = width
        self.inner = inner
        self.rows = clouds * SLOT
        self.block = GROUP * SLOT
        self.blocks = clouds // GROUP
        self.tile = self.rows // 2 if self.rows % 32 == 0 else self.rows
        self.hid = self.proj_low.shape[0]

    def live(self, j):
        return [h for h in range(2) if (2 * j + h) % 2 == 0 or j < self.mp // 2]

    def spread_rows(self):
        zeros = jnp.zeros((SLOT - PAD, self.width), f32)
        self.stage[...] = self.feats[...].astype(f32)
        for c in range(self.clouds):
            self.stream[pl.ds(SLOT * c, PAD), :] = self.stage[pl.ds(PAD * c, PAD), :]
            self.stream[pl.ds(SLOT * c + PAD, SLOT - PAD), :] = zeros
        self.stage[...] = self.cotangent[...].astype(f32)
        for c in range(self.clouds):
            self.middle_grad[pl.ds(SLOT * c, PAD), :] = self.stage[pl.ds(PAD * c, PAD), :]
            self.middle_grad[pl.ds(SLOT * c + PAD, SLOT - PAD), :] = zeros

    def keep_block(self, b, shape, dim):
        place = lax.broadcasted_iota(jnp.int32, shape, dim)
        bound = jnp.zeros(shape, jnp.int32)
        for i in range(GROUP):
            limit = self.counts[b * GROUP + i] + SLOT * i
            inside = (place >= SLOT * i) & (place < limit)
            bound = jnp.where(inside, 1, bound)
        return bound > 0

    def masks(self):
        n = self.block

        def step(b, carry):
            keys = lax.broadcasted_iota(jnp.int32, (n, n), 0)
            query = lax.broadcasted_iota(jnp.int32, (n, n), 1)
            fill = jnp.full((n, n), neg_fill, f32)
            for i in range(GROUP):
                limit = self.counts[b * GROUP + i] + SLOT * i
                inside = (keys >= SLOT * i) & (keys < limit)
                mine = (query >= SLOT * i) & (query < SLOT * (i + 1))
                fill = jnp.where(inside & mine, 0.0, fill)
            self.mask[b] = fill
            self.keep[pl.ds(b * n, n), :] = jnp.where(self.keep_block(b, (n, 128), 0), 1.0, 0.0)
            return carry

        lax.fori_loop(0, self.blocks, step, 0)

    def norm(self, x):
        centre = x - jnp.mean(x, axis=-1, keepdims=True)
        spread = jnp.mean(centre * centre, axis=-1, keepdims=True)
        rate = lax.rsqrt(spread + norm_eps)
        return centre * rate, rate

    def norm_back(self, grad, hat, rate, gain):
        scaled = grad * gain
        first = jnp.mean(scaled, axis=-1, keepdims=True)
        second = jnp.mean(scaled * hat, axis=-1, keepdims=True)
        return rate * (scaled - first - hat * second)

    def entry(self):
        t = self.tile

        def step(i, carry):
            rows = pl.ds(i * t, t)
            pre = dot(self.points[rows, :], self.pos_hidden[...], NN, highest)
            value, slope = gelu_pair(pre)
            hidden = value.astype(bf16)
            self.pos_slope[rows, :] = slope
            self.hidden[rows, :] = hidden
            term = dot(hidden, self.proj_low[...]) + self.vec[6:7, :]
            x = self.stream[rows, :] + term
            hat, rate = self.norm(x)
            self.stream[rows, :] = x
            self.hat_one[rows, :] = hat
            self.rate_one[rows, :] = jnp.broadcast_to(rate, (t, 128))
            self.normed_one[rows, :] = (hat * self.vec[0:1, :] + self.vec[2:3, :]).astype(bf16)
            return carry

        lax.fori_loop(0, self.rows // t, step, 0)

    def project(self, j):
        w = self.width
        t = self.tile

        def step(i, carry):
            rows = pl.ds(i * t, t)
            self.qkv[j, rows, :] = dot(self.normed_one[rows, :], self.w_qkv(j)).astype(bf16)
            return carry

        lax.fori_loop(0, self.rows // t, step, 0)

    def lanes(self, h, n):
        lane = lax.broadcasted_iota(jnp.int32, (n, 128), 1)
        return (lane < HD) if h == 0 else (lane >= HD)

    def attend(self, j, first):
        n = self.block

        def step(b, carry):
            rows = pl.ds(b * n, n)
            query = self.qkv[j, rows, 0:128] * jnp.asarray(1.0 / math.sqrt(HD), bf16)
            keys = self.qkv[j, rows, 128:256]
            values = self.qkv[j, rows, 256:384]
            zero = jnp.zeros_like(query)
            mixed = jnp.zeros((n, 128), f32)
            for place, h in enumerate(self.live(j)):
                own = self.lanes(h, n)
                scores = dot(keys, jnp.where(own, query, zero), NT) + self.mask[b]
                top = jnp.max(scores, axis=0, keepdims=True)
                expo = jnp.exp(scores - top)
                total = jnp.sum(expo, axis=0, keepdims=True)
                probs = expo / total
                self.probs[first + place, b] = probs
                mixed = jnp.where(own, dot(probs.astype(bf16), values, TN), mixed)
            self.attn_low[j, rows, :] = mixed.astype(bf16)
            return carry

        lax.fori_loop(0, self.blocks, step, 0)

    def middle(self):
        t = self.tile

        def step(i, carry):
            rows = pl.ds(i * t, t)
            x = self.stream[rows, :] + self.vec[4:5, :]
            for j in range(self.mp):
                x = x + dot(self.attn_low[j, rows, :], self.w_out(j), NT)
            hat, rate = self.norm(x)
            self.stream[rows, :] = x
            self.hat_two[rows, :] = hat
            self.rate_two[rows, :] = jnp.broadcast_to(rate, (t, 128))
            self.normed_two[rows, :] = (hat * self.vec[1:2, :] + self.vec[3:4, :]).astype(bf16)
            return carry

        lax.fori_loop(0, self.rows // t, step, 0)

    def feed(self, j):
        t = self.tile

        def step(i, carry):
            rows = pl.ds(i * t, t)
            pre = dot(self.normed_two[rows, :], self.w_up(j)) + self.up_bias[j, 0:1, :]
            value, slope = gelu_pair(pre)
            low = value.astype(bf16)
            self.activated[j, rows, :] = low
            self.slope[j, rows, :] = slope
            self.stream[rows, :] += dot(low, self.w_down(j), NT)
            return carry

        lax.fori_loop(0, self.rows // t, step, 0)

    def top(self):
        t = self.tile

        def step(i, carry):
            rows = pl.ds(i * t, t)
            keep = jnp.concatenate([self.keep[rows, :]] * (self.width // 128), axis=1)
            self.stream[rows, :] = (self.stream[rows, :] + self.vec[5:6, :]) * keep
            grad = self.middle_grad[rows, :] * keep
            self.middle_grad[rows, :] = grad
            self.grad_top[rows, :] = grad.astype(bf16)
            self.vec_grad[5:6, :] += jnp.sum(grad, axis=0, keepdims=True)
            return carry

        self.vec_grad[...] = jnp.zeros_like(self.vec_grad)
        self.up_bias_grad[...] = jnp.zeros_like(self.up_bias_grad)
        lax.fori_loop(0, self.rows // t, step, 0)

    def feed_back(self, j):
        t = self.tile

        def step(i, carry):
            rows = pl.ds(i * t, t)
            grad = dot(self.grad_top[rows, :], self.w_down(j)) * self.slope[j, rows, :]
            low = grad.astype(bf16)
            self.grad_pre[j, rows, :] = low
            self.up_bias_grad[j, 0:1, :] += jnp.sum(low.astype(f32), axis=0, keepdims=True)
            term = dot(low, self.w_up(j), NT)
            if j == 0:
                self.normed_grad[rows, :] = term
            else:
                self.normed_grad[rows, :] += term
            return carry

        lax.fori_loop(0, self.rows // t, step, 0)

    def middle_back(self):
        t = self.tile

        def step(i, carry):
            rows = pl.ds(i * t, t)
            grad, hat = self.normed_grad[rows, :], self.hat_two[rows, :]
            rate = jnp.concatenate([self.rate_two[rows, :]] * (self.width // 128), axis=1)
            self.vec_grad[1:2, :] += jnp.sum(grad * hat, axis=0, keepdims=True)
            self.vec_grad[3:4, :] += jnp.sum(grad, axis=0, keepdims=True)
            out = self.middle_grad[rows, :] + self.norm_back(grad, hat, rate, self.vec[1:2, :])
            self.middle_grad[rows, :] = out
            self.vec_grad[4:5, :] += jnp.sum(out, axis=0, keepdims=True)
            self.middle_low[rows, :] = out.astype(bf16)
            return carry

        lax.fori_loop(0, self.rows // t, step, 0)

    def attend_grad(self, j):
        t = self.tile

        def step(i, carry):
            rows = pl.ds(i * t, t)
            self.attn_grad[j, rows, :] = dot(self.middle_low[rows, :], self.w_out(j)).astype(bf16)
            return carry

        lax.fori_loop(0, self.rows // t, step, 0)

    def attend_back(self, j, first):
        n = self.block

        def step(b, carry):
            rows = pl.ds(b * n, n)
            scale = 1.0 / math.sqrt(HD)
            query = self.qkv[j, rows, 0:128] * jnp.asarray(scale, bf16)
            keys = self.qkv[j, rows, 128:256]
            values = self.qkv[j, rows, 256:384]
            grad_out = self.attn_grad[j, rows, :]
            zero = jnp.zeros_like(query)
            grad_query = jnp.zeros((n, 128), f32)
            grad_keys = jnp.zeros((n, 128), f32)
            grad_values = jnp.zeros((n, 128), f32)
            for place, h in enumerate(self.live(j)):
                own = self.lanes(h, n)
                mine = jnp.where(own, grad_out, zero)
                probs = self.probs[first + place, b]
                grad_probs = dot(values, mine, NT)
                grad_values = grad_values + dot(probs.astype(bf16), mine)
                inner = jnp.sum(probs * grad_probs, axis=0, keepdims=True)
                grad_scores = (probs * (grad_probs - inner)).astype(bf16)
                grad_keys = grad_keys + dot(grad_scores, jnp.where(own, query, zero))
                grad_query = jnp.where(own, dot(grad_scores, keys, TN), grad_query)
            self.grad_proj[j, rows, 0:128] = (grad_query * scale).astype(bf16)
            self.grad_proj[j, rows, 128:256] = grad_keys.astype(bf16)
            self.grad_proj[j, rows, 256:384] = grad_values.astype(bf16)
            return carry

        lax.fori_loop(0, self.blocks, step, 0)

    def entry_back(self):
        t = self.tile

        def step(i, carry):
            rows = pl.ds(i * t, t)
            grad = jnp.zeros((t, self.width), f32)
            for j in range(self.mp):
                grad = grad + dot(self.grad_proj[j, rows, :], self.w_qkv(j), NT)
            hat = self.hat_one[rows, :]
            rate = jnp.concatenate([self.rate_one[rows, :]] * (self.width // 128), axis=1)
            self.vec_grad[0:1, :] += jnp.sum(grad * hat, axis=0, keepdims=True)
            self.vec_grad[2:3, :] += jnp.sum(grad, axis=0, keepdims=True)
            out = self.middle_grad[rows, :] + self.norm_back(grad, hat, rate, self.vec[0:1, :])
            self.middle_grad[rows, :] = out
            self.vec_grad[6:7, :] += jnp.sum(out, axis=0, keepdims=True)
            low = out.astype(bf16)
            self.pos_low[rows, :] = low
            self.pre_grad[rows, :] = dot(low, self.proj_low[...], NT) * self.pos_slope[rows, :]
            return carry

        lax.fori_loop(0, self.rows // t, step, 0)

    def turn(self, source, target):
        n = 128

        def step(i, carry):
            block = source[pl.ds(i * n, n), :].astype(f32)
            target[:, pl.ds(pl.multiple_of(i * n, n), n)] = block.T.astype(bf16)
            return carry

        lax.fori_loop(0, self.rows // n, step, 0)

    def gather_rows(self, source, target):
        for c in range(self.clouds):
            target[pl.ds(PAD * c, PAD), :] = source[pl.ds(SLOT * c, PAD), :]


def layer_scratch(mp, clouds, width, inner, hid):
    rows = clouds * SLOT
    block = GROUP * SLOT
    cols = inner // mp
    heads = mp + mp // 2
    shapes = dict(
        stage=((clouds * PAD, width), f32),
        stream=((rows, width), f32),
        middle_grad=((rows, width), f32),
        mask=((clouds // GROUP, block, block), f32),
        keep=((rows, 128), f32),
        pos_slope=((rows, hid), f32),
        hidden=((rows, hid), bf16),
        hat_one=((rows, width), f32),
        rate_one=((rows, 128), f32),
        normed_one=((rows, width), bf16),
        qkv=((mp, rows, 384), bf16),
        probs=((heads, clouds // GROUP, block, block), f32),
        attn_low=((mp, rows, 128), bf16),
        hat_two=((rows, width), f32),
        rate_two=((rows, 128), f32),
        normed_two=((rows, width), bf16),
        activated=((mp, rows, cols), bf16),
        slope=((mp, rows, cols), f32),
        grad_top=((rows, width), bf16),
        grad_pre=((mp, rows, cols), bf16),
        normed_grad=((rows, width), f32),
        middle_low=((rows, width), bf16),
        attn_grad=((mp, rows, 128), bf16),
        grad_proj=((mp, rows, 384), bf16),
        pos_low=((rows, width), bf16),
        pre_grad=((rows, hid), f32),
        turned=((width, rows), bf16),
    )
    return shapes


def heads_before(mp, j):
    return sum(2 if i < mp // 2 else 1 for i in range(j))


def compute_kernel(names, mp, clouds, width, inner, *args):
    refs = dict(zip(names, args))
    layer = Layer(refs, mp, clouds, width, inner)
    w = layer.w
    cols = inner // mp
    layer.w_qkv = lambda j: w[j, :, 0:384]
    layer.w_out = lambda j: w[j, :, 384:512]
    layer.w_up = lambda j: w[j, :, 512 : 512 + cols]
    layer.w_down = lambda j: w[j, :, 512 + cols : 512 + 2 * cols]
    layer.proj_low[...] = layer.pos_proj[...].astype(bf16)
    layer.spread_rows()
    layer.masks()
    layer.entry()
    for j in range(mp):
        layer.project(j)
        layer.attend(j, heads_before(mp, j))
    layer.middle()
    for j in range(mp):
        layer.feed(j)
    layer.top()
    layer.gather_rows(layer.stream, layer.stage)
    layer.block_out[...] = layer.stage[...].astype(bf16)
    for j in range(mp):
        layer.feed_back(j)
    g = layer.grads
    layer.turn(layer.grad_top, layer.turned)
    for j in range(mp):
        g[j, :, 512 + cols : 512 + 2 * cols] = dot(layer.turned[...], layer.activated[j])
    layer.turn(layer.normed_two, layer.turned)
    for j in range(mp):
        g[j, :, 512 : 512 + cols] = dot(layer.turned[...], layer.grad_pre[j])
    layer.middle_back()
    layer.turn(layer.middle_low, layer.turned)
    for j in range(mp):
        g[j, :, 384:512] = dot(layer.turned[...], layer.attn_low[j])
        layer.attend_grad(j)
        layer.attend_back(j, heads_before(mp, j))
    layer.turn(layer.normed_one, layer.turned)
    for j in range(mp):
        g[j, :, 0:384] = dot(layer.turned[...], layer.grad_proj[j])
    layer.entry_back()
    layer.gather_rows(layer.middle_grad, layer.feats_grad)
    layer.proj_grad[...] = dot(layer.hidden[...], layer.pos_low[...], TN)
    layer.pos_grad[...] = dot(layer.points[...], layer.pre_grad[...], TN, highest)


def compute(mp, width, inner, counts, feats, cotangent, points, w, up_bias, vec, pos_hidden, pos_proj):
    clouds = counts.shape[0]
    hid = pos_proj.shape[0]
    inputs = ["counts", "feats", "cotangent", "points", "w", "up_bias", "vec", "pos_hidden", "pos_proj"]
    outs = dict(
        block_out=((clouds * PAD, width), bf16),
        feats_grad=((clouds * PAD, width), f32),
        grads=(w.shape, f32),
        up_bias_grad=((mp, 8, inner // mp), f32),
        vec_grad=((8, width), f32),
        pos_grad=((8, hid), f32),
        proj_grad=((hid, width), f32),
    )
    scratch = layer_scratch(mp, clouds, width, inner, hid)
    scratch["proj_low"] = ((hid, width), bf16)
    names = inputs + list(outs) + list(scratch)
    vmem = pl.BlockSpec(memory_space=pltpu.VMEM)
    return pl.pallas_call(
        functools.partial(compute_kernel, names, mp, clouds, width, inner),
        out_shape=[jax.ShapeDtypeStruct(*v) for v in outs.values()],
        in_specs=[pl.BlockSpec(memory_space=pltpu.SMEM)] + [vmem] * (len(inputs) - 1),
        out_specs=[vmem] * len(outs),
        scratch_shapes=[pltpu.VMEM(*v) for v in scratch.values()],
        compiler_params=pltpu.CompilerParams(vmem_limit_bytes=60 * 1024 * 1024),
    )(counts, feats, cotangent, points, w, up_bias, vec, pos_hidden, pos_proj)


def shards(
    feats,
    centres,
    counts,
    cotangent,
    qkv_weight,
    out_weight,
    up_weight,
    up_bias,
    down_weight,
    norm_vectors,
    pos_hidden,
    pos_proj,
    qkv_moment,
    out_moment,
    up_moment,
    bias_moment,
    down_moment,
    vector_moment,
    hidden_moment,
    proj_moment,
    qkv_second,
    out_second,
    up_second,
    bias_second,
    down_second,
    vector_second,
    hidden_second,
    proj_second,
):
    mp_count = lax.axis_size("mp")
    mp_index = lax.axis_index("mp")
    dp_index = lax.axis_index("dp")
    share = feats.shape[0] // mp_count
    clouds = share // PAD
    width = feats.shape[1]
    cols = up_weight.shape[1]
    inner = cols * mp_count
    start = mp_index * share
    my_feats = lax.dynamic_slice_in_dim(feats, start, share, 0)
    my_top = lax.dynamic_slice_in_dim(cotangent, start, share, 0)
    my_counts = lax.dynamic_slice_in_dim(counts, mp_index * clouds, clouds, 0)
    my_points = lax.dynamic_slice_in_dim(centres, start, share, 1).T.reshape(clouds, PAD, 3)
    points = jnp.pad(my_points, ((0, 0), (0, SLOT - PAD), (0, 0)))
    points = jnp.concatenate((points, jnp.ones((clouds, SLOT, 1), f32)), axis=2)
    points = jnp.pad(points.reshape(clouds * SLOT, 4), ((0, 0), (0, 4)))
    packed = jnp.concatenate(
        (qkv_weight[0], qkv_weight[1], qkv_weight[2], out_weight.T, up_weight, down_weight.T), axis=1
    ).astype(bf16)
    whole = lax.all_gather(packed, "dp", axis=0, tiled=True)
    whole = lax.all_gather(whole, "mp", axis=0)
    bias = lax.all_gather(jnp.broadcast_to(up_bias[None], (8, cols)), "mp", axis=0)
    vec = jnp.pad(norm_vectors, ((0, 1), (0, 0)))
    hidden = jnp.pad(pos_hidden, ((0, 4), (0, 0)))
    block_out, feats_grad, grads, bias_grad, vec_grad, pos_grad, proj_grad = compute(
        mp_count, width, inner, my_counts, my_feats, my_top, points, whole, bias, vec, hidden, pos_proj
    )
    own = lax.psum_scatter(grads, "mp", scatter_dimension=0, tiled=True)[0]
    own = lax.psum_scatter(own, "dp", scatter_dimension=0, tiled=True)
    bias_grad, vector_grad, pos_grad, proj_grad = lax.psum(
        (bias_grad[:, 0], vec_grad[:7], pos_grad[:4], proj_grad), ("dp", "mp")
    )
    bias_grad = lax.dynamic_index_in_dim(bias_grad, mp_index, 0, keepdims=False)
    qkv_grad = jnp.stack((own[:, 0:128], own[:, 128:256], own[:, 256:384]))
    out_grad = own[:, 384:512].T
    up_grad = own[:, 512 : 512 + cols]
    down_grad = own[:, 512 + cols :].T
    leader = ((dp_index == 0) & (mp_index == 0)).astype(f32)
    first_dp = (dp_index == 0).astype(f32)
    owners = [1.0, 1.0, 1.0, first_dp, 1.0, leader, leader, leader]
    weights = [qkv_weight, out_weight, up_weight, up_bias, down_weight, norm_vectors, pos_hidden, pos_proj]
    moments = [
        qkv_moment,
        out_moment,
        up_moment,
        bias_moment,
        down_moment,
        vector_moment,
        hidden_moment,
        proj_moment,
    ]
    seconds = [
        qkv_second,
        out_second,
        up_second,
        bias_second,
        down_second,
        vector_second,
        hidden_second,
        proj_second,
    ]
    grads = [qkv_grad, out_grad, up_grad, bias_grad, down_grad, vector_grad, pos_grad, proj_grad]
    grad_square = jnp.zeros((), f32)
    weight_square = []
    for i in range(8):
        grad_square = grad_square + owners[i] * jnp.sum(grads[i] * grads[i])
        weight_square.append(owners[i] * piece_squares(weights[i], i))
    totals = lax.psum(jnp.concatenate([grad_square[None]] + weight_square), ("dp", "mp"))
    clip_norm = jnp.sqrt(totals[0])
    factor = jnp.minimum(1.0, clip_max / (clip_norm + 1e-06))
    clipped_list, moment_list, second_list, direction_list, update_square = [], [], [], [], []
    for i in range(8):
        clipped = grads[i] * factor
        moment_new = beta_one * moments[i] + (1.0 - beta_one) * clipped
        second_new = beta_two * seconds[i] + (1.0 - beta_two) * clipped * clipped
        direction = (
            moment_new
            / (1.0 - beta_one**step_count)
            / (jnp.sqrt(second_new / (1.0 - beta_two**step_count)) + adam_eps)
            + decay_rate * weights[i]
        )
        clipped_list.append(clipped)
        moment_list.append(moment_new)
        second_list.append(second_new)
        direction_list.append(direction)
        update_square.append(owners[i] * piece_squares(direction, i))
    update_total = lax.psum(jnp.concatenate(update_square), ("dp", "mp"))
    weight_norm = jnp.sqrt(totals[1:])
    update_norm = jnp.sqrt(update_total)
    trust_ratio = weight_norm / (update_norm + 1e-06)
    outputs = [block_out, feats_grad, clip_norm, jnp.stack((weight_norm, update_norm))]
    for i in range(8):
        new_weight = weights[i] - learn_rate * piece_ratio(trust_ratio, i) * direction_list[i]
        outputs.append(clipped_list[i])
        outputs.append(new_weight)
        outputs.append(moment_list[i])
        outputs.append(second_list[i])
        outputs.append(new_weight.astype(bf16))
    return tuple(outputs)


def solution(mesh):
    qkv, outw, upw, bias, whole = P(None, "dp", "mp"), P("mp", "dp"), P("dp", "mp"), P("mp"), P()
    params = (qkv, outw, upw, bias, outw, whole, whole, whole)
    in_specs = (P("dp", None), P(None, "dp"), P("dp"), P("dp", None)) + params * 3
    rows = P(("dp", "mp"), None)
    out_specs = (rows, rows, P(), P()) + tuple(spec for spec in params for _ in range(5))
    return jax.shard_map(shards, mesh=mesh, in_specs=in_specs, out_specs=out_specs, check_vma=False)
```

time: 903 us -> 531 us (0.59)
  waiting for transfers between devices: 412 us -> 242 us
  blocking collectives: 250 us -> 160 us
  matrix products: 73.6 us -> 0 us
  Pallas kernels: 0 us -> 53.9 us
  local copies, waits for them, and re-layouts: 63.1 us -> 12.9 us
  other arithmetic: 65.6 us -> 31.6 us
    all_gather x4 -> x2, blocking collectives: 129 us -> 41.7 us  [the longest x1 36.5 us: shards(): whole = lax.all_gather(packed, 'dp', axis=0, tiled=True)]
    unnamed x11 -> x4, waiting for transfers between devices: 76.5 us -> 0.73 us
    dot_general x45 -> x0, matrix products: 73.6 us -> none  [the longest x8 8.91 us: block_scores(): jnp.einsum('qsd,ksd->sqk', query, keys, preferred_element_type=jnp.float32)]
    psum x3 -> x1, waiting for transfers between devices: 138 us -> 79.9 us  [shards(): lax.psum((bias_grad[:, 0], vec_grad[:7], pos_grad[:4], proj_grad), ('dp',...]
    pallas_call x0 -> x1, Pallas kernels: none -> 53.9 us  [compute(): pl.pallas_call(functools.partial(compute_kernel, names, mp, clouds, width...]
    reduce_scatter x5 -> x2, waiting for transfers between devices: 183 us -> 137 us  [the longest x1 69.2 us: shards(): own = lax.psum_scatter(own, 'dp', scatter_dimension=0, tiled=True)]
    reduce_sum x24 -> x7, other arithmetic: 34.1 us -> 7 us  [shards(): grad_square = grad_square + owners[i] * jnp.sum(grads[i] * grads[i])]
    another operation x15 -> x0, local copies, waits for them, and re-layouts: 21 us -> none  [the longest x7 18.2 us: shards(): jnp.stack((grad_query, grad_keys, grad_values))]
  transfers between devices with their start and end apart: 10 -> 4, of which waited for: 9 -> 4; matrix products, arithmetic and copies ran while one was open for 11% -> 3% of each run, Pallas kernels for 0% -> 0%
where the time goes in v1:
time: 531 us; the launch traced here: 530 us
  waiting for transfers between devices  242 us (46%)
  blocking collectives  160 us (30%)
  Pallas kernels  53.9 us (10%)
  other arithmetic  31.6 us (6%)
  between operations  29.3 us (6%)
  local copies, waits for them, and re-layouts  12.9 us (2%)
    psum x1, waiting for transfers between devices, shards(): lax.psum((bias_grad[:, 0], vec_grad[:7], pos_grad[:4], proj_grad), ('dp',...  79.9 us
    reduce_scatter x1, waiting for transfers between devices, shards(): own = lax.psum_scatter(own, 'dp', scatter_dimension=0, tiled=True)  69.2 us
    reduce_scatter x1, waiting for transfers between devices, shards(): own = lax.psum_scatter(grads, 'mp', scatter_dimension=0, tiled=True)[0]  68.2 us
    pallas_call x1, Pallas kernels, compute(): pl.pallas_call(functools.partial(compute_kernel, names, mp, clouds, width...  53.9 us
    psum x1, blocking collectives, shards(): lax.psum((bias_grad[:, 0], vec_grad[:7], pos_grad[:4], proj_grad), ('dp',...  39.7 us
    psum x1, blocking collectives, shards(): update_total = lax.psum(jnp.concatenate(update_square), ('dp', 'mp'))  39.6 us
    psum x1, blocking collectives, shards(): lax.psum(jnp.concatenate([grad_square[None]] + weight_square), ('dp', 'mp'))  39.5 us
    all_gather x1, blocking collectives, shards(): whole = lax.all_gather(packed, 'dp', axis=0, tiled=True)  36.5 us
  transfers between devices with their start and end apart: 4, of which 4 were waited for; matrix products, arithmetic and copies ran while one was open for 3% of the time, Pallas kernels for 0%

profile of v1, /device:TPU:0, one launch (start us, length us, event | category | flops | bytes accessed | tf_op | source)
XLA Modules:
  0.0 530.1 jit_solution(3619452868182071710)
XLA Ops:
  7.3 1.6 multiply_reduce_fusion.8
  8.9 0.7 constant_dynamic-update-slice_fusion
  9.7 0.9 convert_dynamic-update-slice_fusion
  10.6 0.9 bitcast_dynamic-update-slice_fusion
  11.5 36.5 %all_gather.12 = bf16[384,1280]{1,0:T(8,128)(2,1)} all-gather(bf16[48,1280]{1,0:T(8,128)(2,1)S(1)} %bitcast_dynamic-update-slice_fusion), channel_id=1, replica_groups=mesh['dp'=8,'mp'=4] {'dp'}, dimensions={0}, use_global_device_ids=true | all-gather | bytes 1105920 | tf_op jit(solution)/shard_map/all_gather | solution.py:508
  48.5 5.2 all-gather.2
  53.7 0.8 pad.18.args_3_
  56.3 2.3 constant_dynamic-slice_fusion.1
  58.6 23.7 %all-gather.5.cloned.1.call-done = bf16[1536,1280]{1,0:T(8,128)(2,1)} async-done(((bf16[384,1280]{1,0:T(8,128)(2,1)}), bf16[1536,1280]{1,0:T(8,128)(2,1)}) %all-gather.5.cloned.1.call-update) | async-done | bytes 3932176 | tf_op jit(solution)/shard_map/all_gather | solution.py:509
  82.9 53.9 %shard_map.611 = (bf16[608,384]{1,0:T(8,128)(2,1)}, f32[608,384]{1,0:T(8,128)}, f32[4,384,1280]{2,1,0:T(8,128)}, f32[4,8,384]{2,1,0:T(8,128)}, f32[8,384]{1,0:T(...) custom-call(s32[16]{0:T(128)} %dynamic_slice.16.args_0_, bf16[608,384]{1,0:T(8,128)(2,1)} %get-tuple-element.129.args_1_, ...), custom_call_target="tpu_custom_call" | custom-call | tf_op jit(solution)/shard_map/pallas_call | solution.py:449
  137.7 68.2 %reduce-scatter.3.cloned.1.call-done = f32[1,384,1280]{2,1,0:T(8,128)} async-done(((f32[4,384,1280]{2,1,0:T(8,128)}), f32[1,384,1280]{2,1,0:T(8,128)}) %reduce-scatter.3.cloned.1.call-update) | async-done | bytes 1966096 | tf_op jit(solution)/shard_map/reduce_scatter | solution.py:516
  211.9 0.8 slice.77
  212.8 39.7 %all-reduce.5 = (f32[4,384]{1,0:T(4,128)S(1)}, f32[7,384]{1,0:T(8,128)S(1)}, f32[4,128]{1,0:T(4,128)S(1)}) all-reduce(f32[4,384]{1,0:T(4,128)S(1)} %bitcast.74, f32[7,384]{1,0:T(8,128)S(1)} %bitcast.75, f32[4,128]{1,0:T(4,128)S(1)} %slice.80), channel_id=1, replica_groups=mesh['dp'=8,'mp'=4] {'dp','mp'}, use_global_device_ids=true, to_apply=%region_5.6 | all-reduce | flops 4736 | bytes 37888 | tf_op jit(solution)/shard_map/psum | solution.py:518
  256.2 79.9 %all-reduce.8.cloned.1.call-done = f32[128,384]{1,0:T(8,128)} async-done(((f32[128,384]{1,0:T(8,128)}), f32[128,384]{1,0:T(8,128)}) %all-reduce.8.cloned.1.call-update) | async-done | bytes 196624 | tf_op jit(solution)/shard_map/psum | solution.py:518
  336.1 1.6 multiply_reduce_fusion.2
  338.4 69.2 %reduce-scatter.5.cloned.1.call-done = f32[48,1280]{1,0:T(8,128)} async-done(((f32[384,1280]{1,0:T(8,128)}), f32[48,1280]{1,0:T(8,128)}) %reduce-scatter.5.cloned.1.call-update) | async-done | bytes 245776 | tf_op jit(solution)/shard_map/reduce_scatter | solution.py:517
  407.6 1.4 multiply_reduce_fusion.14
  411.0 1.5 multiply_reduce_fusion.9
  413.8 2.7 concatenate.15
  416.5 39.5 %psum.46 = f32[15]{0:T(128)S(1)} all-reduce(f32[15]{0:T(128)S(1)} %concatenate.15), channel_id=1, replica_groups=mesh['dp'=8,'mp'=4] {'dp','mp'}, use_global_device_ids=true, to_apply=%region_22.23 | all-reduce | flops 15 | bytes 120 | tf_op jit(solution)/shard_map/psum | solution.py:556
  456.2 2.3 multiply_reduce_fusion
  459.2 1.2 multiply_reduce_fusion.18
  461.1 0.7 multiply_reduce_fusion.15
  461.8 1.2 multiply_reduce_fusion.19
  463.7 1.3 multiply_reduce_fusion.5
  465.0 1.3 multiply_reduce_fusion.3
  466.3 1.3 multiply_reduce_fusion.4
  467.6 1.2 multiply_reduce_fusion.12
  468.9 2.7 concatenate.16
  471.5 39.6 %psum.47 = f32[14]{0:T(128)S(1)} all-reduce(f32[14]{0:T(128)S(1)} %concatenate.16), channel_id=1, replica_groups=mesh['dp'=8,'mp'=4] {'dp','mp'}, use_global_device_ids=true, to_apply=%region_31.32 | all-reduce | flops 14 | bytes 112 | tf_op jit(solution)/shard_map/psum | solution.py:575
  518.2 0.8 fusion.10
  521.7 0.7 fusion.17
  (131 shorter events, 15.4 us)
Async XLA Ops:
  7.3 75.0 %all-gather.5.cloned.1.call-start = ((), (), s32[]{:S(2)}) async-start(), calls=%async_computation.5 | async-start | bytes 4915200 | tf_op jit(solution)/shard_map/all_gather | solution.py:509
  48.0 157.9 %reduce-scatter.3.cloned.1.call-start = ((), (), s32[]{:S(2)}) async-start(), calls=%async_computation.2 | async-start | bytes 9830400 | tf_op jit(solution)/shard_map/reduce_scatter | solution.py:516
  136.9 70.5 %copy-start.1 = (f32[128,384]{1,0:T(8,128)S(1)}, f32[128,384]{1,0:T(8,128)}, u32[]{:S(2)}) copy-start(f32[128,384]{1,0:T(8,128)} %args_8_.4) | copy-start | bytes 589828
  136.9 73.2 %copy-start.8 = (f32[128,48]{0,1:T(8,128)S(1)}, f32[128,48]{0,1:T(8,128)}, u32[]{:S(2)}) copy-start(f32[128,48]{0,1:T(8,128)} %param.33) | copy-start | bytes 73732
  136.9 73.8 %copy-start.3 = (f32[48,384]{1,0:T(8,128)S(1)}, f32[48,384]{1,0:T(8,128)}, u32[]{:S(2)}) copy-start(f32[48,384]{1,0:T(8,128)} %param.34) | copy-start | bytes 221188
  136.9 74.4 %copy-start.2 = (f32[384,48]{0,1:T(8,128)S(1)}, f32[384,48]{0,1:T(8,128)}, u32[]{:S(2)}) copy-start(f32[384,48]{0,1:T(8,128)} %param.36) | copy-start | bytes 221188
  136.9 75.8 %copy-start.40 = (f32[8,128]{1,0:T(8,128)S(1)}, f32[8,128]{1,0:T(8,128)}, u32[]{:S(2)}) copy-start(f32[8,128]{1,0:T(8,128)} %get-tuple-element.56) | copy-start | bytes 12292
  136.9 75.8 %copy-start.32 = (f32[8,384]{1,0:T(8,128)S(1)}, f32[8,384]{1,0:T(8,128)}, u32[]{:S(2)}) copy-start(f32[8,384]{1,0:T(8,128)} %get-tuple-element.55) | copy-start | bytes 36868
  136.9 319.2 %copy-start.15 = (f32[128,384]{1,0:T(8,128)S(1)}, f32[128,384]{1,0:T(8,128)}, u32[]{:S(2)}) copy-start(f32[128,384]{1,0:T(8,128)} %param.47) | copy-start | bytes 589828
  136.9 319.2 %copy-start.16 = (f32[128,384]{1,0:T(8,128)S(1)}, f32[128,384]{1,0:T(8,128)}, u32[]{:S(2)}) copy-start(f32[128,384]{1,0:T(8,128)} %param.55) | copy-start | bytes 589828
  137.0 199.2 %all-reduce.8.cloned.1.call-start = ((), (), s32[]{:S(2)}) async-start(), calls=%async_computation.4 | async-start | bytes 393216 | tf_op jit(solution)/shard_map/psum | solution.py:518
  137.7 269.9 %reduce-scatter.5.cloned.1.call-start = ((), (), s32[]{:S(2)}) async-start(), calls=%async_computation.3 | async-start | bytes 2211840 | tf_op jit(solution)/shard_map/reduce_scatter | solution.py:517
  206.0 253.2 %copy-start.36 = (f32[4,128]{1,0:T(4,128)S(1)}, f32[4,128]{1,0:T(4,128)}, u32[]{:S(2)}) copy-start(f32[4,128]{1,0:T(4,128)} %param.46) | copy-start | bytes 6148
  206.0 253.2 %copy-start.37 = (f32[4,128]{1,0:T(4,128)S(1)}, f32[4,128]{1,0:T(4,128)}, u32[]{:S(2)}) copy-start(f32[4,128]{1,0:T(4,128)} %param.54) | copy-start | bytes 6148
  206.0 255.1 %copy-start.33 = (f32[7,384]{1,0:T(8,128)S(1)}, f32[7,384]{1,0:T(8,128)}, u32[]{:S(2)}) copy-start(f32[7,384]{1,0:T(8,128)} %param.45) | copy-start | bytes 32260
  206.0 255.1 %copy-start.34 = (f32[7,384]{1,0:T(8,128)S(1)}, f32[7,384]{1,0:T(8,128)}, u32[]{:S(2)}) copy-start(f32[7,384]{1,0:T(8,128)} %param.53) | copy-start | bytes 32260
  206.0 255.8 %copy-start.38 = (f32[384]{0:T(512)S(1)}, f32[384]{0:T(512)}, u32[]{:S(2)}) copy-start(f32[384]{0:T(512)} %param.43) | copy-start | bytes 4612
  206.0 255.8 %copy-start.39 = (f32[384]{0:T(512)S(1)}, f32[384]{0:T(512)}, u32[]{:S(2)}) copy-start(f32[384]{0:T(512)} %param.51) | copy-start | bytes 4612
  206.0 257.7 %copy-start.7 = (f32[3,48,128]{2,1,0:T(8,128)S(1)}, f32[3,48,128]{2,1,0:T(8,128)}, u32[]{:S(2)}) copy-start(f32[3,48,128]{2,1,0:T(8,128)} %param.32) | copy-start | bytes 221188
  206.0 257.7 %copy-start.20 = (f32[3,48,128]{2,1,0:T(8,128)S(1)}, f32[3,48,128]{2,1,0:T(8,128)}, u32[]{:S(2)}) copy-start(f32[3,48,128]{2,1,0:T(8,128)} %param.40) | copy-start | bytes 221188
  206.0 257.7 %copy-start.21 = (f32[3,48,128]{2,1,0:T(8,128)S(1)}, f32[3,48,128]{2,1,0:T(8,128)}, u32[]{:S(2)}) copy-start(f32[3,48,128]{2,1,0:T(8,128)} %param.48) | copy-start | bytes 221188
  206.1 258.9 %copy-start.22 = (f32[384,48]{0,1:T(8,128)S(1)}, f32[384,48]{0,1:T(8,128)}, u32[]{:S(2)}) copy-start(f32[384,48]{0,1:T(8,128)} %param.44) | copy-start | bytes 221188
  206.1 258.9 %copy-start.23 = (f32[384,48]{0,1:T(8,128)S(1)}, f32[384,48]{0,1:T(8,128)}, u32[]{:S(2)}) copy-start(f32[384,48]{0,1:T(8,128)} %param.52) | copy-start | bytes 221188
  206.1 260.2 %copy-start.24 = (f32[48,384]{1,0:T(8,128)S(1)}, f32[48,384]{1,0:T(8,128)}, u32[]{:S(2)}) copy-start(f32[48,384]{1,0:T(8,128)} %param.42) | copy-start | bytes 221188
  206.1 260.2 %copy-start.25 = (f32[48,384]{1,0:T(8,128)S(1)}, f32[48,384]{1,0:T(8,128)}, u32[]{:S(2)}) copy-start(f32[48,384]{1,0:T(8,128)} %param.50) | copy-start | bytes 221188
  253.7 213.9 %copy-start.30 = (f32[128,48]{0,1:T(8,128)S(1)}, f32[128,48]{0,1:T(8,128)}, u32[]{:S(2)}) copy-start(f32[128,48]{0,1:T(8,128)} %param.41) | copy-start | bytes 73732
  253.7 213.9 %copy-start.31 = (f32[128,48]{0,1:T(8,128)S(1)}, f32[128,48]{0,1:T(8,128)}, u32[]{:S(2)}) copy-start(f32[128,48]{0,1:T(8,128)} %param.49) | copy-start | bytes 73732
  456.2 62.8 %copy-start.35 = (f32[384]{0:T(512)}, f32[384]{0:T(512)S(1)}, u32[]{:S(2)}) copy-start(f32[384]{0:T(512)S(1)} %multiply_reduce_fusion.23) | copy-start | bytes 4612
  458.5 63.8 %copy-start.4 = (f32[128,384]{1,0:T(8,128)}, f32[128,384]{1,0:T(8,128)S(1)}, u32[]{:S(2)}) copy-start(f32[128,384]{1,0:T(8,128)S(1)} %get-tuple-element.80) | copy-start | bytes 589828
  458.5 63.8 %copy-start.5 = (f32[128,384]{1,0:T(8,128)}, f32[128,384]{1,0:T(8,128)S(1)}, u32[]{:S(2)}) copy-start(f32[128,384]{1,0:T(8,128)S(1)} %get-tuple-element.81) | copy-start | bytes 589828
  461.8 60.6 %copy-start.26 = (f32[7,384]{1,0:T(8,128)}, f32[7,384]{1,0:T(8,128)S(1)}, u32[]{:S(2)}) copy-start(f32[7,384]{1,0:T(8,128)S(1)} %get-tuple-element.89) | copy-start | bytes 32260
  461.8 60.6 %copy-start.27 = (f32[7,384]{1,0:T(8,128)}, f32[7,384]{1,0:T(8,128)S(1)}, u32[]{:S(2)}) copy-start(f32[7,384]{1,0:T(8,128)S(1)} %get-tuple-element.90) | copy-start | bytes 32260
  (14 other events, 714.4 us)
Sparse Core Ops, SparseCore 0:
  48.2 34.0 all-gather.4
  137.0 68.9 reduce-scatter.2
  213.0 123.0 all-reduce.7
  339.9 67.7 reduce-scatter.4

commit v2 on v1

--- a/solution.py
+++ b/solution.py
@@ -375,6 +375,7 @@
         pos_low=((rows, width), bf16),
         pre_grad=((rows, hid), f32),
         turned=((width, rows), bf16),
+        turned_mid=((width, rows), bf16),
     )
     return shapes
 
@@ -587,10 +588,732 @@
     return tuple(outputs)
 
 
+class Links:
+    def __init__(self, send, recv):
+        dp, mp = lax.axis_index("dp"), lax.axis_index("mp")
+        self.z, self.y = dp // 2, lax.rem(dp, 2)
+        self.x, self.c = mp // 2, lax.rem(mp, 2)
+        self.mp = mp
+        self.plane = self.y * 4 + mp
+        self.send_sem, self.recv_sem = send, recv
+        self.count = 0
+        self.sent = []
+
+    def at(self, z, y, x, c):
+        return (z * 2 + y, x * 2 + c)
+
+    def core(self):
+        return self.at(self.z, self.y, self.x, 1 - self.c)
+
+    def side(self):
+        return self.at(self.z, self.y, 1 - self.x, self.c)
+
+    def deep(self):
+        return self.at(self.z, 1 - self.y, self.x, self.c)
+
+    def far(self, k):
+        return self.at(lax.rem(self.z + k, 4), self.y, self.x, self.c)
+
+    def back(self, k):
+        return lax.rem(self.z + 4 - k, 4)
+
+    def round(self, k):
+        other = lax.rem(self.plane + k, 8)
+        return (self.z * 2 + other // 4, lax.rem(other, 4))
+
+    def peers(self):
+        return [self.far(k) for k in range(1, 4)] + [self.round(k) for k in range(1, 8)]
+
+    def greet(self):
+        barrier = pltpu.get_barrier_semaphore()
+        for who in self.peers():
+            pl.semaphore_signal(barrier, inc=1, device_id=who, device_id_type=pl.DeviceIdType.MESH)
+
+    def met(self):
+        pl.semaphore_wait(pltpu.get_barrier_semaphore(), 10)
+
+    def copy(self, source, target, who, i):
+        return pltpu.make_async_remote_copy(
+            src_ref=source,
+            dst_ref=target,
+            send_sem=self.send_sem.at[i],
+            recv_sem=self.recv_sem.at[i],
+            device_id=who,
+            device_id_type=pl.DeviceIdType.MESH,
+        )
+
+    def send(self, source, target, who):
+        i = self.count
+        self.count += 1
+        copy = self.copy(source, target, who, i)
+        copy.start()
+        self.sent.append(copy)
+        return i
+
+    def wait(self, i, target):
+        self.copy(target, target, self.core(), i).wait_recv()
+
+    def finish(self):
+        for copy in self.sent:
+            copy.wait_send()
+
+
+class Gather:
+    def __init__(self, links, w, lo, hi, flip):
+        self.links, self.w, self.lo, self.hi, self.flip = links, w, lo, hi, flip
+
+    def part(self, mp, z, y):
+        return self.w.at[mp, z, y, :, self.lo : self.hi]
+
+    def spread(self, block):
+        k = self.links
+        return (k.send(block, block, k.deep()), k.send(block, block, k.side()), k.send(block, block, k.core()))
+
+    def start(self):
+        k = self.links
+        own = self.part(k.mp, k.z, k.y)
+        self.along = [k.send(own, own, k.far(i)) for i in (3, 2, 1)][::-1]
+        self.spreads = [self.spread(own)]
+
+    def second(self):
+        k = self.links
+        for i in (1, 2, 3):
+            block = self.part(k.mp, k.back(i), k.y)
+            k.wait(self.along[i - 1], block)
+            self.spreads.append(self.spread(block))
+
+    def third(self):
+        k = self.links
+        other = k.mp + 2 - 4 * k.x
+        for i in range(4):
+            z = k.back(i)
+            if self.flip:
+                k.wait(self.spreads[i][1], self.part(other, z, k.y))
+            else:
+                k.wait(self.spreads[i][0], self.part(k.mp, z, 1 - k.y))
+        if self.flip:
+            block = self.part(other, slice(None), k.y)
+            self.wide = k.send(block, block, k.deep())
+            self.core_first = k.send(block, block, k.core())
+        else:
+            block = self.part(k.mp, slice(None), 1 - k.y)
+            self.wide = k.send(block, block, k.side())
+            self.core_first = k.send(block, block, k.core())
+
+    def fourth(self):
+        k = self.links
+        other = k.mp + 2 - 4 * k.x
+        for i in range(4):
+            z = k.back(i)
+            if self.flip:
+                k.wait(self.spreads[i][0], self.part(k.mp, z, 1 - k.y))
+            else:
+                k.wait(self.spreads[i][1], self.part(other, z, k.y))
+        if self.flip:
+            near = self.part(k.mp, slice(None), 1 - k.y)
+            self.core_second = k.send(near, near, k.core())
+            self.far_wait = self.part(other, slice(None), 1 - k.y)
+            k.wait(self.wide, self.far_wait)
+            self.core_third = k.send(self.far_wait, self.far_wait, k.core())
+        else:
+            near = self.part(other, slice(None), k.y)
+            self.core_second = k.send(near, near, k.core())
+            self.far_wait = self.part(other, slice(None), 1 - k.y)
+            k.wait(self.wide, self.far_wait)
+            self.core_third = k.send(self.far_wait, self.far_wait, k.core())
+
+    def end(self):
+        k = self.links
+        twin = k.mp + 1 - 2 * k.c
+        other = twin + 2 - 4 * k.x
+        for i in range(4):
+            k.wait(self.spreads[i][2], self.part(twin, k.back(i), k.y))
+        if self.flip:
+            k.wait(self.core_first, self.part(other, slice(None), k.y))
+            k.wait(self.core_second, self.part(twin, slice(None), 1 - k.y))
+        else:
+            k.wait(self.core_first, self.part(twin, slice(None), 1 - k.y))
+            k.wait(self.core_second, self.part(other, slice(None), k.y))
+        k.wait(self.core_third, self.part(other, slice(None), 1 - k.y))
+
+
+class Scatter:
+    def __init__(self, links, refs, flip):
+        self.links, self.flip = links, flip
+        self.__dict__.update(refs)
+
+    def start(self):
+        k = self.links
+        self.first = k.send(self.core_out, self.core_in, k.core())
+
+    def pair(self, x, z, y):
+        return self.kept[x, z, y] + self.core_in[x, z, y].astype(f32)
+
+    def second(self):
+        k = self.links
+        k.wait(self.first, self.core_in)
+        if self.flip:
+            for x in range(2):
+                for z in range(4):
+                    self.next_out[x, z] = self.pair(x, z, 1 - k.y).astype(bf16)
+            self.next = k.send(self.next_out, self.next_in, k.deep())
+        else:
+            for y in range(2):
+                for z in range(4):
+                    self.next_out[y, z] = self.pair(1 - k.x, z, y).astype(bf16)
+            self.next = k.send(self.next_out, self.next_in, k.side())
+
+    def third(self):
+        k = self.links
+        k.wait(self.next, self.next_in)
+        for z in range(4):
+            if self.flip:
+                total = self.pair(1 - k.x, z, k.y) + self.next_in[1 - k.x, z].astype(f32)
+            else:
+                total = self.pair(k.x, z, 1 - k.y) + self.next_in[1 - k.y, z].astype(f32)
+            self.last_out[z] = total.astype(bf16)
+        self.last = k.send(self.last_out, self.last_in, k.side() if self.flip else k.deep())
+
+    def fourth(self):
+        k = self.links
+        k.wait(self.last, self.last_in)
+        self.along = []
+        for i in range(4):
+            z = lax.rem(k.z + i, 4)
+            mid = self.next_in[k.x, z] if self.flip else self.next_in[k.y, z]
+            total = self.pair(k.x, z, k.y) + mid.astype(f32) + self.last_in[z].astype(f32)
+            if i == 0:
+                self.own[...] = total
+            else:
+                self.far_out[i - 1] = total.astype(bf16)
+                self.along.append(k.send(self.far_out.at[i - 1], self.far_in.at[i - 1], k.far(i)))
+
+    def end(self):
+        k = self.links
+        total = self.own[...]
+        for i in range(3):
+            k.wait(self.along[i], self.far_in.at[i])
+            total = total + self.far_in[i].astype(f32)
+        return total
+
+
+def scatter_scratch(tag, cols):
+    return {
+        tag + "kept": ((2, 4, 2, 48, cols), f32),
+        tag + "core_out": ((2, 4, 2, 48, cols), bf16),
+        tag + "core_in": ((2, 4, 2, 48, cols), bf16),
+        tag + "next_out": ((2, 4, 48, cols), bf16),
+        tag + "next_in": ((2, 4, 48, cols), bf16),
+        tag + "last_out": ((4, 48, cols), bf16),
+        tag + "last_in": ((4, 48, cols), bf16),
+        tag + "far_out": ((3, 48, cols), bf16),
+        tag + "far_in": ((3, 48, cols), bf16),
+        tag + "own": ((48, cols), f32),
+    }
+
+
+def stack_rows(rows, height=8):
+    place = lax.broadcasted_iota(jnp.int32, (height, 128), 0)
+    out = jnp.zeros((height, 128), f32)
+    for i, row in enumerate(rows):
+        out = jnp.where(place == i, jnp.broadcast_to(row, (height, 128)), out)
+    return out
+
+
+def square_row(array):
+    total = jnp.sum(jnp.sum(array * array, axis=0, keepdims=True), axis=1, keepdims=True)
+    return jnp.broadcast_to(total, (1, 128))
+
+
+def adam(grad, factor, moment, second, weight):
+    clipped = grad * factor
+    moment_new = beta_one * moment + (1.0 - beta_one) * clipped
+    second_new = beta_two * second + (1.0 - beta_two) * clipped * clipped
+    direction = (
+        moment_new
+        / (1.0 - beta_one**step_count)
+        / (jnp.sqrt(second_new / (1.0 - beta_two**step_count)) + adam_eps)
+        + decay_rate * weight
+    )
+    return clipped, moment_new, second_new, direction
+
+
+PIECES = ("qkv", "out", "up", "bias", "down", "vector", "hidden", "proj")
+
+
+def own_parts(own, small, mp):
+    cols = (own.shape[1] - 512) // 2
+
+    def wide(row, count):
+        return jnp.concatenate([small[row + 8 * i : row + 8 * i + count, :] for i in range(3)], axis=1)
+
+    place = lax.broadcasted_iota(jnp.int32, (8, cols), 0)
+
+    return {
+        "qkv": [own[:, 128 * i : 128 * i + 128] for i in range(3)],
+        "out": [own[:, 384:512]],
+        "up": [own[:, 512 : 512 + cols]],
+        "bias": [jnp.sum(jnp.where(place == mp, wide(416, 8), 0.0), axis=0, keepdims=True)],
+        "down": [own[:, 512 + cols : 512 + 2 * cols]],
+        "vector": [wide(384, 7)],
+        "hidden": [small[408:412, :]],
+        "proj": [jnp.concatenate([small[128 * i : 128 * i + 128, :] for i in range(3)], axis=1)],
+    }
+
+
+def load(refs, kind, name):
+    ref = refs[name + "_" + kind]
+    if name == "qkv":
+        return [ref[i] for i in range(3)]
+    return [ref[...]]
+
+
+def main_kernel(names, mp, clouds, width, inner, *args):
+    refs = dict(zip(names, args))
+    layer = Layer(refs, mp, clouds, width, inner)
+    cols = inner // mp
+    links = Links(layer.send_sem, layer.recv_sem)
+    w = layer.w
+    links.greet()
+    share = clouds * PAD
+    rows = pl.ds(pl.multiple_of(links.mp * share, 16), share)
+    local = [
+        pltpu.make_async_copy(layer.feats_all.at[rows, :], layer.feats, layer.load_sem.at[0]),
+        pltpu.make_async_copy(layer.top_all.at[rows, :], layer.cotangent, layer.load_sem.at[1]),
+    ]
+    late = []
+    for i, name in enumerate(name for name in PIECES for kind in ("moment", "second")):
+        kind = ("moment", "second")[i % 2]
+        source, target = refs[name + "_" + kind + "_all"], refs[name + "_" + kind]
+        late.append(pltpu.make_async_copy(source, target, layer.load_sem.at[2 + i]))
+    for copy in local + late:
+        copy.start()
+
+    def flat(j, lo, hi):
+        return w[j, :, :, :, lo:hi].reshape(width, hi - lo)
+
+    layer.w_qkv = lambda j: flat(j, 0, 384)
+    layer.w_out = lambda j: flat(j, 384, 512)
+    layer.w_up = lambda j: flat(j, 512, 512 + cols)
+    layer.w_down = lambda j: flat(j, 512 + cols, 512 + 2 * cols)
+    for i in range(3):
+        w[links.mp, links.z, links.y, :, 128 * i : 128 * i + 128] = refs["qkv_weight"][i].astype(bf16)
+    w[links.mp, links.z, links.y, :, 384:512] = refs["out_weight"][...].astype(bf16)
+    w[links.mp, links.z, links.y, :, 512 : 512 + cols] = refs["up_weight"][...].astype(bf16)
+    w[links.mp, links.z, links.y, :, 512 + cols : 512 + 2 * cols] = refs["down_weight"][...].astype(bf16)
+    layer.up_bias[links.mp] = jnp.broadcast_to(refs["bias_weight"][...], (8, cols))
+    links.met()
+    gathers = [
+        Gather(links, w, 0, 256, False),
+        Gather(links, w, 256, 512, True),
+        Gather(links, w, 512, 512 + cols, False),
+        Gather(links, w, 512 + cols, 512 + 2 * cols, True),
+    ]
+    for g in gathers[:2]:
+        g.start()
+    own_bias = layer.up_bias.at[links.mp]
+    bias_side = links.send(own_bias, own_bias, links.side())
+    bias_core = links.send(own_bias, own_bias, links.core())
+    for g in gathers[2:]:
+        g.start()
+    layer.proj_low[...] = refs["proj_weight"][...].astype(bf16)
+    layer.vec = refs["vector_weight"]
+    layer.pos_hidden[...] = jnp.zeros((8, 128), f32)
+    layer.pos_hidden[0:4, :] = refs["hidden_weight"][...]
+    for copy in local:
+        copy.wait()
+    layer.counts = _Shifted(layer.counts_all, links.mp * clouds)
+    layer.spread_rows()
+    for g in gathers[:2]:
+        g.second()
+    layer.masks()
+    for g in gathers[:2]:
+        g.third()
+    layer.entry()
+    for g in gathers[2:]:
+        g.second()
+    for g in gathers[:2]:
+        g.fourth()
+    other_bias = layer.up_bias.at[links.mp + 2 - 4 * links.x]
+    links.wait(bias_side, other_bias)
+    bias_last = links.send(other_bias, other_bias, links.core())
+    for g in gathers[:2]:
+        g.end()
+    layer.project(0)
+    for g in gathers[2:]:
+        g.third()
+    layer.attend(0, heads_before(mp, 0))
+    for j in range(1, mp):
+        layer.project(j)
+        layer.attend(j, heads_before(mp, j))
+        if j == 1:
+            for g in gathers[2:]:
+                g.fourth()
+    layer.middle()
+    for g in gathers[2:]:
+        g.end()
+    twin = links.mp + 1 - 2 * links.c
+    links.wait(bias_core, layer.up_bias.at[twin])
+    links.wait(bias_last, layer.up_bias.at[twin + 2 - 4 * links.x])
+    for j in range(mp):
+        layer.feed(j)
+    layer.top()
+    layer.gather_rows(layer.stream, layer.stage)
+    layer.block_out[...] = layer.stage[...].astype(bf16)
+
+    def scatter(tag, flip):
+        return Scatter(links, {n[len(tag) :]: refs[n] for n in names if n.startswith(tag)}, flip)
+
+    down, up = scatter("down__", True), scatter("up__", False)
+    qk, vo = scatter("qk__", False), scatter("vo__", True)
+
+    def weigh(target, product):
+        for x in range(2):
+            block = product(x * 2 + 1 - links.c).astype(bf16)
+            target.core_out[x] = block.reshape(4, 2, 48, block.shape[-1])
+        for x in range(2):
+            block = product(x * 2 + links.c)
+            target.kept[x] = block.reshape(4, 2, 48, block.shape[-1])
+
+    def values_out(j):
+        values = dot(layer.turned[...], layer.grad_proj[j, :, 256:384])
+        return jnp.concatenate([values, dot(layer.turned_mid[...], layer.attn_low[j])], axis=1)
+
+    layer.turn(layer.grad_top, layer.turned)
+    weigh(down, lambda j: dot(layer.turned[...], layer.activated[j]))
+    down.start()
+    layer.feed_back(0)
+    down.second()
+    for j in range(1, mp):
+        layer.feed_back(j)
+    layer.turn(layer.normed_two, layer.turned)
+    weigh(up, lambda j: dot(layer.turned[...], layer.grad_pre[j]))
+    up.start()
+    down.third()
+    layer.middle_back()
+    up.second()
+    layer.turn(layer.middle_low, layer.turned_mid)
+    for j in range(mp):
+        layer.attend_grad(j)
+    layer.attend_back(0, heads_before(mp, 0))
+    down.fourth()
+    up.third()
+    layer.attend_back(1, heads_before(mp, 1))
+    up.fourth()
+    for j in range(2, mp):
+        layer.attend_back(j, heads_before(mp, j))
+    layer.turn(layer.normed_one, layer.turned)
+    weigh(vo, values_out)
+    vo.start()
+    weigh(qk, lambda j: dot(layer.turned[...], layer.grad_proj[j, :, 0:256]))
+    qk.start()
+    vo.second()
+    layer.entry_back()
+    qk.second()
+    vo.third()
+    layer.proj_grad[...] = dot(layer.hidden[...], layer.pos_low[...], TN)
+    layer.pos_grad[...] = dot(layer.points[...], layer.pre_grad[...], TN, highest)
+    small = layer.small
+    for i in range(3):
+        lanes = slice(128 * i, 128 * i + 128)
+        small[128 * i : 128 * i + 128, :] = layer.proj_grad[:, lanes]
+        small[384 + 8 * i : 392 + 8 * i, :] = layer.vec_grad[:, lanes]
+        small[416 + 8 * i : 424 + 8 * i, :] = stack_rows([layer.up_bias_grad[j, 0:1, lanes] for j in range(mp)])
+    small[408:416, :] = layer.pos_grad[...]
+    small[440:512, :] = jnp.zeros((72, 128), f32)
+    layer.plane_out[...] = small[...].astype(bf16).reshape(8, 64, 128)
+    layer.plane_in[links.plane] = layer.plane_out[links.plane]
+    sums = []
+    for k in range(1, 8):
+        who = links.round(k)
+        block = layer.plane_out.at[lax.rem(links.plane + k, 8)]
+        sums.append(links.send(block, layer.plane_in.at[links.plane], who))
+    qk.third()
+    vo.fourth()
+    layer.gather_rows(layer.middle_grad, layer.feats_grad)
+    for k in range(1, 8):
+        links.wait(sums[k - 1], layer.plane_in.at[lax.rem(links.plane + 8 - k, 8)])
+    total = layer.plane_in[0].astype(f32)
+    for i in range(1, 8):
+        total = total + layer.plane_in[i].astype(f32)
+    layer.line_out[...] = total.astype(bf16).reshape(4, 16, 128)
+    layer.line_in[links.z] = layer.line_out[links.z]
+    sums = []
+    for k in range(1, 4):
+        block = layer.line_out.at[lax.rem(links.z + k, 4)]
+        sums.append(links.send(block, layer.line_in.at[links.z], links.far(k)))
+    qk.fourth()
+    own = layer.own_grad
+    own[:, 512 + cols :] = down.end()
+    own[:, 512 : 512 + cols] = up.end()
+    own[:, 256:512] = vo.end()
+    for k in range(1, 4):
+        links.wait(sums[k - 1], layer.line_in.at[links.back(k)])
+    total = layer.line_in[0].astype(f32)
+    for i in range(1, 4):
+        total = total + layer.line_in[i].astype(f32)
+    layer.whole[links.plane, links.z] = total.astype(bf16)
+    sums = []
+    for k in range(1, 4):
+        block = layer.whole.at[links.plane, links.z]
+        sums.append(links.send(block, block, links.far(k)))
+    own[:, 0:256] = qk.end()
+    lead = (links.z * 2 + links.y == 0).astype(f32)
+    weights = {name: load(refs, "weight", name) for name in PIECES}
+
+    def all_sum(slots, planes, rows):
+        slots[links.z] = rows
+        marks = []
+        for k in range(1, 4):
+            block = slots.at[links.z]
+            marks.append(links.send(block, block, links.far(k)))
+        for k in range(1, 4):
+            links.wait(marks[k - 1], slots.at[links.back(k)])
+        planes[links.plane] = slots[0] + slots[1] + slots[2] + slots[3]
+        marks = []
+        for k in range(1, 8):
+            block = planes.at[links.plane]
+            marks.append(links.send(block, block, links.round(k)))
+        return marks
+
+    def all_end(planes, marks):
+        for k in range(1, 8):
+            links.wait(marks[k - 1], planes.at[lax.rem(links.plane + 8 - k, 8)])
+        total = planes[0]
+        for i in range(1, 8):
+            total = total + planes[i]
+        return total
+
+    def five(parts):
+        out = []
+        for name in ("qkv", "out", "up", "bias", "down"):
+            row = sum(square_row(p) for p in parts[name])
+            out.append(row * lead if name == "bias" else row)
+        return out
+
+    rows = stack_rows([square_row(own[...])] + five(weights))
+    marks = all_sum(layer.line_a, layer.plane_a, rows)
+    for k in range(1, 4):
+        links.wait(sums[k - 1], layer.whole.at[links.plane, links.back(k)])
+    sums = []
+    for k in range(1, 8):
+        block = layer.whole.at[links.plane]
+        sums.append(links.send(block, block, links.round(k)))
+    for k in range(1, 8):
+        links.wait(sums[k - 1], layer.whole.at[lax.rem(links.plane + 8 - k, 8)])
+    small[...] = layer.whole[...].astype(f32).reshape(512, 128)
+    first = all_end(layer.plane_a, marks)
+    layer.small_out[...] = small[...]
+    total = first[0:1] + square_row(small[0:440, :])
+    factor = jnp.minimum(1.0, clip_max / (jnp.sqrt(total) + 1e-06))[0:1, 0:1]
+    for copy in late:
+        copy.wait()
+    grads = own_parts(own, small, links.mp)
+    ways = {}
+    for name in ("qkv", "out", "up", "bias", "down"):
+        ways[name] = [
+            adam(g, factor, m, s, p)[3]
+            for g, m, s, p in zip(grads[name], load(refs, "moment", name), load(refs, "second", name), weights[name])
+        ]
+    marks = all_sum(layer.line_b, layer.plane_b, stack_rows(five(ways)))
+    second = all_end(layer.plane_b, marks)
+    place = lax.broadcasted_iota(jnp.int32, (8, 128), 0)
+    layer.sums[0:8, :] = jnp.where(place == 0, jnp.broadcast_to(total, (8, 128)), first)
+    layer.sums[8:16, :] = second
+    links.finish()
+
+
+class _Shifted:
+    def __init__(self, ref, start):
+        self.ref, self.start = ref, start
+
+    def __getitem__(self, i):
+        return self.ref[self.start + i]
+
+
+SHAPES = ("weight", "moment", "second")
+
+
+def main_call(mp, inner, counts, feats, cotangent, points, params):
+    clouds = counts.shape[0] // mp
+    width = feats.shape[1]
+    hid = params["proj_weight"].shape[0]
+    cols = inner // mp
+    smem, vmem = pl.BlockSpec(memory_space=pltpu.SMEM), pl.BlockSpec(memory_space=pltpu.VMEM)
+    anywhere = pl.BlockSpec(memory_space=pl.ANY)
+    inputs = {"counts_all": (counts, smem), "feats_all": (feats, anywhere), "top_all": (cotangent, anywhere)}
+    inputs["points"] = (points, vmem)
+    scratch = layer_scratch(mp, clouds, width, inner, hid)
+    for name in PIECES:
+        inputs[name + "_weight"] = (params[name + "_weight"], vmem)
+        for kind in SHAPES[1:]:
+            array = params[name + "_" + kind]
+            inputs[name + "_" + kind + "_all"] = (array, anywhere)
+            scratch[name + "_" + kind] = (array.shape, f32)
+    outs = dict(
+        block_out=((clouds * PAD, width), bf16),
+        feats_grad=((clouds * PAD, width), f32),
+        own_grad=((48, 512 + 2 * cols), f32),
+        small_out=((512, 128), f32),
+        sums=((16, 128), f32),
+    )
+    scratch.update(
+        feats=((clouds * PAD, width), bf16),
+        cotangent=((clouds * PAD, width), bf16),
+        proj_low=((hid, width), bf16),
+        pos_hidden=((8, hid), f32),
+        w=((mp, 4, 2, 48, 512 + 2 * cols), bf16),
+        up_bias=((mp, 8, cols), f32),
+        up_bias_grad=((mp, 8, cols), f32),
+        vec_grad=((8, width), f32),
+        pos_grad=((8, hid), f32),
+        proj_grad=((hid, width), f32),
+        small=((512, 128), f32),
+        plane_out=((8, 64, 128), bf16),
+        plane_in=((8, 64, 128), bf16),
+        line_out=((4, 16, 128), bf16),
+        line_in=((4, 16, 128), bf16),
+        whole=((8, 4, 16, 128), bf16),
+        line_a=((4, 8, 128), f32),
+        plane_a=((8, 8, 128), f32),
+        line_b=((4, 8, 128), f32),
+        plane_b=((8, 8, 128), f32),
+    )
+    for tag, n in (("down__", cols), ("up__", cols), ("qk__", 256), ("vo__", 256)):
+        scratch.update(scatter_scratch(tag, n))
+    sems = dict(send_sem=192, recv_sem=192, load_sem=18)
+    names = list(inputs) + list(outs) + list(scratch) + list(sems)
+    return pl.pallas_call(
+        functools.partial(main_kernel, names, mp, clouds, width, inner),
+        out_shape=[jax.ShapeDtypeStruct(*v) for v in outs.values()],
+        in_specs=[v[1] for v in inputs.values()],
+        out_specs=[vmem] * len(outs),
+        scratch_shapes=[pltpu.VMEM(*v) for v in scratch.values()]
+        + [pltpu.SemaphoreType.DMA((n,)) for n in sems.values()],
+        compiler_params=pltpu.CompilerParams(
+            vmem_limit_bytes=60 * 1024 * 1024, collective_id=0, has_side_effects=True
+        ),
+    )(*[v[0] for v in inputs.values()])
+
+
+def update_kernel(names, *args):
+    refs = dict(zip(names, args))
+    copies = [
+        pltpu.make_async_copy(refs["block_in"], refs["block_out"], refs["sem"].at[0]),
+        pltpu.make_async_copy(refs["feats_in"], refs["feats_out"], refs["sem"].at[1]),
+    ]
+    for copy in copies:
+        copy.start()
+    mp = lax.axis_index("mp")
+    sums = refs["sums"][...]
+    clip = jnp.sqrt(sums[0:1])
+    factor = jnp.minimum(1.0, clip_max / (clip + 1e-06))[0:1, 0:1]
+    refs["clip_out"][...] = clip
+    grads = own_parts(refs["own"], refs["small"], mp)
+    order, squares, steps = 0, [], []
+    for name in PIECES:
+        weights = load(refs, "weight", name)
+        parts = [
+            adam(g, factor, m, s, p)
+            for g, m, s, p in zip(grads[name], load(refs, "moment", name), load(refs, "second", name), weights)
+        ]
+        if order < 5:
+            pair = [(sums[1 + order : 2 + order, 0:1], sums[8 + order : 9 + order, 0:1])]
+        else:
+            kept = 1 if name == "vector" else None
+            pair = []
+            for a in (weights[0], parts[0][3]):
+                total = jnp.sum(a * a, axis=1, keepdims=True)
+                pair.append(total if kept else jnp.sum(total, axis=0, keepdims=True))
+            pair = [tuple(pair)]
+        order += 1
+        old, way = jnp.sqrt(pair[0][0]), jnp.sqrt(pair[0][1])
+        squares.append((old, way))
+        ratio = old / (way + 1e-06)
+        for i, (weight, part) in enumerate(zip(weights, parts)):
+            new = weight - learn_rate * ratio * part[3]
+            stored = {"grad": part[0], "new": new, "m": part[1], "s": part[2], "copy": new.astype(bf16)}
+            for kind, value in stored.items():
+                ref = refs[name + "_out_" + kind]
+                if name == "qkv":
+                    ref[i] = value
+                else:
+                    ref[...] = value
+    for side in range(2):
+        column = jnp.concatenate([s[side] for s in squares], axis=0)
+        refs["trust_out"][:, side : side + 1] = column
+    for copy in copies:
+        copy.wait()
+
+
+OUT_KINDS = (("grad", f32), ("new", f32), ("m", f32), ("s", f32), ("copy", bf16))
+
+
+def update_call(block, feats, own, small, sums, params):
+    vmem = pl.BlockSpec(memory_space=pltpu.VMEM)
+    anywhere = pl.BlockSpec(memory_space=pl.ANY)
+    inputs = {"block_in": (block, anywhere), "feats_in": (feats, anywhere)}
+    inputs.update(own=(own, vmem), small=(small, vmem), sums=(sums, vmem))
+    for name in PIECES:
+        for kind in SHAPES:
+            inputs[name + "_" + kind] = (params[name + "_" + kind], vmem)
+    outs = {"block_out": (block.shape, bf16, anywhere), "feats_out": (feats.shape, f32, anywhere)}
+    outs["clip_out"] = ((1, 128), f32, vmem)
+    outs["trust_out"] = ((14, 2), f32, vmem)
+    for name in PIECES:
+        for kind, dtype in OUT_KINDS:
+            outs[name + "_out_" + kind] = (params[name + "_weight"].shape, dtype, vmem)
+    names = list(inputs) + list(outs) + ["sem"]
+    result = pl.pallas_call(
+        functools.partial(update_kernel, names),
+        out_shape=[jax.ShapeDtypeStruct(*v[:2]) for v in outs.values()],
+        in_specs=[v[1] for v in inputs.values()],
+        out_specs=[v[2] for v in outs.values()],
+        scratch_shapes=[pltpu.SemaphoreType.DMA((2,))],
+        compiler_params=pltpu.CompilerParams(vmem_limit_bytes=60 * 1024 * 1024),
+    )(*[v[0] for v in inputs.values()])
+    return dict(zip(outs, result))
+
+
+def close_shards(*arrays):
+    feats, centres, counts, cotangent = arrays[:4]
+    mp_count = lax.axis_size("mp")
+    mp_index = lax.axis_index("mp")
+    share = feats.shape[0] // mp_count
+    clouds = share // PAD
+    inner = arrays[6].shape[1] * mp_count
+    params = {}
+    for k, kind in enumerate(SHAPES):
+        for i, name in enumerate(PIECES):
+            array = arrays[4 + 8 * k + i]
+            if name in ("out", "down"):
+                array = array.T
+            if name == "bias":
+                array = array[None]
+            params[name + "_" + kind] = array
+    mine = lax.dynamic_slice_in_dim(centres, mp_index * share, share, 1).T.reshape(clouds, PAD, 3)
+    points = jnp.pad(mine, ((0, 0), (0, SLOT - PAD), (0, 0)))
+    points = jnp.concatenate((points, jnp.ones((clouds, SLOT, 1), f32)), axis=2)
+    points = jnp.pad(points.reshape(clouds * SLOT, 4), ((0, 0), (0, 4)))
+    block, grad, own, small, sums = main_call(mp_count, inner, counts, feats, cotangent, points, params)
+    out = update_call(block, grad, own, small, sums, params)
+    outputs = [out["block_out"], out["feats_out"], out["clip_out"][0, 0], out["trust_out"].T]
+    for name in PIECES:
+        for kind, _ in OUT_KINDS:
+            array = out[name + "_out_" + kind]
+            if name in ("out", "down"):
+                array = array.T
+            if name == "bias":
+                array = array[0]
+            outputs.append(array)
+    return tuple(outputs)
+
+
 def solution(mesh):
     qkv, outw, upw, bias, whole = P(None, "dp", "mp"), P("mp", "dp"), P("dp", "mp"), P("mp"), P()
     params = (qkv, outw, upw, bias, outw, whole, whole, whole)
     in_specs = (P("dp", None), P(None, "dp"), P("dp"), P("dp", None)) + params * 3
     rows = P(("dp", "mp"), None)
     out_specs = (rows, rows, P(), P()) + tuple(spec for spec in params for _ in range(5))
-    return jax.shard_map(shards, mesh=mesh, in_specs=in_specs, out_specs=out_specs, check_vma=False)
+    form = close_shards if (mesh.shape["dp"], mesh.shape["mp"]) == (8, 4) else shards
+    return jax.shard_map(form, mesh=mesh, in_specs=in_specs, out_specs=out_specs, check_vma=False)

time: 531 us -> 176 us (0.33)
  waiting for transfers between devices: 242 us -> 0 us
  blocking collectives: 160 us -> 0 us
  Pallas kernels: 53.9 us -> 163 us
  between operations: 29.3 us -> 0.74 us
  other arithmetic: 31.6 us -> 6.32 us
  local copies, waits for them, and re-layouts: 12.9 us -> 6.23 us
    reduce_scatter x2 -> x0, waiting for transfers between devices: 137 us -> none  [the longest x1 69.2 us: shards(): own = lax.psum_scatter(own, 'dp', scatter_dimension=0, tiled=True)]
    psum x3 -> x0, blocking collectives: 119 us -> none  [the longest x1 39.7 us: shards(): lax.psum((bias_grad[:, 0], vec_grad[:7], pos_grad[:4], proj_grad), ('dp',...]
    pallas_call x1 -> x2, Pallas kernels: 53.9 us -> 163 us  [the longest x1 116 us: main_call(): pl.pallas_call(functools.partial(main_kernel, names, mp, clouds, width, i...]
    psum x1 -> x0, waiting for transfers between devices: 79.9 us -> none  [shards(): lax.psum((bias_grad[:, 0], vec_grad[:7], pos_grad[:4], proj_grad), ('dp',...]
    all_gather x2 -> x0, blocking collectives: 41.7 us -> none  [the longest x1 36.5 us: shards(): whole = lax.all_gather(packed, 'dp', axis=0, tiled=True)]
    all_gather x1 -> x0, waiting for transfers between devices: 23.7 us -> none  [shards(): whole = lax.all_gather(whole, 'mp', axis=0)]
    reduce_sum x23 -> x0, other arithmetic: 22.9 us -> none  [the longest x14 15.1 us: piece_squares(): return jnp.sum(array * array)[None]]
    pallas_call x0 -> x5, other arithmetic: none -> 6.28 us  [update_call(): pl.pallas_call(functools.partial(update_kernel, names), out_shape=[jax.Sh...]
  transfers between devices with their start and end apart: 4 -> 0, of which waited for: 4 -> 0; matrix products, arithmetic and copies ran while one was open for 3% -> 0% of each run, Pallas kernels for 0% -> 0%
where the time goes in v2:
time: 176 us
  Pallas kernels  163 us (93%)
  other arithmetic  6.32 us (4%)
  local copies, waits for them, and re-layouts  6.23 us (4%)
    pallas_call x1, Pallas kernels, main_call(): pl.pallas_call(functools.partial(main_kernel, names, mp, clouds, width, i...  116 us
    pallas_call x1, Pallas kernels, update_call(): pl.pallas_call(functools.partial(update_kernel, names), out_shape=[jax.Sh...  46.6 us
    pallas_call x5, other arithmetic, update_call(): pl.pallas_call(functools.partial(update_kernel, names), out_shape=[jax.Sh...  6.28 us
    broadcast_in_dim x3, local copies, waits for them, and re-layouts, close_shards(): array = array[None]  3.74 us

profile of v2, /device:TPU:0, one launch (start us, length us, event | category | flops | bytes accessed | tf_op | source)
XLA Modules:
  0.0 175.9 jit_solution(513596927394621954)
XLA Ops:
  0.7 0.0 copy-start
  0.7 1.2 broadcast_in_dim.10.args_13_.args_14_
  2.0 1.2 broadcast_in_dim.11.args_14_.args_15_
  3.2 1.2 broadcast_in_dim.12.args_15_.args_16_
  4.5 0.0 copy-done
  4.5 0.1 dynamic-slice_bitcast_fusion
  4.5 0.1 reshape.94
  4.6 0.2 copy.72
  4.9 0.8 pad.10.args_3_
  5.6 116.0 %shard_map.611 = (bf16[608,384]{1,0:T(8,128)(2,1)}, f32[608,384]{1,0:T(8,128)}, f32[48,1280]{1,0:T(8,128)}, f32[512,128]{1,0:T(8,128)}, f32[16,128]{1,0:T(8,128)}) custom-call(s32[64]{0:T(128)} %args_0_.4, bf16[2432,384]{1,0:T(8,128)(2,1)} %args_1_.4, bf16[2432,384]{1,0:T(8,128)(2,1)} %args_2_.4, f32[640,8]{1,0:T(8,128)} %pad.10.args_3_, ...), custom_call_target="tpu_custom_call" | custom-call | tf_op jit(solution)/shard_map/pallas_call | solution.py:1186
  121.7 46.6 %shard_map.612 = (bf16[608,384]{1,0:T(8,128)(2,1)}, f32[608,384]{1,0:T(8,128)}, f32[1,128]{1,0:T(1,128)}, f32[14,2]{1,0:T(8,128)}, f32[3,48,128]{2,1,0:T(8,128)}...) custom-call(bf16[608,384]{1,0:T(8,128)(2,1)} %get-tuple-element.93.a, ...), custom_call_target="tpu_custom_call" | custom-call | tf_op jit(solution)/shard_map/pallas_call | solution.py:1267
  168.3 1.3 copy.73
  169.7 1.3 reduce.4
  170.9 1.3 reduce
  172.2 1.3 reduce.1
  173.5 1.3 reduce.2
  174.7 1.2 reduce.3
  (1 shorter events, 0.0 us)
Async XLA Ops:
  0.7 3.8 %copy-start = (f32[3,2432]{1,0:T(4,128)S(1)}, f32[3,2432]{1,0:T(4,128)}, u32[]{:S(2)}) copy-start(f32[3,2432]{1,0:T(4,128)} %param.29) | copy-start | bytes 87556

commit v3 on v2

--- a/solution.py
+++ b/solution.py
@@ -64,7 +64,6 @@
         self.rows = clouds * SLOT
         self.block = GROUP * SLOT
         self.blocks = clouds // GROUP
-        self.tile = self.rows // 2 if self.rows % 32 == 0 else self.rows
         self.hid = self.proj_low.shape[0]
 
     def live(self, j):
@@ -121,221 +120,164 @@
         return rate * (scaled - first - hat * second)
 
     def entry(self):
-        t = self.tile
-
-        def step(i, carry):
-            rows = pl.ds(i * t, t)
-            pre = dot(self.points[rows, :], self.pos_hidden[...], NN, highest)
-            value, slope = gelu_pair(pre)
-            hidden = value.astype(bf16)
-            self.pos_slope[rows, :] = slope
-            self.hidden[rows, :] = hidden
-            term = dot(hidden, self.proj_low[...]) + self.vec[6:7, :]
-            x = self.stream[rows, :] + term
-            hat, rate = self.norm(x)
-            self.stream[rows, :] = x
-            self.hat_one[rows, :] = hat
-            self.rate_one[rows, :] = jnp.broadcast_to(rate, (t, 128))
-            self.normed_one[rows, :] = (hat * self.vec[0:1, :] + self.vec[2:3, :]).astype(bf16)
-            return carry
-
-        lax.fori_loop(0, self.rows // t, step, 0)
-
-    def project(self, j):
-        w = self.width
-        t = self.tile
-
-        def step(i, carry):
-            rows = pl.ds(i * t, t)
-            self.qkv[j, rows, :] = dot(self.normed_one[rows, :], self.w_qkv(j)).astype(bf16)
-            return carry
-
-        lax.fori_loop(0, self.rows // t, step, 0)
+        value, slope = gelu_pair(dot(self.points[...], self.pos_hidden[...], NN, highest))
+        hidden = value.astype(bf16)
+        self.pos_slope[...] = slope
+        self.hidden[...] = hidden
+        x = self.stream[...] + (dot(hidden, self.proj_low[...]) + self.vec[6:7, :])
+        hat, rate = self.norm(x)
+        self.stream[...] = x
+        self.hat_one[...] = hat
+        self.rate_one[...] = jnp.broadcast_to(rate, (self.rows, 128))
+        self.normed_one[...] = (hat * self.vec[0:1, :] + self.vec[2:3, :]).astype(bf16)
+
+    def project(self):
+        for j in range(self.mp):
+            self.qkv[j] = dot(self.normed_one[...], self.w_qkv(j)).astype(bf16)
 
     def lanes(self, h, n):
         lane = lax.broadcasted_iota(jnp.int32, (n, 128), 1)
         return (lane < HD) if h == 0 else (lane >= HD)
 
-    def attend(self, j, first):
+    def heads(self, rows):
+        for j in range(self.mp):
+            query = self.qkv[j, rows, 0:128] * jnp.asarray(1.0 / math.sqrt(HD), bf16)
+            for h in self.live(j):
+                own = self.lanes(h, self.block)
+                alone = jnp.where(own, query, jnp.zeros_like(query))
+                yield j, own, alone, self.qkv[j, rows, 128:256], self.qkv[j, rows, 256:384]
+
+    def attend(self):
         n = self.block
 
         def step(b, carry):
-            rows = pl.ds(b * n, n)
-            query = self.qkv[j, rows, 0:128] * jnp.asarray(1.0 / math.sqrt(HD), bf16)
-            keys = self.qkv[j, rows, 128:256]
-            values = self.qkv[j, rows, 256:384]
-            zero = jnp.zeros_like(query)
-            mixed = jnp.zeros((n, 128), f32)
-            for place, h in enumerate(self.live(j)):
-                own = self.lanes(h, n)
-                scores = dot(keys, jnp.where(own, query, zero), NT) + self.mask[b]
-                top = jnp.max(scores, axis=0, keepdims=True)
-                expo = jnp.exp(scores - top)
-                total = jnp.sum(expo, axis=0, keepdims=True)
-                probs = expo / total
-                self.probs[first + place, b] = probs
-                mixed = jnp.where(own, dot(probs.astype(bf16), values, TN), mixed)
-            self.attn_low[j, rows, :] = mixed.astype(bf16)
+            rows = pl.ds(pl.multiple_of(b * n, n), n)
+            mask = self.mask[b]
+            live = list(self.heads(rows))
+            scores = [dot(keys, query, NT) + mask for _, _, query, keys, _ in live]
+            low = []
+            for i, score in enumerate(scores):
+                expo = jnp.exp(score - jnp.max(score, axis=0, keepdims=True))
+                probs = expo * (1.0 / jnp.sum(expo, axis=0, keepdims=True))
+                self.probs[i, b] = probs
+                low.append(probs.astype(bf16))
+            mixed = [jnp.zeros((n, 128), f32)] * self.mp
+            for probs, (j, own, _, _, values) in zip(low, live):
+                mixed[j] = jnp.where(own, dot(probs, values, TN), mixed[j])
+            for j in range(self.mp):
+                self.attn_low[j, rows, :] = mixed[j].astype(bf16)
             return carry
 
-        lax.fori_loop(0, self.blocks, step, 0)
+        lax.fori_loop(0, self.blocks, step, 0, unroll=2)
 
     def middle(self):
-        t = self.tile
-
-        def step(i, carry):
-            rows = pl.ds(i * t, t)
-            x = self.stream[rows, :] + self.vec[4:5, :]
-            for j in range(self.mp):
-                x = x + dot(self.attn_low[j, rows, :], self.w_out(j), NT)
-            hat, rate = self.norm(x)
-            self.stream[rows, :] = x
-            self.hat_two[rows, :] = hat
-            self.rate_two[rows, :] = jnp.broadcast_to(rate, (t, 128))
-            self.normed_two[rows, :] = (hat * self.vec[1:2, :] + self.vec[3:4, :]).astype(bf16)
-            return carry
-
-        lax.fori_loop(0, self.rows // t, step, 0)
-
-    def feed(self, j):
-        t = self.tile
-
-        def step(i, carry):
-            rows = pl.ds(i * t, t)
-            pre = dot(self.normed_two[rows, :], self.w_up(j)) + self.up_bias[j, 0:1, :]
+        x = self.stream[...] + self.vec[4:5, :]
+        for j in range(self.mp):
+            x = x + dot(self.attn_low[j], self.w_out(j), NT)
+        hat, rate = self.norm(x)
+        self.stream[...] = x
+        self.hat_two[...] = hat
+        self.rate_two[...] = jnp.broadcast_to(rate, (self.rows, 128))
+        self.normed_two[...] = (hat * self.vec[1:2, :] + self.vec[3:4, :]).astype(bf16)
+
+    def feed(self):
+        total = self.stream[...]
+        for j in range(self.mp):
+            pre = dot(self.normed_two[...], self.w_up(j)) + self.up_bias[j, 0:1, :]
             value, slope = gelu_pair(pre)
             low = value.astype(bf16)
-            self.activated[j, rows, :] = low
-            self.slope[j, rows, :] = slope
-            self.stream[rows, :] += dot(low, self.w_down(j), NT)
+            self.activated[j] = low
+            self.slope[j] = slope
+            total = total + dot(low, self.w_down(j), NT)
+        self.stream[...] = total
+
+    def top(self):
+        keep = jnp.concatenate([self.keep[...]] * (self.width // 128), axis=1)
+        self.stream[...] = (self.stream[...] + self.vec[5:6, :]) * keep
+
+    def grad_start(self):
+        self.vec_grad[...] = jnp.zeros_like(self.vec_grad)
+        keep = jnp.concatenate([self.keep[...]] * (self.width // 128), axis=1)
+        grad = self.middle_grad[...] * keep
+        self.middle_grad[...] = grad
+        self.grad_top[...] = grad.astype(bf16)
+        self.vec_grad[5:6, :] = jnp.sum(grad, axis=0, keepdims=True)
+
+    def feed_back(self):
+        total = None
+        for j in range(self.mp):
+            grad = dot(self.grad_top[...], self.w_down(j)) * self.slope[j]
+            low = grad.astype(bf16)
+            self.grad_pre[j] = low
+            self.up_bias_grad[j, 0:1, :] = jnp.sum(low.astype(f32), axis=0, keepdims=True)
+            term = dot(low, self.w_up(j), NT)
+            total = term if j == 0 else total + term
+        self.normed_grad[...] = total
+
+    def middle_back(self):
+        grad, hat = self.normed_grad[...], self.hat_two[...]
+        rate = jnp.concatenate([self.rate_two[...]] * (self.width // 128), axis=1)
+        self.vec_grad[1:2, :] = jnp.sum(grad * hat, axis=0, keepdims=True)
+        self.vec_grad[3:4, :] = jnp.sum(grad, axis=0, keepdims=True)
+        out = self.middle_grad[...] + self.norm_back(grad, hat, rate, self.vec[1:2, :])
+        self.middle_grad[...] = out
+        self.vec_grad[4:5, :] = jnp.sum(out, axis=0, keepdims=True)
+        low = out.astype(bf16)
+        self.middle_low[...] = low
+        for j in range(self.mp):
+            self.attn_grad[j] = dot(low, self.w_out(j)).astype(bf16)
+
+    def attend_back(self):
+        n = self.block
+        scale = 1.0 / math.sqrt(HD)
+
+        def step(b, carry):
+            rows = pl.ds(pl.multiple_of(b * n, n), n)
+            live = list(self.heads(rows))
+            mine = []
+            for j, own, _, _, _ in live:
+                grad = self.attn_grad[j, rows, :]
+                mine.append(jnp.where(own, grad, jnp.zeros_like(grad)))
+            grad_probs = [dot(values, g, NT) for g, (_, _, _, _, values) in zip(mine, live)]
+            scores = []
+            grad_values = [jnp.zeros((n, 128), f32)] * self.mp
+            for i, (j, _, _, _, _) in enumerate(live):
+                probs = self.probs[i, b]
+                grad_values[j] = grad_values[j] + dot(probs.astype(bf16), mine[i])
+                inner = jnp.sum(probs * grad_probs[i], axis=0, keepdims=True)
+                scores.append((probs * (grad_probs[i] - inner)).astype(bf16))
+            grad_query = [jnp.zeros((n, 128), f32)] * self.mp
+            grad_keys = [jnp.zeros((n, 128), f32)] * self.mp
+            for grad, (j, own, query, keys, _) in zip(scores, live):
+                grad_keys[j] = grad_keys[j] + dot(grad, query)
+                grad_query[j] = jnp.where(own, dot(grad, keys, TN), grad_query[j])
+            for j in range(self.mp):
+                self.grad_proj[j, rows, 0:128] = (grad_query[j] * scale).astype(bf16)
+                self.grad_proj[j, rows, 128:256] = grad_keys[j].astype(bf16)
+                self.grad_proj[j, rows, 256:384] = grad_values[j].astype(bf16)
             return carry
 
-        lax.fori_loop(0, self.rows // t, step, 0)
-
-    def top(self):
-        t = self.tile
-
-        def step(i, carry):
-            rows = pl.ds(i * t, t)
-            keep = jnp.concatenate([self.keep[rows, :]] * (self.width // 128), axis=1)
-            self.stream[rows, :] = (self.stream[rows, :] + self.vec[5:6, :]) * keep
-            grad = self.middle_grad[rows, :] * keep
-            self.middle_grad[rows, :] = grad
-            self.grad_top[rows, :] = grad.astype(bf16)
-            self.vec_grad[5:6, :] += jnp.sum(grad, axis=0, keepdims=True)
-            return carry
-
-        self.vec_grad[...] = jnp.zeros_like(self.vec_grad)
-        self.up_bias_grad[...] = jnp.zeros_like(self.up_bias_grad)
-        lax.fori_loop(0, self.rows // t, step, 0)
-
-    def feed_back(self, j):
-        t = self.tile
-
-        def step(i, carry):
-            rows = pl.ds(i * t, t)
-            grad = dot(self.grad_top[rows, :], self.w_down(j)) * self.slope[j, rows, :]
-            low = grad.astype(bf16)
-            self.grad_pre[j, rows, :] = low
-            self.up_bias_grad[j, 0:1, :] += jnp.sum(low.astype(f32), axis=0, keepdims=True)
-            term = dot(low, self.w_up(j), NT)
-            if j == 0:
-                self.normed_grad[rows, :] = term
-            else:
-                self.normed_grad[rows, :] += term
-            return carry
-
-        lax.fori_loop(0, self.rows // t, step, 0)
-
-    def middle_back(self):
-        t = self.tile
-
-        def step(i, carry):
-            rows = pl.ds(i * t, t)
-            grad, hat = self.normed_grad[rows, :], self.hat_two[rows, :]
-            rate = jnp.concatenate([self.rate_two[rows, :]] * (self.width // 128), axis=1)
-            self.vec_grad[1:2, :] += jnp.sum(grad * hat, axis=0, keepdims=True)
-            self.vec_grad[3:4, :] += jnp.sum(grad, axis=0, keepdims=True)
-            out = self.middle_grad[rows, :] + self.norm_back(grad, hat, rate, self.vec[1:2, :])
-            self.middle_grad[rows, :] = out
-            self.vec_grad[4:5, :] += jnp.sum(out, axis=0, keepdims=True)
-            self.middle_low[rows, :] = out.astype(bf16)
-            return carry
-
-        lax.fori_loop(0, self.rows // t, step, 0)
-
-    def attend_grad(self, j):
-        t = self.tile
-
-        def step(i, carry):
-            rows = pl.ds(i * t, t)
-            self.attn_grad[j, rows, :] = dot(self.middle_low[rows, :], self.w_out(j)).astype(bf16)
-            return carry
-
-        lax.fori_loop(0, self.rows // t, step, 0)
-
-    def attend_back(self, j, first):
-        n = self.block
-
-        def step(b, carry):
-            rows = pl.ds(b * n, n)
-            scale = 1.0 / math.sqrt(HD)
-            query = self.qkv[j, rows, 0:128] * jnp.asarray(scale, bf16)
-            keys = self.qkv[j, rows, 128:256]
-            values = self.qkv[j, rows, 256:384]
-            grad_out = self.attn_grad[j, rows, :]
-            zero = jnp.zeros_like(query)
-            grad_query = jnp.zeros((n, 128), f32)
-            grad_keys = jnp.zeros((n, 128), f32)
-            grad_values = jnp.zeros((n, 128), f32)
-            for place, h in enumerate(self.live(j)):
-                own = self.lanes(h, n)
-                mine = jnp.where(own, grad_out, zero)
-                probs = self.probs[first + place, b]
-                grad_probs = dot(values, mine, NT)
-                grad_values = grad_values + dot(probs.astype(bf16), mine)
-                inner = jnp.sum(probs * grad_probs, axis=0, keepdims=True)
-                grad_scores = (probs * (grad_probs - inner)).astype(bf16)
-                grad_keys = grad_keys + dot(grad_scores, jnp.where(own, query, zero))
-                grad_query = jnp.where(own, dot(grad_scores, keys, TN), grad_query)
-            self.grad_proj[j, rows, 0:128] = (grad_query * scale).astype(bf16)
-            self.grad_proj[j, rows, 128:256] = grad_keys.astype(bf16)
-            self.grad_proj[j, rows, 256:384] = grad_values.astype(bf16)
-            return carry
-
-        lax.fori_loop(0, self.blocks, step, 0)
+        lax.fori_loop(0, self.blocks, step, 0, unroll=2)
 
     def entry_back(self):
-        t = self.tile
-
-        def step(i, carry):
-            rows = pl.ds(i * t, t)
-            grad = jnp.zeros((t, self.width), f32)
-            for j in range(self.mp):
-                grad = grad + dot(self.grad_proj[j, rows, :], self.w_qkv(j), NT)
-            hat = self.hat_one[rows, :]
-            rate = jnp.concatenate([self.rate_one[rows, :]] * (self.width // 128), axis=1)
-            self.vec_grad[0:1, :] += jnp.sum(grad * hat, axis=0, keepdims=True)
-            self.vec_grad[2:3, :] += jnp.sum(grad, axis=0, keepdims=True)
-            out = self.middle_grad[rows, :] + self.norm_back(grad, hat, rate, self.vec[0:1, :])
-            self.middle_grad[rows, :] = out
-            self.vec_grad[6:7, :] += jnp.sum(out, axis=0, keepdims=True)
-            low = out.astype(bf16)
-            self.pos_low[rows, :] = low
-            self.pre_grad[rows, :] = dot(low, self.proj_low[...], NT) * self.pos_slope[rows, :]
-            return carry
-
-        lax.fori_loop(0, self.rows // t, step, 0)
+        grad = None
+        for j in range(self.mp):
+            term = dot(self.grad_proj[j], self.w_qkv(j), NT)
+            grad = term if j == 0 else grad + term
+        hat = self.hat_one[...]
+        rate = jnp.concatenate([self.rate_one[...]] * (self.width // 128), axis=1)
+        self.vec_grad[0:1, :] = jnp.sum(grad * hat, axis=0, keepdims=True)
+        self.vec_grad[2:3, :] = jnp.sum(grad, axis=0, keepdims=True)
+        out = self.middle_grad[...] + self.norm_back(grad, hat, rate, self.vec[0:1, :])
+        self.middle_grad[...] = out
+        self.vec_grad[6:7, :] = jnp.sum(out, axis=0, keepdims=True)
+        low = out.astype(bf16)
+        self.pos_low[...] = low
+        self.pre_grad[...] = dot(low, self.proj_low[...], NT) * self.pos_slope[...]
 
     def turn(self, source, target):
-        n = 128
-
-        def step(i, carry):
-            block = source[pl.ds(i * n, n), :].astype(f32)
-            target[:, pl.ds(pl.multiple_of(i * n, n), n)] = block.T.astype(bf16)
-            return carry
-
-        lax.fori_loop(0, self.rows // n, step, 0)
+        for i in range(self.rows // 128):
+            target[:, 128 * i : 128 * i + 128] = source[128 * i : 128 * i + 128, :].T
 
     def gather_rows(self, source, target):
         for c in range(self.clouds):
@@ -380,10 +322,6 @@
     return shapes
 
 
-def heads_before(mp, j):
-    return sum(2 if i < mp // 2 else 1 for i in range(j))
-
-
 def compute_kernel(names, mp, clouds, width, inner, *args):
     refs = dict(zip(names, args))
     layer = Layer(refs, mp, clouds, width, inner)
@@ -397,17 +335,15 @@
     layer.spread_rows()
     layer.masks()
     layer.entry()
-    for j in range(mp):
-        layer.project(j)
-        layer.attend(j, heads_before(mp, j))
+    layer.project()
+    layer.attend()
     layer.middle()
-    for j in range(mp):
-        layer.feed(j)
+    layer.feed()
     layer.top()
     layer.gather_rows(layer.stream, layer.stage)
     layer.block_out[...] = layer.stage[...].astype(bf16)
-    for j in range(mp):
-        layer.feed_back(j)
+    layer.grad_start()
+    layer.feed_back()
     g = layer.grads
     layer.turn(layer.grad_top, layer.turned)
     for j in range(mp):
@@ -419,8 +355,7 @@
     layer.turn(layer.middle_low, layer.turned)
     for j in range(mp):
         g[j, :, 384:512] = dot(layer.turned[...], layer.attn_low[j])
-        layer.attend_grad(j)
-        layer.attend_back(j, heads_before(mp, j))
+    layer.attend_back()
     layer.turn(layer.normed_one, layer.turned)
     for j in range(mp):
         g[j, :, 0:384] = dot(layer.turned[...], layer.grad_proj[j])
@@ -865,7 +800,7 @@
     ref = refs[name + "_" + kind]
     if name == "qkv":
         return [ref[i] for i in range(3)]
-    return [ref[...]]
+    return [ref[...].reshape(1, -1)] if name == "bias" else [ref[...]]
 
 
 def main_kernel(names, mp, clouds, width, inner, *args):
@@ -901,7 +836,7 @@
     w[links.mp, links.z, links.y, :, 384:512] = refs["out_weight"][...].astype(bf16)
     w[links.mp, links.z, links.y, :, 512 : 512 + cols] = refs["up_weight"][...].astype(bf16)
     w[links.mp, links.z, links.y, :, 512 + cols : 512 + 2 * cols] = refs["down_weight"][...].astype(bf16)
-    layer.up_bias[links.mp] = jnp.broadcast_to(refs["bias_weight"][...], (8, cols))
+    layer.up_bias[links.mp] = jnp.broadcast_to(refs["bias_weight"][...].reshape(1, cols), (8, cols))
     links.met()
     gathers = [
         Gather(links, w, 0, 256, False),
@@ -939,74 +874,66 @@
     bias_last = links.send(other_bias, other_bias, links.core())
     for g in gathers[:2]:
         g.end()
-    layer.project(0)
+    layer.project()
     for g in gathers[2:]:
         g.third()
-    layer.attend(0, heads_before(mp, 0))
-    for j in range(1, mp):
-        layer.project(j)
-        layer.attend(j, heads_before(mp, j))
-        if j == 1:
-            for g in gathers[2:]:
-                g.fourth()
+    layer.attend()
+    for g in gathers[2:]:
+        g.fourth()
     layer.middle()
     for g in gathers[2:]:
         g.end()
     twin = links.mp + 1 - 2 * links.c
     links.wait(bias_core, layer.up_bias.at[twin])
     links.wait(bias_last, layer.up_bias.at[twin + 2 - 4 * links.x])
-    for j in range(mp):
-        layer.feed(j)
+    layer.feed()
+
+    def scatter(tag, flip):
+        return Scatter(links, {n[len(tag) :]: refs[n] for n in names if n.startswith(tag)}, flip)
+
+    down, up = scatter("down__", True), scatter("up__", False)
+    qk, vo = scatter("qk__", False), scatter("vo__", True)
+
+    def weigh(product, *targets):
+        for x in range(2):
+            pair = [product(2 * x), product(2 * x + 1)]
+            kept = jnp.where(links.c == 0, pair[0], pair[1])
+            sent = jnp.where(links.c == 0, pair[1], pair[0]).astype(bf16)
+            lo = 0
+            for target in targets:
+                hi = lo + target.kept.shape[-1]
+                target.core_out[x] = sent[:, lo:hi].reshape(4, 2, 48, hi - lo)
+                target.kept[x] = kept[:, lo:hi].reshape(4, 2, 48, hi - lo)
+                lo = hi
+
+    def heads_out(j):
+        parts = dot(layer.turned[...], layer.grad_proj[j]), dot(layer.turned_mid[...], layer.attn_low[j])
+        return jnp.concatenate(parts, axis=1)
+
+    layer.grad_start()
+    layer.turn(layer.grad_top, layer.turned)
+    weigh(lambda j: dot(layer.turned[...], layer.activated[j]), down)
+    down.start()
     layer.top()
     layer.gather_rows(layer.stream, layer.stage)
     layer.block_out[...] = layer.stage[...].astype(bf16)
-
-    def scatter(tag, flip):
-        return Scatter(links, {n[len(tag) :]: refs[n] for n in names if n.startswith(tag)}, flip)
-
-    down, up = scatter("down__", True), scatter("up__", False)
-    qk, vo = scatter("qk__", False), scatter("vo__", True)
-
-    def weigh(target, product):
-        for x in range(2):
-            block = product(x * 2 + 1 - links.c).astype(bf16)
-            target.core_out[x] = block.reshape(4, 2, 48, block.shape[-1])
-        for x in range(2):
-            block = product(x * 2 + links.c)
-            target.kept[x] = block.reshape(4, 2, 48, block.shape[-1])
-
-    def values_out(j):
-        values = dot(layer.turned[...], layer.grad_proj[j, :, 256:384])
-        return jnp.concatenate([values, dot(layer.turned_mid[...], layer.attn_low[j])], axis=1)
-
-    layer.turn(layer.grad_top, layer.turned)
-    weigh(down, lambda j: dot(layer.turned[...], layer.activated[j]))
-    down.start()
-    layer.feed_back(0)
     down.second()
-    for j in range(1, mp):
-        layer.feed_back(j)
+    layer.feed_back()
     layer.turn(layer.normed_two, layer.turned)
-    weigh(up, lambda j: dot(layer.turned[...], layer.grad_pre[j]))
+    weigh(lambda j: dot(layer.turned[...], layer.grad_pre[j]), up)
     up.start()
     down.third()
     layer.middle_back()
     up.second()
     layer.turn(layer.middle_low, layer.turned_mid)
-    for j in range(mp):
-        layer.attend_grad(j)
-    layer.attend_back(0, heads_before(mp, 0))
     down.fourth()
+    layer.attend_back()
     up.third()
-    layer.attend_back(1, heads_before(mp, 1))
+    layer.turn(layer.normed_one, layer.turned)
+    weigh(heads_out, qk, vo)
+    qk.start()
+    vo.start()
     up.fourth()
-    for j in range(2, mp):
-        layer.attend_back(j, heads_before(mp, j))
-    layer.turn(layer.normed_one, layer.turned)
-    weigh(vo, values_out)
-    vo.start()
-    weigh(qk, lambda j: dot(layer.turned[...], layer.grad_proj[j, :, 0:256]))
-    qk.start()
     vo.second()
     layer.entry_back()
     qk.second()
@@ -1238,10 +1165,18 @@
                 if name == "qkv":
                     ref[i] = value
                 else:
-                    ref[...] = value
+                    ref[...] = value.reshape(ref.shape)
+    place = lax.broadcasted_iota(jnp.int32, (8, 128), 0)
+    lane = lax.broadcasted_iota(jnp.int32, (8, 128), 1)
+    trust = jnp.zeros((8, 128), f32)
     for side in range(2):
-        column = jnp.concatenate([s[side] for s in squares], axis=0)
-        refs["trust_out"][:, side : side + 1] = column
+        column = 0
+        for pair in squares:
+            for r in range(pair[side].shape[0]):
+                value = jnp.broadcast_to(pair[side][r : r + 1, :], (8, 128))
+                trust = jnp.where((place == side) & (lane == column), value, trust)
+                column += 1
+    refs["trust_out"][...] = trust[0:2, 0:14]
     for copy in copies:
         copy.wait()
 
@@ -1252,14 +1187,14 @@
 def update_call(block, feats, own, small, sums, params):
     vmem = pl.BlockSpec(memory_space=pltpu.VMEM)
     anywhere = pl.BlockSpec(memory_space=pl.ANY)
-    inputs = {"block_in": (block, anywhere), "feats_in": (feats, anywhere)}
+    inputs = {"block_in": (block, vmem), "feats_in": (feats, vmem)}
     inputs.update(own=(own, vmem), small=(small, vmem), sums=(sums, vmem))
     for name in PIECES:
         for kind in SHAPES:
             inputs[name + "_" + kind] = (params[name + "_" + kind], vmem)
     outs = {"block_out": (block.shape, bf16, anywhere), "feats_out": (feats.shape, f32, anywhere)}
     outs["clip_out"] = ((1, 128), f32, vmem)
-    outs["trust_out"] = ((14, 2), f32, vmem)
+    outs["trust_out"] = ((2, 14), f32, vmem)
     for name in PIECES:
         for kind, dtype in OUT_KINDS:
             outs[name + "_out_" + kind] = (params[name + "_weight"].shape, dtype, vmem)
@@ -1288,8 +1223,6 @@
             array = arrays[4 + 8 * k + i]
             if name in ("out", "down"):
                 array = array.T
-            if name == "bias":
-                array = array[None]
             params[name + "_" + kind] = array
     mine = lax.dynamic_slice_in_dim(centres, mp_index * share, share, 1).T.reshape(clouds, PAD, 3)
     points = jnp.pad(mine, ((0, 0), (0, SLOT - PAD), (0, 0)))
@@ -1297,14 +1230,12 @@
     points = jnp.pad(points.reshape(clouds * SLOT, 4), ((0, 0), (0, 4)))
     block, grad, own, small, sums = main_call(mp_count, inner, counts, feats, cotangent, points, params)
     out = update_call(block, grad, own, small, sums, params)
-    outputs = [out["block_out"], out["feats_out"], out["clip_out"][0, 0], out["trust_out"].T]
+    outputs = [out["block_out"], out["feats_out"], out["clip_out"][0, 0], out["trust_out"]]
     for name in PIECES:
         for kind, _ in OUT_KINDS:
             array = out[name + "_out_" + kind]
             if name in ("out", "down"):
                 array = array.T
-            if name == "bias":
-                array = array[0]
             outputs.append(array)
     return tuple(outputs)
 

time: 176 us -> 106 us (0.60)
  Pallas kernels: 163 us -> 103 us
  other arithmetic: 6.32 us -> 0.03 us
  local copies, waits for them, and re-layouts: 6.23 us -> 1.91 us
    pallas_call x1, Pallas kernels: 46.6 us -> 4.54 us  [update_call(): pl.pallas_call(functools.partial(update_kernel, names), out_shape=[jax.Sh...]
    pallas_call x1, Pallas kernels: 116 us -> 98.4 us  [main_call(): pl.pallas_call(functools.partial(main_kernel, names, mp, clouds, width, i...]
    pallas_call x5 -> x0, other arithmetic: 6.28 us -> none  [update_call(): pl.pallas_call(functools.partial(update_kernel, names), out_shape=[jax.Sh...]
    broadcast_in_dim x3 -> x0, local copies, waits for them, and re-layouts: 3.74 us -> none  [close_shards(): array = array[None]]
where the time goes in v3:
time: 106 us
  Pallas kernels  103 us (97%)
  local copies, waits for them, and re-layouts  1.91 us (2%)
    pallas_call x1, Pallas kernels, main_call(): pl.pallas_call(functools.partial(main_kernel, names, mp, clouds, width, i...  98.4 us
    pallas_call x1, Pallas kernels, update_call(): pl.pallas_call(functools.partial(update_kernel, names), out_shape=[jax.Sh...  4.54 us

profile of v3, /device:TPU:0, one launch (start us, length us, event | category | flops | bytes accessed | tf_op | source)
XLA Modules:
  0.0 105.8 jit_solution(2771962726753872939)
XLA Ops:
  0.7 0.0 copy-start
  0.7 0.8 copy-done
  1.5 0.1 dynamic-slice_bitcast_fusion
  1.5 0.1 reshape.94
  1.6 0.2 copy.72
  1.9 0.8 pad.10.args_3_
  2.7 98.4 %shard_map.611 = (bf16[608,384]{1,0:T(8,128)(2,1)}, f32[608,384]{1,0:T(8,128)}, f32[48,1280]{1,0:T(8,128)}, f32[512,128]{1,0:T(8,128)}, f32[16,128]{1,0:T(8,128)}) custom-call(s32[64]{0:T(128)} %args_0_.4, bf16[2432,384]{1,0:T(8,128)(2,1)} %args_1_.4, bf16[2432,384]{1,0:T(8,128)(2,1)} %args_2_.4, f32[640,8]{1,0:T(8,128)} %pad.10.args_3_, ...), custom_call_target="tpu_custom_call" | custom-call | tf_op jit(solution)/shard_map/pallas_call | solution.py:1113
  101.1 4.5 %shard_map.612 = (bf16[608,384]{1,0:T(8,128)(2,1)}, f32[608,384]{1,0:T(8,128)}, f32[1,128]{1,0:T(1,128)}, f32[2,14]{1,0:T(2,128)}, f32[3,48,128]{2,1,0:T(8,128)}...) custom-call(bf16[608,384]{1,0:T(8,128)(2,1)} %get-tuple-element.93.a, ...), custom_call_target="tpu_custom_call" | custom-call | tf_op jit(solution)/shard_map/pallas_call | solution.py:1202
  (1 shorter events, 0.0 us)
Async XLA Ops:
  0.7 0.8 copy-start

commit v4 on v3

--- a/solution.py
+++ b/solution.py
@@ -147,7 +147,7 @@
                 alone = jnp.where(own, query, jnp.zeros_like(query))
                 yield j, own, alone, self.qkv[j, rows, 128:256], self.qkv[j, rows, 256:384]
 
-    def attend(self):
+    def attend(self, start, stop):
         n = self.block
 
         def step(b, carry):
@@ -168,7 +168,7 @@
                 self.attn_low[j, rows, :] = mixed[j].astype(bf16)
             return carry
 
-        lax.fori_loop(0, self.blocks, step, 0, unroll=2)
+        lax.fori_loop(start, stop, step, 0, unroll=2)
 
     def middle(self):
         x = self.stream[...] + self.vec[4:5, :]
@@ -317,7 +317,6 @@
         pos_low=((rows, width), bf16),
         pre_grad=((rows, hid), f32),
         turned=((width, rows), bf16),
-        turned_mid=((width, rows), bf16),
     )
     return shapes
 
@@ -336,7 +335,7 @@
     layer.masks()
     layer.entry()
     layer.project()
-    layer.attend()
+    layer.attend(0, layer.blocks)
     layer.middle()
     layer.feed()
     layer.top()
@@ -530,8 +529,9 @@
         self.x, self.c = mp // 2, lax.rem(mp, 2)
         self.mp = mp
         self.plane = self.y * 4 + mp
+        self.line = [self.z, self.z + 1 - 2 * lax.rem(self.z, 2), lax.rem(self.z + 2, 4), 3 - self.z]
         self.send_sem, self.recv_sem = send, recv
-        self.count = 0
+        self.counts = [0, 0]
         self.sent = []
 
     def at(self, z, y, x, c):
@@ -547,10 +547,7 @@
         return self.at(self.z, 1 - self.y, self.x, self.c)
 
     def far(self, k):
-        return self.at(lax.rem(self.z + k, 4), self.y, self.x, self.c)
-
-    def back(self, k):
-        return lax.rem(self.z + 4 - k, 4)
+        return self.at(self.line[k], self.y, self.x, self.c)
 
     def round(self, k):
         other = lax.rem(self.plane + k, 8)
@@ -567,26 +564,40 @@
     def met(self):
         pl.semaphore_wait(pltpu.get_barrier_semaphore(), 10)
 
-    def copy(self, source, target, who, i):
+    def copy(self, source, target, i):
         return pltpu.make_async_remote_copy(
             src_ref=source,
             dst_ref=target,
-            send_sem=self.send_sem.at[i],
-            recv_sem=self.recv_sem.at[i],
+            send_sem=self.send_sem.at[i] if i < self.send_sem.shape[0] else self.send_sem.at[0],
+            recv_sem=self.recv_sem.at[i] if i < self.recv_sem.shape[0] else self.recv_sem.at[0],
+            device_id=self.core(),
+            device_id_type=pl.DeviceIdType.MESH,
+        )
+
+    def mark(self, side):
+        self.counts[side] += 1
+        return self.counts[side] - 1
+
+    def send(self, source, target, who, out=None, into=None):
+        into = self.mark(1) if into is None else into
+        copy = pltpu.make_async_remote_copy(
+            src_ref=source,
+            dst_ref=target,
+            send_sem=self.send_sem.at[self.mark(0) if out is None else out],
+            recv_sem=self.recv_sem.at[into],
             device_id=who,
             device_id_type=pl.DeviceIdType.MESH,
         )
-
-    def send(self, source, target, who):
-        i = self.count
-        self.count += 1
-        copy = self.copy(source, target, who, i)
         copy.start()
-        self.sent.append(copy)
-        return i
+        if out is None:
+            self.sent.append(copy)
+        return into
 
     def wait(self, i, target):
-        self.copy(target, target, self.core(), i).wait_recv()
+        self.copy(target, target, i).wait_recv()
+
+    def sent_all(self, out, source):
+        self.sent.append(self.copy(source, source, out))
 
     def finish(self):
         for copy in self.sent:
@@ -600,76 +611,61 @@
     def part(self, mp, z, y):
         return self.w.at[mp, z, y, :, self.lo : self.hi]
 
-    def spread(self, block):
-        k = self.links
-        return (k.send(block, block, k.deep()), k.send(block, block, k.side()), k.send(block, block, k.core()))
-
     def start(self):
         k = self.links
         own = self.part(k.mp, k.z, k.y)
-        self.along = [k.send(own, own, k.far(i)) for i in (3, 2, 1)][::-1]
-        self.spreads = [self.spread(own)]
-
-    def second(self):
+        self.along = [k.send(own, own, k.far(i)) for i in (1, 2, 3)]
+        self.out = [k.mark(0) for _ in range(5)]
+        self.first = [k.mark(1) for _ in range(4)]
+        self.into = [k.mark(1) for _ in range(4)]
+
+    def step(self, i):
         k = self.links
-        for i in (1, 2, 3):
-            block = self.part(k.mp, k.back(i), k.y)
+        block = self.part(k.mp, k.line[i], k.y)
+        if i:
             k.wait(self.along[i - 1], block)
-            self.spreads.append(self.spread(block))
-
-    def third(self):
+        near, next_ = (k.side(), k.deep()) if self.flip else (k.deep(), k.side())
+        k.send(block, block, near, self.out[0], self.first[i])
+        k.send(block, block, k.core(), self.out[1], self.into[0])
+        k.send(block, block, next_, self.out[2], self.into[1])
+
+    def regions(self, mp, z):
         k = self.links
-        other = k.mp + 2 - 4 * k.x
-        for i in range(4):
-            z = k.back(i)
-            if self.flip:
-                k.wait(self.spreads[i][1], self.part(other, z, k.y))
-            else:
-                k.wait(self.spreads[i][0], self.part(k.mp, z, 1 - k.y))
-        if self.flip:
-            block = self.part(other, slice(None), k.y)
-            self.wide = k.send(block, block, k.deep())
-            self.core_first = k.send(block, block, k.core())
-        else:
-            block = self.part(k.mp, slice(None), 1 - k.y)
-            self.wide = k.send(block, block, k.side())
-            self.core_first = k.send(block, block, k.core())
-
-    def fourth(self):
+        across = mp + 2 - 4 * k.x
+        side, deep = self.part(across, z, k.y), self.part(mp, z, 1 - k.y)
+        return (side, deep) if self.flip else (deep, side), self.part(across, z, 1 - k.y)
+
+    def hop(self, i):
         k = self.links
-        other = k.mp + 2 - 4 * k.x
-        for i in range(4):
-            z = k.back(i)
-            if self.flip:
-                k.wait(self.spreads[i][0], self.part(k.mp, z, 1 - k.y))
-            else:
-                k.wait(self.spreads[i][1], self.part(other, z, k.y))
-        if self.flip:
-            near = self.part(k.mp, slice(None), 1 - k.y)
-            self.core_second = k.send(near, near, k.core())
-            self.far_wait = self.part(other, slice(None), 1 - k.y)
-            k.wait(self.wide, self.far_wait)
-            self.core_third = k.send(self.far_wait, self.far_wait, k.core())
-        else:
-            near = self.part(other, slice(None), k.y)
-            self.core_second = k.send(near, near, k.core())
-            self.far_wait = self.part(other, slice(None), 1 - k.y)
-            k.wait(self.wide, self.far_wait)
-            self.core_third = k.send(self.far_wait, self.far_wait, k.core())
+        block = self.regions(k.mp, k.line[i])[0][0]
+        k.wait(self.first[i], block)
+        k.send(block, block, k.deep() if self.flip else k.side(), self.out[3], self.into[2])
+        k.send(block, block, k.core(), self.out[4], self.into[3])
+
+    def rest(self):
+        k = self.links
+        block = self.regions(k.mp, slice(None))[0][1]
+        k.wait(self.into[1], block)
+        self.rest_twin = k.send(block, block, k.core())
+
+    def corner(self):
+        k = self.links
+        block = self.regions(k.mp, slice(None))[1]
+        k.wait(self.into[2], block)
+        self.corner_twin = k.send(block, block, k.core())
 
     def end(self):
         k = self.links
         twin = k.mp + 1 - 2 * k.c
-        other = twin + 2 - 4 * k.x
-        for i in range(4):
-            k.wait(self.spreads[i][2], self.part(twin, k.back(i), k.y))
-        if self.flip:
-            k.wait(self.core_first, self.part(other, slice(None), k.y))
-            k.wait(self.core_second, self.part(twin, slice(None), 1 - k.y))
-        else:
-            k.wait(self.core_first, self.part(twin, slice(None), 1 - k.y))
-            k.wait(self.core_second, self.part(other, slice(None), k.y))
-        k.wait(self.core_third, self.part(other, slice(None), 1 - k.y))
+        near, corner = self.regions(twin, slice(None))
+        k.wait(self.into[0], self.part(twin, slice(None), k.y))
+        k.wait(self.into[3], near[0])
+        k.wait(self.rest_twin, near[1])
+        k.wait(self.corner_twin, corner)
+        line = self.part(k.mp, slice(None), k.y)
+        first = self.regions(k.mp, slice(None))[0][0]
+        for out, block in zip(self.out, (line, line, line, first, first)):
+            k.sent_all(out, block)
 
 
 class Scatter:
@@ -714,7 +710,7 @@
         k.wait(self.last, self.last_in)
         self.along = []
         for i in range(4):
-            z = lax.rem(k.z + i, 4)
+            z = k.line[i]
             mid = self.next_in[k.x, z] if self.flip else self.next_in[k.y, z]
             total = self.pair(k.x, z, k.y) + mid.astype(f32) + self.last_in[z].astype(f32)
             if i == 0:
@@ -812,17 +808,20 @@
     links.greet()
     share = clouds * PAD
     rows = pl.ds(pl.multiple_of(links.mp * share, 16), share)
-    local = [
-        pltpu.make_async_copy(layer.feats_all.at[rows, :], layer.feats, layer.load_sem.at[0]),
-        pltpu.make_async_copy(layer.top_all.at[rows, :], layer.cotangent, layer.load_sem.at[1]),
-    ]
-    late = []
-    for i, name in enumerate(name for name in PIECES for kind in ("moment", "second")):
-        kind = ("moment", "second")[i % 2]
-        source, target = refs[name + "_" + kind + "_all"], refs[name + "_" + kind]
-        late.append(pltpu.make_async_copy(source, target, layer.load_sem.at[2 + i]))
-    for copy in local + late:
-        copy.start()
+    sources = {"feats": layer.feats_all.at[rows, :], "cotangent": layer.top_all.at[rows, :]}
+    for kind in SHAPES:
+        for name in PIECES:
+            sources[name + "_" + kind] = refs[name + "_" + kind + "_all"]
+    sources["points"] = layer.points_all
+    copies = {
+        name: pltpu.make_async_copy(source, refs[name], layer.load_sem.at[i])
+        for i, (name, source) in enumerate(sources.items())
+    }
+    first = [name + "_weight" for name in ("qkv", "out", "up", "down", "bias")]
+    early = ["feats", "points", "hidden_weight", "proj_weight", "vector_weight", "cotangent"]
+    late = [copy for name, copy in copies.items() if name not in first + early]
+    for name in first + early:
+        copies[name].start()
 
     def flat(j, lo, hi):
         return w[j, :, :, :, lo:hi].reshape(width, hi - lo)
@@ -831,6 +830,8 @@
     layer.w_out = lambda j: flat(j, 384, 512)
     layer.w_up = lambda j: flat(j, 512, 512 + cols)
     layer.w_down = lambda j: flat(j, 512 + cols, 512 + 2 * cols)
+    for name in first:
+        copies[name].wait()
     for i in range(3):
         w[links.mp, links.z, links.y, :, 128 * i : 128 * i + 128] = refs["qkv_weight"][i].astype(bf16)
     w[links.mp, links.z, links.y, :, 384:512] = refs["out_weight"][...].astype(bf16)
@@ -844,45 +845,71 @@
         Gather(links, w, 512, 512 + cols, False),
         Gather(links, w, 512 + cols, 512 + 2 * cols, True),
     ]
-    for g in gathers[:2]:
-        g.start()
+    near, wide = gathers[:2], gathers[2:]
+
+    def each(group, step, *a):
+        for g in group:
+            getattr(g, step)(*a)
+
+    for group in (near, wide):
+        each(group, "start")
+        each(group, "step", 0)
     own_bias = layer.up_bias.at[links.mp]
     bias_side = links.send(own_bias, own_bias, links.side())
     bias_core = links.send(own_bias, own_bias, links.core())
-    for g in gathers[2:]:
-        g.start()
+    for copy in late:
+        copy.start()
+    for name in early:
+        copies[name].wait()
     layer.proj_low[...] = refs["proj_weight"][...].astype(bf16)
-    layer.vec = refs["vector_weight"]
-    layer.pos_hidden[...] = jnp.zeros((8, 128), f32)
-    layer.pos_hidden[0:4, :] = refs["hidden_weight"][...]
-    for copy in local:
-        copy.wait()
+    layer.vec = jnp.concatenate([refs["vector_weight"][...], jnp.zeros((1, width), f32)], axis=0)
+    layer.pos_hidden[...] = jnp.concatenate([refs["hidden_weight"][...], jnp.zeros((4, 128), f32)], axis=0)
     layer.counts = _Shifted(layer.counts_all, links.mp * clouds)
     layer.spread_rows()
-    for g in gathers[:2]:
-        g.second()
+    each(near, "step", 1)
+    layer.entry()
+    each(near, "step", 2)
     layer.masks()
-    for g in gathers[:2]:
-        g.third()
-    layer.entry()
-    for g in gathers[2:]:
-        g.second()
-    for g in gathers[:2]:
-        g.fourth()
+    each(near, "step", 3)
+    each(near, "hop", 0)
+    each(near, "hop", 1)
+    layer.grad_start()
+    each(near, "hop", 2)
+    each(wide, "step", 1)
+    layer.turn(layer.grad_top, layer.turned_top)
+    each(near, "hop", 3)
+    each(wide, "step", 2)
+    layer.turn(layer.normed_one, layer.turned_one)
     other_bias = layer.up_bias.at[links.mp + 2 - 4 * links.x]
     links.wait(bias_side, other_bias)
     bias_last = links.send(other_bias, other_bias, links.core())
-    for g in gathers[:2]:
-        g.end()
+    lead = (links.z * 2 + links.y == 0).astype(f32)
+
+    def five(parts):
+        out = []
+        for name in ("qkv", "out", "up", "bias", "down"):
+            row = sum(square_row(p) for p in parts[name])
+            out.append(row * lead if name == "bias" else row)
+        return out
+
+    weights = {name: load(refs, "weight", name) for name in PIECES}
+    layer.old_rows[...] = stack_rows([jnp.zeros((1, 128), f32)] + five(weights))
+    each(near, "rest")
+    each(wide, "step", 3)
+    each(near, "corner")
+    each(wide, "hop", 0)
+    each(wide, "hop", 1)
+    each(near, "end")
     layer.project()
-    for g in gathers[2:]:
-        g.third()
-    layer.attend()
-    for g in gathers[2:]:
-        g.fourth()
+    each(wide, "hop", 2)
+    each(wide, "hop", 3)
+    layer.attend(0, layer.blocks // 2)
+    each(wide, "rest")
+    layer.attend(layer.blocks // 2, layer.blocks)
+    each(wide, "corner")
     layer.middle()
-    for g in gathers[2:]:
-        g.end()
+    layer.turn(layer.normed_two, layer.turned_two)
+    each(wide, "end")
     twin = links.mp + 1 - 2 * links.c
     links.wait(bias_core, layer.up_bias.at[twin])
     links.wait(bias_last, layer.up_bias.at[twin + 2 - 4 * links.x])
@@ -907,37 +934,28 @@
                 lo = hi
 
     def heads_out(j):
-        parts = dot(layer.turned[...], layer.grad_proj[j]), dot(layer.turned_mid[...], layer.attn_low[j])
+        parts = dot(layer.turned_one[...], layer.grad_proj[j]), dot(layer.turned_mid[...], layer.attn_low[j])
         return jnp.concatenate(parts, axis=1)
 
-    layer.grad_start()
-    layer.turn(layer.grad_top, layer.turned)
-    weigh(lambda j: dot(layer.turned[...], layer.activated[j]), down)
+    weigh(lambda j: dot(layer.turned_top[...], layer.activated[j]), down)
     down.start()
-    layer.top()
-    layer.gather_rows(layer.stream, layer.stage)
-    layer.block_out[...] = layer.stage[...].astype(bf16)
+    layer.feed_back()
     down.second()
-    layer.feed_back()
-    layer.turn(layer.normed_two, layer.turned)
-    weigh(lambda j: dot(layer.turned[...], layer.grad_pre[j]), up)
+    weigh(lambda j: dot(layer.turned_two[...], layer.grad_pre[j]), up)
     up.start()
-    down.third()
     layer.middle_back()
     up.second()
     layer.turn(layer.middle_low, layer.turned_mid)
-    down.fourth()
     layer.attend_back()
-    up.third()
-    layer.turn(layer.normed_one, layer.turned)
+    down.third()
     weigh(heads_out, qk, vo)
     qk.start()
     vo.start()
-    up.fourth()
+    up.third()
+    down.fourth()
+    qk.second()
     vo.second()
     layer.entry_back()
-    qk.second()
-    vo.third()
     layer.proj_grad[...] = dot(layer.hidden[...], layer.pos_low[...], TN)
     layer.pos_grad[...] = dot(layer.points[...], layer.pre_grad[...], TN, highest)
     small = layer.small
@@ -955,9 +973,17 @@
         who = links.round(k)
         block = layer.plane_out.at[lax.rem(links.plane + k, 8)]
         sums.append(links.send(block, layer.plane_in.at[links.plane], who))
+    up.fourth()
+    layer.gather_rows(layer.middle_grad, layer.stage)
+    out_copies = [pltpu.make_async_copy(layer.stage, layer.feats_grad, layer.store_sem.at[0])]
+    out_copies[0].start()
+    layer.top()
+    layer.gather_rows(layer.stream, layer.stage_top)
+    layer.block_low[...] = layer.stage_top[...].astype(bf16)
+    out_copies.append(pltpu.make_async_copy(layer.block_low, layer.block_out, layer.store_sem.at[1]))
+    out_copies[1].start()
     qk.third()
-    vo.fourth()
-    layer.gather_rows(layer.middle_grad, layer.feats_grad)
+    vo.third()
     for k in range(1, 8):
         links.wait(sums[k - 1], layer.plane_in.at[lax.rem(links.plane + 8 - k, 8)])
     total = layer.plane_in[0].astype(f32)
@@ -967,15 +993,16 @@
     layer.line_in[links.z] = layer.line_out[links.z]
     sums = []
     for k in range(1, 4):
-        block = layer.line_out.at[lax.rem(links.z + k, 4)]
+        block = layer.line_out.at[links.line[k]]
         sums.append(links.send(block, layer.line_in.at[links.z], links.far(k)))
     qk.fourth()
+    vo.fourth()
     own = layer.own_grad
     own[:, 512 + cols :] = down.end()
     own[:, 512 : 512 + cols] = up.end()
     own[:, 256:512] = vo.end()
     for k in range(1, 4):
-        links.wait(sums[k - 1], layer.line_in.at[links.back(k)])
+        links.wait(sums[k - 1], layer.line_in.at[links.line[k]])
     total = layer.line_in[0].astype(f32)
     for i in range(1, 4):
         total = total + layer.line_in[i].astype(f32)
@@ -985,9 +1012,6 @@
         block = layer.whole.at[links.plane, links.z]
         sums.append(links.send(block, block, links.far(k)))
     own[:, 0:256] = qk.end()
-    lead = (links.z * 2 + links.y == 0).astype(f32)
-    weights = {name: load(refs, "weight", name) for name in PIECES}
-
     def all_sum(slots, planes, rows):
         slots[links.z] = rows
         marks = []
@@ -995,7 +1019,7 @@
             block = slots.at[links.z]
             marks.append(links.send(block, block, links.far(k)))
         for k in range(1, 4):
-            links.wait(marks[k - 1], slots.at[links.back(k)])
+            links.wait(marks[k - 1], slots.at[links.line[k]])
         planes[links.plane] = slots[0] + slots[1] + slots[2] + slots[3]
         marks = []
         for k in range(1, 8):
@@ -1011,17 +1035,11 @@
             total = total + planes[i]
         return total
 
-    def five(parts):
-        out = []
-        for name in ("qkv", "out", "up", "bias", "down"):
-            row = sum(square_row(p) for p in parts[name])
-            out.append(row * lead if name == "bias" else row)
-        return out
-
-    rows = stack_rows([square_row(own[...])] + five(weights))
-    marks = all_sum(layer.line_a, layer.plane_a, rows)
+    place = lax.broadcasted_iota(jnp.int32, (8, 128), 0)
+    square = jnp.broadcast_to(square_row(own[...]), (8, 128))
+    marks = all_sum(layer.line_a, layer.plane_a, jnp.where(place == 0, square, layer.old_rows[...]))
     for k in range(1, 4):
-        links.wait(sums[k - 1], layer.whole.at[links.plane, links.back(k)])
+        links.wait(sums[k - 1], layer.whole.at[links.plane, links.line[k]])
     sums = []
     for k in range(1, 8):
         block = layer.whole.at[links.plane]
@@ -1044,10 +1062,12 @@
         ]
     marks = all_sum(layer.line_b, layer.plane_b, stack_rows(five(ways)))
     second = all_end(layer.plane_b, marks)
-    place = lax.broadcasted_iota(jnp.int32, (8, 128), 0)
     layer.sums[0:8, :] = jnp.where(place == 0, jnp.broadcast_to(total, (8, 128)), first)
     layer.sums[8:16, :] = second
+    for copy in out_copies:
+        copy.wait()
     links.finish()
+    assert links.counts == [SENDS, ARRIVALS], links.counts
 
 
 class _Shifted:
@@ -1059,6 +1079,7 @@
 
 
 SHAPES = ("weight", "moment", "second")
+SENDS, ARRIVALS = 107, 119
 
 
 def main_call(mp, inner, counts, feats, cotangent, points, params):
@@ -1066,14 +1087,15 @@
     width = feats.shape[1]
     hid = params["proj_weight"].shape[0]
     cols = inner // mp
+    rows = clouds * SLOT
     smem, vmem = pl.BlockSpec(memory_space=pltpu.SMEM), pl.BlockSpec(memory_space=pltpu.VMEM)
     anywhere = pl.BlockSpec(memory_space=pl.ANY)
     inputs = {"counts_all": (counts, smem), "feats_all": (feats, anywhere), "top_all": (cotangent, anywhere)}
-    inputs["points"] = (points, vmem)
+    inputs["points_all"] = (points, anywhere)
     scratch = layer_scratch(mp, clouds, width, inner, hid)
+    scratch["points"] = (points.shape, f32)
     for name in PIECES:
-        inputs[name + "_weight"] = (params[name + "_weight"], vmem)
-        for kind in SHAPES[1:]:
+        for kind in SHAPES:
             array = params[name + "_" + kind]
             inputs[name + "_" + kind + "_all"] = (array, anywhere)
             scratch[name + "_" + kind] = (array.shape, f32)
@@ -1085,6 +1107,13 @@
         sums=((16, 128), f32),
     )
     scratch.update(
+        stage_top=((clouds * PAD, width), f32),
+        block_low=((clouds * PAD, width), bf16),
+        old_rows=((8, 128), f32),
+        turned_top=((width, rows), bf16),
+        turned_one=((width, rows), bf16),
+        turned_two=((width, rows), bf16),
+        turned_mid=((width, rows), bf16),
         feats=((clouds * PAD, width), bf16),
         cotangent=((clouds * PAD, width), bf16),
         proj_low=((hid, width), bf16),
@@ -1108,13 +1137,13 @@
     )
     for tag, n in (("down__", cols), ("up__", cols), ("qk__", 256), ("vo__", 256)):
         scratch.update(scatter_scratch(tag, n))
-    sems = dict(send_sem=192, recv_sem=192, load_sem=18)
+    sems = dict(send_sem=SENDS, recv_sem=ARRIVALS, load_sem=27, store_sem=2)
     names = list(inputs) + list(outs) + list(scratch) + list(sems)
     return pl.pallas_call(
         functools.partial(main_kernel, names, mp, clouds, width, inner),
         out_shape=[jax.ShapeDtypeStruct(*v) for v in outs.values()],
         in_specs=[v[1] for v in inputs.values()],
-        out_specs=[vmem] * len(outs),
+        out_specs=[anywhere, anywhere, vmem, vmem, vmem],
         scratch_shapes=[pltpu.VMEM(*v) for v in scratch.values()]
         + [pltpu.SemaphoreType.DMA((n,)) for n in sems.values()],
         compiler_params=pltpu.CompilerParams(

time: 106 us -> 91.3 us (0.86)
  Pallas kernels: 103 us -> 88.2 us
    pallas_call x1, Pallas kernels: 98.4 us -> 83.7 us  [main_call(): pl.pallas_call(functools.partial(main_kernel, names, mp, clouds, width, i...]
where the time goes in v4:
time: 91.3 us; the launch traced here: 91 us
  Pallas kernels  88.2 us (97%)
  local copies, waits for them, and re-layouts  1.91 us (2%)
    pallas_call x1, Pallas kernels, main_call(): pl.pallas_call(functools.partial(main_kernel, names, mp, clouds, width, i...  83.7 us
    pallas_call x1, Pallas kernels, update_call(): pl.pallas_call(functools.partial(update_kernel, names), out_shape=[jax.Sh...  4.54 us

profile of v4, /device:TPU:0, one launch (start us, length us, event | category | flops | bytes accessed | tf_op | source)
XLA Modules:
  0.0 91.0 jit_solution(3838690473363960077)
XLA Ops:
  0.7 0.0 copy-start
  0.7 0.8 copy-done
  1.5 0.1 dynamic-slice_bitcast_fusion
  1.5 0.1 reshape.94
  1.6 0.2 copy.72
  1.9 0.8 pad.10.args_3_
  2.7 83.7 %shard_map.611 = (bf16[608,384]{1,0:T(8,128)(2,1)}, f32[608,384]{1,0:T(8,128)}, f32[48,1280]{1,0:T(8,128)}, f32[512,128]{1,0:T(8,128)}, f32[16,128]{1,0:T(8,128)}) custom-call(s32[64]{0:T(128)} %args_0_.4, bf16[2432,384]{1,0:T(8,128)(2,1)} %args_1_.4, bf16[2432,384]{1,0:T(8,128)(2,1)} %args_2_.4, f32[640,8]{1,0:T(8,128)} %pad.10.args_3_, ...), custom_call_target="tpu_custom_call" | custom-call | tf_op jit(solution)/shard_map/pallas_call | solution.py:1142
  86.3 4.5 %shard_map.612 = (bf16[608,384]{1,0:T(8,128)(2,1)}, f32[608,384]{1,0:T(8,128)}, f32[1,128]{1,0:T(1,128)}, f32[2,14]{1,0:T(2,128)}, f32[3,48,128]{2,1,0:T(8,128)}...) custom-call(bf16[608,384]{1,0:T(8,128)(2,1)} %get-tuple-element.93.a, ...), custom_call_target="tpu_custom_call" | custom-call | tf_op jit(solution)/shard_map/pallas_call | solution.py:1231
  (1 shorter events, 0.0 us)
Async XLA Ops:
  0.7 0.8 copy-start

commit v5 on v4

--- a/solution.py
+++ b/solution.py
@@ -54,6 +54,10 @@
     return trust_ratio[tensor_index + 6]
 
 
+def side_by_side(take, parts):
+    return jnp.concatenate([take(j) for j in parts], axis=1)
+
+
 class Layer:
     def __init__(self, refs, mp, clouds, width, inner):
         self.__dict__.update(refs)
@@ -132,8 +136,9 @@
         self.normed_one[...] = (hat * self.vec[0:1, :] + self.vec[2:3, :]).astype(bf16)
 
     def project(self):
-        for j in range(self.mp):
-            self.qkv[j] = dot(self.normed_one[...], self.w_qkv(j)).astype(bf16)
+        for j in range(0, self.mp, 2):
+            both = dot(self.normed_one[...], side_by_side(self.w_qkv, (j, j + 1))).astype(bf16)
+            self.qkv[j], self.qkv[j + 1] = both[:, :384], both[:, 384:]
 
     def lanes(self, h, n):
         lane = lax.broadcasted_iota(jnp.int32, (n, 128), 1)
@@ -171,9 +176,9 @@
         lax.fori_loop(start, stop, step, 0, unroll=2)
 
     def middle(self):
-        x = self.stream[...] + self.vec[4:5, :]
-        for j in range(self.mp):
-            x = x + dot(self.attn_low[j], self.w_out(j), NT)
+        parts = range(self.mp)
+        mixed = side_by_side(lambda j: self.attn_low[j], parts)
+        x = self.stream[...] + self.vec[4:5, :] + dot(mixed, side_by_side(self.w_out, parts), NT)
         hat, rate = self.norm(x)
         self.stream[...] = x
         self.hat_two[...] = hat
@@ -182,13 +187,16 @@
 
     def feed(self):
         total = self.stream[...]
-        for j in range(self.mp):
-            pre = dot(self.normed_two[...], self.w_up(j)) + self.up_bias[j, 0:1, :]
-            value, slope = gelu_pair(pre)
+        for j in range(0, self.mp, 2):
+            pair = (j, j + 1)
+            bias = side_by_side(lambda i: self.up_bias[i, 0:1, :], pair)
+            value, slope = gelu_pair(dot(self.normed_two[...], side_by_side(self.w_up, pair)) + bias)
             low = value.astype(bf16)
-            self.activated[j] = low
-            self.slope[j] = slope
-            total = total + dot(low, self.w_down(j), NT)
+            half = low.shape[1] // 2
+            for k, i in enumerate(pair):
+                self.activated[i] = low[:, k * half : (k + 1) * half]
+                self.slope[i] = slope[:, k * half : (k + 1) * half]
+            total = total + dot(low, side_by_side(self.w_down, pair), NT)
         self.stream[...] = total
 
     def top(self):
@@ -205,12 +213,16 @@
 
     def feed_back(self):
         total = None
-        for j in range(self.mp):
-            grad = dot(self.grad_top[...], self.w_down(j)) * self.slope[j]
-            low = grad.astype(bf16)
-            self.grad_pre[j] = low
-            self.up_bias_grad[j, 0:1, :] = jnp.sum(low.astype(f32), axis=0, keepdims=True)
-            term = dot(low, self.w_up(j), NT)
+        for j in range(0, self.mp, 2):
+            pair = (j, j + 1)
+            grad = dot(self.grad_top[...], side_by_side(self.w_down, pair))
+            low = (grad * side_by_side(lambda i: self.slope[i], pair)).astype(bf16)
+            bias = jnp.sum(low.astype(f32), axis=0, keepdims=True)
+            half = low.shape[1] // 2
+            for k, i in enumerate(pair):
+                self.grad_pre[i] = low[:, k * half : (k + 1) * half]
+                self.up_bias_grad[i, 0:1, :] = bias[:, k * half : (k + 1) * half]
+            term = dot(low, side_by_side(self.w_up, pair), NT)
             total = term if j == 0 else total + term
         self.normed_grad[...] = total
 
@@ -224,8 +236,9 @@
         self.vec_grad[4:5, :] = jnp.sum(out, axis=0, keepdims=True)
         low = out.astype(bf16)
         self.middle_low[...] = low
+        grads = dot(low, side_by_side(self.w_out, range(self.mp))).astype(bf16)
         for j in range(self.mp):
-            self.attn_grad[j] = dot(low, self.w_out(j)).astype(bf16)
+            self.attn_grad[j] = grads[:, 128 * j : 128 * j + 128]
 
     def attend_back(self):
         n = self.block
@@ -261,8 +274,9 @@
 
     def entry_back(self):
         grad = None
-        for j in range(self.mp):
-            term = dot(self.grad_proj[j], self.w_qkv(j), NT)
+        for j in range(0, self.mp, 2):
+            pair = (j, j + 1)
+            term = dot(side_by_side(lambda i: self.grad_proj[i], pair), side_by_side(self.w_qkv, pair), NT)
             grad = term if j == 0 else grad + term
         hat = self.hat_one[...]
         rate = jnp.concatenate([self.rate_one[...]] * (self.width // 128), axis=1)
@@ -529,6 +543,7 @@
         self.x, self.c = mp // 2, lax.rem(mp, 2)
         self.mp = mp
         self.plane = self.y * 4 + mp
+        self.me = dp * 4 + mp
         self.line = [self.z, self.z + 1 - 2 * lax.rem(self.z, 2), lax.rem(self.z + 2, 4), 3 - self.z]
         self.send_sem, self.recv_sem = send, recv
         self.counts = [0, 0]
@@ -553,16 +568,20 @@
         other = lax.rem(self.plane + k, 8)
         return (self.z * 2 + other // 4, lax.rem(other, 4))
 
+    def any(self, k):
+        other = lax.rem(self.me + k, 32)
+        return (other // 4, lax.rem(other, 4))
+
     def peers(self):
         return [self.far(k) for k in range(1, 4)] + [self.round(k) for k in range(1, 8)]
 
-    def greet(self):
+    def greet(self, everyone=False):
         barrier = pltpu.get_barrier_semaphore()
-        for who in self.peers():
+        for who in [self.any(k) for k in range(1, 32)] if everyone else self.peers():
             pl.semaphore_signal(barrier, inc=1, device_id=who, device_id_type=pl.DeviceIdType.MESH)
 
-    def met(self):
-        pl.semaphore_wait(pltpu.get_barrier_semaphore(), 10)
+    def met(self, count):
+        pl.semaphore_wait(pltpu.get_barrier_semaphore(), count)
 
     def copy(self, source, target, i):
         return pltpu.make_async_remote_copy(
@@ -751,6 +770,19 @@
     return out
 
 
+def lane_row(rows, base=None):
+    lane = lax.broadcasted_iota(jnp.int32, (1, 128), 1)
+    out = jnp.zeros((1, 128), f32) if base is None else base
+    for i, row in enumerate(rows):
+        out = jnp.where(lane == i, row, out)
+    return out
+
+
+def lane_value(row, i):
+    lane = lax.broadcasted_iota(jnp.int32, (1, 128), 1)
+    return jnp.sum(jnp.where(lane == i, row, 0.0), axis=1, keepdims=True)
+
+
 def square_row(array):
     total = jnp.sum(jnp.sum(array * array, axis=0, keepdims=True), axis=1, keepdims=True)
     return jnp.broadcast_to(total, (1, 128))
@@ -805,7 +837,7 @@
     cols = inner // mp
     links = Links(layer.send_sem, layer.recv_sem)
     w = layer.w
-    links.greet()
+    links.greet(True)
     share = clouds * PAD
     rows = pl.ds(pl.multiple_of(links.mp * share, 16), share)
     sources = {"feats": layer.feats_all.at[rows, :], "cotangent": layer.top_all.at[rows, :]}
@@ -838,7 +870,7 @@
     w[links.mp, links.z, links.y, :, 512 : 512 + cols] = refs["up_weight"][...].astype(bf16)
     w[links.mp, links.z, links.y, :, 512 + cols : 512 + 2 * cols] = refs["down_weight"][...].astype(bf16)
     layer.up_bias[links.mp] = jnp.broadcast_to(refs["bias_weight"][...].reshape(1, cols), (8, cols))
-    links.met()
+    links.met(31)
     gathers = [
         Gather(links, w, 0, 256, False),
         Gather(links, w, 256, 512, True),
@@ -893,7 +925,8 @@
         return out
 
     weights = {name: load(refs, "weight", name) for name in PIECES}
-    layer.old_rows[...] = stack_rows([jnp.zeros((1, 128), f32)] + five(weights))
+    zero = jnp.zeros((1, 1), f32)
+    layer.old_rows[...] = lane_row([jnp.zeros((1, 128), f32)] + five(weights))
     each(near, "rest")
     each(wide, "step", 3)
     each(near, "corner")
@@ -923,7 +956,7 @@
 
     def weigh(product, *targets):
         for x in range(2):
-            pair = [product(2 * x), product(2 * x + 1)]
+            pair = product((2 * x, 2 * x + 1))
             kept = jnp.where(links.c == 0, pair[0], pair[1])
             sent = jnp.where(links.c == 0, pair[1], pair[0]).astype(bf16)
             lo = 0
@@ -933,26 +966,36 @@
                 target.kept[x] = kept[:, lo:hi].reshape(4, 2, 48, hi - lo)
                 lo = hi
 
-    def heads_out(j):
-        parts = dot(layer.turned_one[...], layer.grad_proj[j]), dot(layer.turned_mid[...], layer.attn_low[j])
-        return jnp.concatenate(parts, axis=1)
-
-    weigh(lambda j: dot(layer.turned_top[...], layer.activated[j]), down)
+    def halves(turned, source, pair):
+        both = dot(turned[...], side_by_side(lambda j: source[j], pair))
+        half = both.shape[1] // 2
+        return both[:, :half], both[:, half:]
+
+    def heads_out(pair):
+        heads = halves(layer.turned_one, layer.grad_proj, pair)
+        mixed = halves(layer.turned_mid, layer.attn_low, pair)
+        return [jnp.concatenate(parts, axis=1) for parts in zip(heads, mixed)]
+
+    weigh(lambda pair: halves(layer.turned_top, layer.activated, pair), down)
     down.start()
     layer.feed_back()
     down.second()
-    weigh(lambda j: dot(layer.turned_two[...], layer.grad_pre[j]), up)
+    weigh(lambda pair: halves(layer.turned_two, layer.grad_pre, pair), up)
     up.start()
     layer.middle_back()
     up.second()
     layer.turn(layer.middle_low, layer.turned_mid)
     layer.attend_back()
+    layer.top()
+    layer.gather_rows(layer.stream, layer.stage_top)
+    layer.block_low[...] = layer.stage_top[...].astype(bf16)
+    out_copies = [pltpu.make_async_copy(layer.block_low, layer.block_out, layer.store_sem.at[1])]
+    out_copies[0].start()
     down.third()
     weigh(heads_out, qk, vo)
     qk.start()
     vo.start()
     up.third()
-    down.fourth()
     qk.second()
     vo.second()
     layer.entry_back()
@@ -973,17 +1016,13 @@
         who = links.round(k)
         block = layer.plane_out.at[lax.rem(links.plane + k, 8)]
         sums.append(links.send(block, layer.plane_in.at[links.plane], who))
-    up.fourth()
+    down.fourth()
     layer.gather_rows(layer.middle_grad, layer.stage)
-    out_copies = [pltpu.make_async_copy(layer.stage, layer.feats_grad, layer.store_sem.at[0])]
-    out_copies[0].start()
-    layer.top()
-    layer.gather_rows(layer.stream, layer.stage_top)
-    layer.block_low[...] = layer.stage_top[...].astype(bf16)
-    out_copies.append(pltpu.make_async_copy(layer.block_low, layer.block_out, layer.store_sem.at[1]))
+    out_copies.append(pltpu.make_async_copy(layer.stage, layer.feats_grad, layer.store_sem.at[0]))
     out_copies[1].start()
     qk.third()
     vo.third()
+    up.fourth()
     for k in range(1, 8):
         links.wait(sums[k - 1], layer.plane_in.at[lax.rem(links.plane + 8 - k, 8)])
     total = layer.plane_in[0].astype(f32)
@@ -1012,32 +1051,22 @@
         block = layer.whole.at[links.plane, links.z]
         sums.append(links.send(block, block, links.far(k)))
     own[:, 0:256] = qk.end()
-    def all_sum(slots, planes, rows):
-        slots[links.z] = rows
-        marks = []
-        for k in range(1, 4):
-            block = slots.at[links.z]
-            marks.append(links.send(block, block, links.far(k)))
-        for k in range(1, 4):
-            links.wait(marks[k - 1], slots.at[links.line[k]])
-        planes[links.plane] = slots[0] + slots[1] + slots[2] + slots[3]
-        marks = []
-        for k in range(1, 8):
-            block = planes.at[links.plane]
-            marks.append(links.send(block, block, links.round(k)))
-        return marks
-
-    def all_end(planes, marks):
-        for k in range(1, 8):
-            links.wait(marks[k - 1], planes.at[lax.rem(links.plane + 8 - k, 8)])
-        total = planes[0]
-        for i in range(1, 8):
-            total = total + planes[i]
+    def all_start(slots, row):
+        slots[31] = row
+        out, into = links.mark(0), links.mark(1)
+        for k in range(1, 32):
+            links.send(slots.at[31], slots.at[k - 1], links.any(k), out, into)
+        links.sent_all(out, slots.at[0:31])
+        return into
+
+    def all_end(slots, into):
+        links.wait(into, slots.at[0:31])
+        total = slots[lax.rem(links.me + 31, 32)]
+        for i in range(1, 32):
+            total = total + slots[lax.rem(links.me + 31 - i + 32, 32)]
         return total
 
-    place = lax.broadcasted_iota(jnp.int32, (8, 128), 0)
-    square = jnp.broadcast_to(square_row(own[...]), (8, 128))
-    marks = all_sum(layer.line_a, layer.plane_a, jnp.where(place == 0, square, layer.old_rows[...]))
+    mark = all_start(layer.slots_a, lane_row([square_row(own[...])], layer.old_rows[...]))
     for k in range(1, 4):
         links.wait(sums[k - 1], layer.whole.at[links.plane, links.line[k]])
     sums = []
@@ -1047,10 +1076,10 @@
     for k in range(1, 8):
         links.wait(sums[k - 1], layer.whole.at[lax.rem(links.plane + 8 - k, 8)])
     small[...] = layer.whole[...].astype(f32).reshape(512, 128)
-    first = all_end(layer.plane_a, marks)
+    first = all_end(layer.slots_a, mark)
     layer.small_out[...] = small[...]
-    total = first[0:1] + square_row(small[0:440, :])
-    factor = jnp.minimum(1.0, clip_max / (jnp.sqrt(total) + 1e-06))[0:1, 0:1]
+    total = lane_value(first, 0) + square_row(small[0:440, :])[0:1, 0:1]
+    factor = jnp.minimum(1.0, clip_max / (jnp.sqrt(total) + 1e-06))
     for copy in late:
         copy.wait()
     grads = own_parts(own, small, links.mp)
@@ -1060,10 +1089,11 @@
             adam(g, factor, m, s, p)[3]
             for g, m, s, p in zip(grads[name], load(refs, "moment", name), load(refs, "second", name), weights[name])
         ]
-    marks = all_sum(layer.line_b, layer.plane_b, stack_rows(five(ways)))
-    second = all_end(layer.plane_b, marks)
-    layer.sums[0:8, :] = jnp.where(place == 0, jnp.broadcast_to(total, (8, 128)), first)
-    layer.sums[8:16, :] = second
+    mark = all_start(layer.slots_b, lane_row(five(ways)))
+    second = all_end(layer.slots_b, mark)
+    rows = [total] + [lane_value(first, i) for i in range(1, 6)] + [zero, zero]
+    rows += [lane_value(second, i) for i in range(5)]
+    layer.sums[...] = stack_rows([jnp.broadcast_to(r, (1, 128)) for r in rows], 16)
     for copy in out_copies:
         copy.wait()
     links.finish()
@@ -1079,7 +1109,7 @@
 
 
 SHAPES = ("weight", "moment", "second")
-SENDS, ARRIVALS = 107, 119
+SENDS, ARRIVALS = 89, 101
 
 
 def main_call(mp, inner, counts, feats, cotangent, points, params):
@@ -1109,7 +1139,7 @@
     scratch.update(
         stage_top=((clouds * PAD, width), f32),
         block_low=((clouds * PAD, width), bf16),
-        old_rows=((8, 128), f32),
+        old_rows=((1, 128), f32),
         turned_top=((width, rows), bf16),
         turned_one=((width, rows), bf16),
         turned_two=((width, rows), bf16),
@@ -1130,10 +1160,8 @@
         line_out=((4, 16, 128), bf16),
         line_in=((4, 16, 128), bf16),
         whole=((8, 4, 16, 128), bf16),
-        line_a=((4, 8, 128), f32),
-        plane_a=((8, 8, 128), f32),
-        line_b=((4, 8, 128), f32),
-        plane_b=((8, 8, 128), f32),
+        slots_a=((32, 1, 128), f32),
+        slots_b=((32, 1, 128), f32),
     )
     for tag, n in (("down__", cols), ("up__", cols), ("qk__", 256), ("vo__", 256)):
         scratch.update(scatter_scratch(tag, n))

time: 91.3 us -> 87.5 us (0.958)
  Pallas kernels: 88.2 us -> 84.4 us
    pallas_call x1, Pallas kernels: 83.7 us -> 79.9 us  [main_call(): pl.pallas_call(functools.partial(main_kernel, names, mp, clouds, width, i...]
where the time goes in v5:
time: 87.5 us; the launch traced here: 87.3 us
  Pallas kernels  84.4 us (96%)
  local copies, waits for them, and re-layouts  1.91 us (2%)
  between operations  0.91 us (1%)
    pallas_call x1, Pallas kernels, main_call(): pl.pallas_call(functools.partial(main_kernel, names, mp, clouds, width, i...  79.9 us
    pallas_call x1, Pallas kernels, update_call(): pl.pallas_call(functools.partial(update_kernel, names), out_shape=[jax.Sh...  4.54 us

profile of v5, /device:TPU:0, one launch (start us, length us, event | category | flops | bytes accessed | tf_op | source)
XLA Modules:
  0.0 87.3 jit_solution(3901926546065812198)
XLA Ops:
  0.7 0.0 copy-start
  0.7 0.8 copy-done
  1.5 0.1 dynamic-slice_bitcast_fusion
  1.5 0.1 reshape.94
  1.6 0.2 copy.72
  1.9 0.8 pad.10.args_3_
  2.7 79.9 %shard_map.611 = (bf16[608,384]{1,0:T(8,128)(2,1)}, f32[608,384]{1,0:T(8,128)}, f32[48,1280]{1,0:T(8,128)}, f32[512,128]{1,0:T(8,128)}, f32[16,128]{1,0:T(8,128)}) custom-call(s32[64]{0:T(128)} %args_0_.4, bf16[2432,384]{1,0:T(8,128)(2,1)} %args_1_.4, bf16[2432,384]{1,0:T(8,128)(2,1)} %args_2_.4, f32[640,8]{1,0:T(8,128)} %pad.10.args_3_, ...), custom_call_target="tpu_custom_call" | custom-call | tf_op jit(solution)/shard_map/pallas_call | solution.py:1170
  82.6 4.5 %shard_map.612 = (bf16[608,384]{1,0:T(8,128)(2,1)}, f32[608,384]{1,0:T(8,128)}, f32[1,128]{1,0:T(1,128)}, f32[2,14]{1,0:T(2,128)}, f32[3,48,128]{2,1,0:T(8,128)}...) custom-call(bf16[608,384]{1,0:T(8,128)(2,1)} %get-tuple-element.93.a, ...), custom_call_target="tpu_custom_call" | custom-call | tf_op jit(solution)/shard_map/pallas_call | solution.py:1259
  (1 shorter events, 0.0 us)
Async XLA Ops:
  0.7 0.8 copy-start

commit v6 on v5

--- a/solution.py
+++ b/solution.py
@@ -1051,6 +1051,8 @@
         block = layer.whole.at[links.plane, links.z]
         sums.append(links.send(block, block, links.far(k)))
     own[:, 0:256] = qk.end()
+    out_copies.append(pltpu.make_async_copy(own, layer.own_out, layer.store_sem.at[2]))
+    out_copies[2].start()
     def all_start(slots, row):
         slots[31] = row
         out, into = links.mark(0), links.mark(1)
@@ -1077,7 +1079,8 @@
         links.wait(sums[k - 1], layer.whole.at[lax.rem(links.plane + 8 - k, 8)])
     small[...] = layer.whole[...].astype(f32).reshape(512, 128)
     first = all_end(layer.slots_a, mark)
-    layer.small_out[...] = small[...]
+    out_copies.append(pltpu.make_async_copy(small, layer.small_out, layer.store_sem.at[3]))
+    out_copies[3].start()
     total = lane_value(first, 0) + square_row(small[0:440, :])[0:1, 0:1]
     factor = jnp.minimum(1.0, clip_max / (jnp.sqrt(total) + 1e-06))
     for copy in late:
@@ -1132,7 +1135,7 @@
     outs = dict(
         block_out=((clouds * PAD, width), bf16),
         feats_grad=((clouds * PAD, width), f32),
-        own_grad=((48, 512 + 2 * cols), f32),
+        own_out=((48, 512 + 2 * cols), f32),
         small_out=((512, 128), f32),
         sums=((16, 128), f32),
     )
@@ -1140,6 +1143,7 @@
         stage_top=((clouds * PAD, width), f32),
         block_low=((clouds * PAD, width), bf16),
         old_rows=((1, 128), f32),
+        own_grad=((48, 512 + 2 * cols), f32),
         turned_top=((width, rows), bf16),
         turned_one=((width, rows), bf16),
         turned_two=((width, rows), bf16),
@@ -1165,13 +1169,13 @@
     )
     for tag, n in (("down__", cols), ("up__", cols), ("qk__", 256), ("vo__", 256)):
         scratch.update(scatter_scratch(tag, n))
-    sems = dict(send_sem=SENDS, recv_sem=ARRIVALS, load_sem=27, store_sem=2)
+    sems = dict(send_sem=SENDS, recv_sem=ARRIVALS, load_sem=27, store_sem=4)
     names = list(inputs) + list(outs) + list(scratch) + list(sems)
     return pl.pallas_call(
         functools.partial(main_kernel, names, mp, clouds, width, inner),
         out_shape=[jax.ShapeDtypeStruct(*v) for v in outs.values()],
         in_specs=[v[1] for v in inputs.values()],
-        out_specs=[anywhere, anywhere, vmem, vmem, vmem],
+        out_specs=[anywhere] * 4 + [vmem],
         scratch_shapes=[pltpu.VMEM(*v) for v in scratch.values()]
         + [pltpu.SemaphoreType.DMA((n,)) for n in sems.values()],
         compiler_params=pltpu.CompilerParams(

time: 87.5 us -> 87.3 us (level)
  no operation moved by 1% of the time
where the time goes in v6:
time: 87.3 us; the launch traced here: 87.1 us
  Pallas kernels  84.2 us (96%)
  local copies, waits for them, and re-layouts  1.91 us (2%)
  between operations  0.91 us (1%)
    pallas_call x1, Pallas kernels, main_call(): pl.pallas_call(functools.partial(main_kernel, names, mp, clouds, width, i...  79.7 us
    pallas_call x1, Pallas kernels, update_call(): pl.pallas_call(functools.partial(update_kernel, names), out_shape=[jax.Sh...  4.54 us

profile of v6, /device:TPU:0, one launch (start us, length us, event | category | flops | bytes accessed | tf_op | source)
XLA Modules:
  0.0 87.1 jit_solution(16309786539733477125)
XLA Ops:
  0.7 0.0 copy-start
  0.7 0.8 copy-done
  1.5 0.1 dynamic-slice_bitcast_fusion
  1.5 0.1 reshape.94
  1.6 0.2 copy.72
  1.9 0.8 pad.10.args_3_
  2.7 79.7 %shard_map.611 = (bf16[608,384]{1,0:T(8,128)(2,1)}, f32[608,384]{1,0:T(8,128)}, f32[48,1280]{1,0:T(8,128)}, f32[512,128]{1,0:T(8,128)}, f32[16,128]{1,0:T(8,128)}) custom-call(s32[64]{0:T(128)} %args_0_.4, bf16[2432,384]{1,0:T(8,128)(2,1)} %args_1_.4, bf16[2432,384]{1,0:T(8,128)(2,1)} %args_2_.4, f32[640,8]{1,0:T(8,128)} %pad.10.args_3_, ...), custom_call_target="tpu_custom_call" | custom-call | tf_op jit(solution)/shard_map/pallas_call | solution.py:1174
  82.4 4.5 %shard_map.612 = (bf16[608,384]{1,0:T(8,128)(2,1)}, f32[608,384]{1,0:T(8,128)}, f32[1,128]{1,0:T(1,128)}, f32[2,14]{1,0:T(2,128)}, f32[3,48,128]{2,1,0:T(8,128)}...) custom-call(bf16[608,384]{1,0:T(8,128)(2,1)} %get-tuple-element.93.a, ...), custom_call_target="tpu_custom_call" | custom-call | tf_op jit(solution)/shard_map/pallas_call | solution.py:1263
  (1 shorter events, 0.0 us)
Async XLA Ops:
  0.7 0.8 copy-start
